TPU v7x, 128 devices: a whole 4x4x4 slice. The times are simulated.
128 devices in a mesh: row: 8 (over y_hi, z), col: 16 (over y_lo, x, core).
Axes of the slice: x: 4, y: 4 (y_hi: 2, y_lo: 2; y = y_hi * 2 + y_lo), z: 4, core: 2. Of those that a mesh axis runs over, the one named last changes fastest.
Arguments:
- matrix: float32 [64, 64, 4096], P('row', None, 'col'), may hold values from -0.72 to 0.72
- pattern_cols: int32 [64, 16, 4], replicated, may hold values from 0 to 3, as said below
- pattern_counts: int32 [64, 16], replicated, may hold values from 0 to 4, as said below
Outputs:
- next_sign: float32 [64, 64, 4096], P('row', None, 'col')
Inputs may be any that keep to these rules, and one draw needn't show every extreme that they name: `pattern_cols`: for each block row and panel the used slots name distinct block columns; unused slots hold the panel's other columns. Every block row's diagonal block is in its pattern. `pattern_counts`: some block row of every panel uses all 4 slots; a panel may hold no block of a block row. In a panel more than 2 panels away (cyclically) from a block row's own panel (block row // 4), the count is at most 1, except for at most one block row per panel.
All inputs are finite; a program needn't handle non-finite values.
Results may differ from a plain program's by a relative error of at most 0.000082.
Values sent between devices are 32-bit elements; how exact they have to be, the bound alone decides.
No kernel may reach another device: no remote copies, remote signals or barrier semaphores. Data moves between devices by JAX's collectives and lax.ppermute only.
A program may use at most 64 MiB of HBM per device.

v0:
```python
import jax
import jax.numpy as jnp
from jax import lax
from jax.sharding import PartitionSpec as P


def from_behind(value, axis, steps):
    count = lax.axis_size(axis)
    pairs = [(source, (source + steps) % count) for source in range(count)]
    return lax.ppermute(value, axis, pairs)


def block_onehot(block_cols, block_valid, width):
    onehot = (block_cols[..., None] == jnp.arange(width, dtype=jnp.int32)) & block_valid[..., None]
    return onehot.astype(jnp.float32)


def spread_blocks(tiles, onehot):
    count, height, breadth = tiles.shape
    slot_count = onehot.shape[1]
    block_size = breadth // slot_count
    blocks = tiles.reshape(count, height, slot_count, block_size)
    dense = jnp.einsum("rman,raj->rmjn", blocks, onehot, precision=lax.Precision.HIGHEST)
    return dense.reshape(count, height, onehot.shape[2] * block_size)


def collect_blocks(dense, onehot):
    count, height, breadth = dense.shape
    width = onehot.shape[2]
    block_size = breadth // width
    blocks = dense.reshape(count, height, width, block_size)
    slotted = jnp.einsum("rmjn,raj->rman", blocks, onehot, precision=lax.Precision.HIGHEST)
    return slotted.reshape(count, height, onehot.shape[1] * block_size)


def per_device(matrix, pattern_cols, pattern_counts):
    row_count = matrix.shape[0]
    block_size = matrix.shape[1]
    strip_width = matrix.shape[2]
    slot_count = pattern_cols.shape[2]
    row_devices = lax.axis_size("row")
    col_devices = lax.axis_size("col")
    lane_count = col_devices // row_devices
    panel_size = row_count // lane_count
    dense_width = panel_size * block_size
    row_place = lax.axis_index("row")
    col_place = lax.axis_index("col")
    own_rows = row_place * row_count + jnp.arange(row_count, dtype=jnp.int32)
    slot_ids = jnp.arange(slot_count, dtype=jnp.int32)
    own_patterns = pattern_cols[own_rows]
    own_counts = pattern_counts[own_rows]
    own_cols = jnp.take(own_patterns, col_place, axis=1)
    own_valid = slot_ids[None, :] < jnp.take(own_counts, col_place, axis=1)[:, None]
    own_onehot = block_onehot(own_cols, own_valid, panel_size)

    def local_product(left_tiles, right_panel, k_panel):
        left_cols = jnp.take(own_patterns, k_panel, axis=1)
        left_valid = slot_ids[None, :] < jnp.take(own_counts, k_panel, axis=1)[:, None]
        right_rows = k_panel * panel_size + jnp.arange(panel_size, dtype=jnp.int32)
        right_cols = jnp.take(pattern_cols[right_rows], col_place, axis=1)
        right_valid = (
            slot_ids[None, :] < jnp.take(pattern_counts[right_rows], col_place, axis=1)[:, None]
        )
        left_dense = spread_blocks(left_tiles, block_onehot(left_cols, left_valid, panel_size))
        right_dense = spread_blocks(right_panel, block_onehot(right_cols, right_valid, panel_size))
        return jnp.dot(
            left_dense.reshape(row_count * block_size, dense_width),
            right_dense.reshape(dense_width, dense_width),
            precision=lax.Precision.HIGHEST,
            preferred_element_type=jnp.float32,
        )

    def advance_cols(left_tiles):
        return from_behind(left_tiles, "col", -1)

    def rotate_lanes(lane_stack):
        incoming = from_behind(lane_stack[0], "row", -1)
        return jnp.concatenate([lane_stack[1:], incoming[None]], axis=0)

    def block_product(left_tiles, right_tiles):
        for bit_index in range(row_devices.bit_length() - 1):
            moved_tiles = from_behind(left_tiles, "col", -(lane_count << bit_index))
            left_tiles = jnp.where(row_place >> bit_index & 1 == 1, moved_tiles, left_tiles)
        lane_stack = right_tiles.reshape(lane_count, panel_size, block_size, strip_width)
        lane_stack = jnp.where(col_place & 1 == 1, rotate_lanes(lane_stack), lane_stack)
        for bit_index in range(1, col_devices.bit_length() - 1):
            moved_lanes = from_behind(lane_stack, "row", -(1 << bit_index - 1))
            lane_stack = jnp.where(col_place >> bit_index & 1 == 1, moved_lanes, lane_stack)
        start_panel = (col_place + lane_count * row_place) % col_devices
        zero_dense = jnp.zeros((row_count * block_size, dense_width), jnp.float32)

        def one_step(step_index, carry):
            running, left_now, lanes_now = carry
            running = running + local_product(
                left_now, lanes_now[0], (start_panel + step_index) % col_devices
            )
            return (running, advance_cols(left_now), rotate_lanes(lanes_now))

        running, left_tiles, lane_stack = lax.fori_loop(
            0, col_devices - 1, one_step, (zero_dense, left_tiles, lane_stack)
        )
        running = running + local_product(
            left_tiles, lane_stack[0], (start_panel + col_devices - 1) % col_devices
        )
        slotted = collect_blocks(running.reshape(row_count, block_size, dense_width), own_onehot)
        return (slotted, left_tiles)

    square, left_last = block_product(matrix, matrix)
    on_diagonal = (
        (own_rows // panel_size == col_place)[:, None]
        & (own_cols == (own_rows % panel_size)[:, None])
        & own_valid
    )
    identity = jnp.eye(block_size, dtype=jnp.float32)
    diagonal_tiles = on_diagonal.astype(jnp.float32)[:, None, :, None] * identity[None, :, None, :]
    diagonal_tiles = diagonal_tiles.reshape(row_count, block_size, slot_count * block_size)
    shifted = 3.0 * diagonal_tiles - square
    product, unused_tiles = block_product(matrix, shifted)
    return 0.5 * product


def solution(mesh):
    return jax.shard_map(
        per_device,
        mesh=mesh,
        in_specs=(P("row", None, "col"), P(), P()),
        out_specs=P("row", None, "col"),
        check_vma=False,
    )
```

profile of v0, /device:TPU:8, one launch (start us, length us, event | category | flops | bytes accessed | tf_op | source)
XLA Modules:
  0.0 659.2 jit_solution(13252768479509197548)
XLA Ops:
  3.7 6.1 collective-permute-start.7
  15.2 6.2 collective-permute-start.8
  25.8 5.6 collective-permute-done.8
  40.1 6.2 collective-permute-done.9
  53.3 6.6 %collective-permute-done.6 = f32[8,64,256]{2,1,0:T(8,128)} collective-permute-done((f32[8,64,256]{2,1,0:T(8,128)S(1)}, f32[8,64,256]{2,1,0:T(8,128)}, u32[]{:S(2)}, u32[]{:S(2)}) %collective-permute-start.6) | collective-permute-done | bytes 524320 | tf_op jit(solution)/shard_map/ppermute | solution.py:10
  60.8 6.3 collective-permute-done.10
  68.1 282.0 %while.46 = (s32[]{:T(128)}, f32[512,256]{1,0:T(8,128)}, f32[8,64,256]{2,1,0:T(8,128)S(1)}, f32[2,4,64,256]{3,2,1,0:T(8,128)S(1)}, s32[]{:T(128)}, /*index=5*/s3...) while((s32[]{:T(128)}, f32[512,256]{1,0:T(8,128)}, ...), condition=%wide.region_1.6_spmd.clone.clone, body=%wide.region_0.5_spmd.clone.clone.sunk | while | flops 412485152 | bytes 18358452 | solution.py:99
  69.3 20.9 %collective-permute-start = (f32[8,64,256]{2,1,0:T(8,128)S(1)}, f32[8,64,256]{2,1,0:T(8,128)S(1)}, u32[]{:S(2)}, u32[]{:S(2)}) collective-permute-start(f32[8,64,256]{2,1,0:T(8,128)S(1)} %copy.76), channel_id=1, source_target_pairs={{0,15},{1,0},{2,1},{3,2},{4,3},{5,4},{6,5},{7,6},{8,7},{9,8},{10,9... | collective-permute-start | bytes 1572872 | tf_op jit(solution)/shard_map/while/body/eval_jaxpr/ppermute | solution.py:10
  101.2 6.4 collective-permute-start
  136.9 7.9 %collective-permute-start = (f32[8,64,256]{2,1,0:T(8,128)S(1)}, f32[8,64,256]{2,1,0:T(8,128)S(1)}, u32[]{:S(2)}, u32[]{:S(2)}) collective-permute-start(f32[8,64,256]{2,1,0:T(8,128)S(1)} %copy.76), channel_id=1, source_target_pairs={{0,15},{1,0},{2,1},{3,2},{4,3},{5,4},{6,5},{7,6},{8,7},{9,8},{10,9... | collective-permute-start | bytes 1572872 | tf_op jit(solution)/shard_map/while/body/eval_jaxpr/ppermute | solution.py:10
  155.7 6.0 collective-permute-start
  172.7 6.8 %collective-permute-start = (f32[8,64,256]{2,1,0:T(8,128)S(1)}, f32[8,64,256]{2,1,0:T(8,128)S(1)}, u32[]{:S(2)}, u32[]{:S(2)}) collective-permute-start(f32[8,64,256]{2,1,0:T(8,128)S(1)} %copy.76), channel_id=1, source_target_pairs={{0,15},{1,0},{2,1},{3,2},{4,3},{5,4},{6,5},{7,6},{8,7},{9,8},{10,9... | collective-permute-start | bytes 1572872 | tf_op jit(solution)/shard_map/while/body/eval_jaxpr/ppermute | solution.py:10
  190.6 6.8 %collective-permute-start = (f32[8,64,256]{2,1,0:T(8,128)S(1)}, f32[8,64,256]{2,1,0:T(8,128)S(1)}, u32[]{:S(2)}, u32[]{:S(2)}) collective-permute-start(f32[8,64,256]{2,1,0:T(8,128)S(1)} %copy.76), channel_id=1, source_target_pairs={{0,15},{1,0},{2,1},{3,2},{4,3},{5,4},{6,5},{7,6},{8,7},{9,8},{10,9... | collective-permute-start | bytes 1572872 | tf_op jit(solution)/shard_map/while/body/eval_jaxpr/ppermute | solution.py:10
  208.4 6.8 %collective-permute-start = (f32[8,64,256]{2,1,0:T(8,128)S(1)}, f32[8,64,256]{2,1,0:T(8,128)S(1)}, u32[]{:S(2)}, u32[]{:S(2)}) collective-permute-start(f32[8,64,256]{2,1,0:T(8,128)S(1)} %copy.76), channel_id=1, source_target_pairs={{0,15},{1,0},{2,1},{3,2},{4,3},{5,4},{6,5},{7,6},{8,7},{9,8},{10,9... | collective-permute-start | bytes 1572872 | tf_op jit(solution)/shard_map/while/body/eval_jaxpr/ppermute | solution.py:10
  226.2 6.9 %collective-permute-start = (f32[8,64,256]{2,1,0:T(8,128)S(1)}, f32[8,64,256]{2,1,0:T(8,128)S(1)}, u32[]{:S(2)}, u32[]{:S(2)}) collective-permute-start(f32[8,64,256]{2,1,0:T(8,128)S(1)} %copy.76), channel_id=1, source_target_pairs={{0,15},{1,0},{2,1},{3,2},{4,3},{5,4},{6,5},{7,6},{8,7},{9,8},{10,9... | collective-permute-start | bytes 1572872 | tf_op jit(solution)/shard_map/while/body/eval_jaxpr/ppermute | solution.py:10
  244.1 6.8 %collective-permute-start = (f32[8,64,256]{2,1,0:T(8,128)S(1)}, f32[8,64,256]{2,1,0:T(8,128)S(1)}, u32[]{:S(2)}, u32[]{:S(2)}) collective-permute-start(f32[8,64,256]{2,1,0:T(8,128)S(1)} %copy.76), channel_id=1, source_target_pairs={{0,15},{1,0},{2,1},{3,2},{4,3},{5,4},{6,5},{7,6},{8,7},{9,8},{10,9... | collective-permute-start | bytes 1572872 | tf_op jit(solution)/shard_map/while/body/eval_jaxpr/ppermute | solution.py:10
  261.9 6.8 %collective-permute-start = (f32[8,64,256]{2,1,0:T(8,128)S(1)}, f32[8,64,256]{2,1,0:T(8,128)S(1)}, u32[]{:S(2)}, u32[]{:S(2)}) collective-permute-start(f32[8,64,256]{2,1,0:T(8,128)S(1)} %copy.76), channel_id=1, source_target_pairs={{0,15},{1,0},{2,1},{3,2},{4,3},{5,4},{6,5},{7,6},{8,7},{9,8},{10,9... | collective-permute-start | bytes 1572872 | tf_op jit(solution)/shard_map/while/body/eval_jaxpr/ppermute | solution.py:10
  279.7 6.8 %collective-permute-start = (f32[8,64,256]{2,1,0:T(8,128)S(1)}, f32[8,64,256]{2,1,0:T(8,128)S(1)}, u32[]{:S(2)}, u32[]{:S(2)}) collective-permute-start(f32[8,64,256]{2,1,0:T(8,128)S(1)} %copy.76), channel_id=1, source_target_pairs={{0,15},{1,0},{2,1},{3,2},{4,3},{5,4},{6,5},{7,6},{8,7},{9,8},{10,9... | collective-permute-start | bytes 1572872 | tf_op jit(solution)/shard_map/while/body/eval_jaxpr/ppermute | solution.py:10
  297.6 6.8 %collective-permute-start = (f32[8,64,256]{2,1,0:T(8,128)S(1)}, f32[8,64,256]{2,1,0:T(8,128)S(1)}, u32[]{:S(2)}, u32[]{:S(2)}) collective-permute-start(f32[8,64,256]{2,1,0:T(8,128)S(1)} %copy.76), channel_id=1, source_target_pairs={{0,15},{1,0},{2,1},{3,2},{4,3},{5,4},{6,5},{7,6},{8,7},{9,8},{10,9... | collective-permute-start | bytes 1572872 | tf_op jit(solution)/shard_map/while/body/eval_jaxpr/ppermute | solution.py:10
  315.4 6.9 %collective-permute-start = (f32[8,64,256]{2,1,0:T(8,128)S(1)}, f32[8,64,256]{2,1,0:T(8,128)S(1)}, u32[]{:S(2)}, u32[]{:S(2)}) collective-permute-start(f32[8,64,256]{2,1,0:T(8,128)S(1)} %copy.76), channel_id=1, source_target_pairs={{0,15},{1,0},{2,1},{3,2},{4,3},{5,4},{6,5},{7,6},{8,7},{9,8},{10,9... | collective-permute-start | bytes 1572872 | tf_op jit(solution)/shard_map/while/body/eval_jaxpr/ppermute | solution.py:10
  333.3 6.8 %collective-permute-start = (f32[8,64,256]{2,1,0:T(8,128)S(1)}, f32[8,64,256]{2,1,0:T(8,128)S(1)}, u32[]{:S(2)}, u32[]{:S(2)}) collective-permute-start(f32[8,64,256]{2,1,0:T(8,128)S(1)} %copy.76), channel_id=1, source_target_pairs={{0,15},{1,0},{2,1},{3,2},{4,3},{5,4},{6,5},{7,6},{8,7},{9,8},{10,9... | collective-permute-start | bytes 1572872 | tf_op jit(solution)/shard_map/while/body/eval_jaxpr/ppermute | solution.py:10
  359.4 7.8 %collective-permute-done.11 = f32[4,64,256]{2,1,0:T(8,128)S(1)} collective-permute-done((f32[4,64,256]{2,1,0:T(8,128)S(1)}, f32[4,64,256]{2,1,0:T(8,128)S(1)}, u32[]{:S(2)}, u32[]{:S(2)}) %collective-permute-start.11) | collective-permute-done | bytes 262176 | tf_op jit(solution)/shard_map/ppermute | solution.py:10
  369.1 11.7 %collective-permute-done.12 = f32[2,4,64,256]{3,2,1,0:T(8,128)S(1)} collective-permute-done((f32[2,4,64,256]{3,2,1,0:T(8,128)S(1)}, f32[2,4,64,256]{3,2,1,0:T(8,128)S(1)}, u32[]{:S(2)}, u32[]{:S(2)}) %collective-permute-start.12) | collective-permute-done | bytes 524320 | tf_op jit(solution)/shard_map/ppermute | solution.py:10
  381.0 10.7 %collective-permute-done.13 = f32[2,4,64,256]{3,2,1,0:T(8,128)S(1)} collective-permute-done((f32[2,4,64,256]{3,2,1,0:T(8,128)S(1)}, f32[2,4,64,256]{3,2,1,0:T(8,128)S(1)}, u32[]{:S(2)}, u32[]{:S(2)}) %collective-permute-start.13) | collective-permute-done | bytes 524320 | tf_op jit(solution)/shard_map/ppermute | solution.py:10
  391.7 4.9 collective-permute-start.14
  396.7 9.5 %collective-permute-done.14 = f32[2,4,64,256]{3,2,1,0:T(8,128)S(1)} collective-permute-done((f32[2,4,64,256]{3,2,1,0:T(8,128)S(1)}, f32[2,4,64,256]{3,2,1,0:T(8,128)S(1)}, u32[]{:S(2)}, u32[]{:S(2)}) %collective-permute-start.14) | collective-permute-done | bytes 524320 | tf_op jit(solution)/shard_map/ppermute | solution.py:10
  406.3 244.6 %while.47 = (s32[]{:T(128)}, f32[512,256]{1,0:T(8,128)}, f32[8,64,256]{2,1,0:T(8,128)S(1)}, f32[2,4,64,256]{3,2,1,0:T(8,128)S(1)}, s32[]{:T(128)}, /*index=5*/s3...) while((s32[]{:T(128)}, f32[512,256]{1,0:T(8,128)}, ...), condition=%wide.region_3.8_spmd.clone.clone, body=%wide.region_2.7_spmd.clone.clone.sunk | while | flops 412485152 | bytes 18358452 | solution.py:99
  407.2 6.7 %collective-permute-start.3 = (f32[4,64,256]{2,1,0:T(8,128)}, f32[4,64,256]{2,1,0:T(8,128)}, u32[]{:S(2)}, u32[]{:S(2)}) collective-permute-start(f32[4,64,256]{2,1,0:T(8,128)} %get-tuple-element.969), channel_id=1, source_target_pairs={{0,112},{16,0},{32,16},{48,32},{64,48},{80,64},{96,80},{112,96},{1... | collective-permute-start | bytes 786440 | tf_op jit(solution)/shard_map/while/body/eval_jaxpr/ppermute | solution.py:10
  413.9 12.5 %collective-permute-start.2 = (f32[8,64,256]{2,1,0:T(8,128)S(1)}, f32[8,64,256]{2,1,0:T(8,128)S(1)}, u32[]{:S(2)}, u32[]{:S(2)}) collective-permute-start(f32[8,64,256]{2,1,0:T(8,128)S(1)} %copy.88), channel_id=1, source_target_pairs={{0,15},{1,0},{2,1},{3,2},{4,3},{5,4},{6,5},{7,6},{8,7},{9,8},{10,9... | collective-permute-start | bytes 1572872 | tf_op jit(solution)/shard_map/while/body/eval_jaxpr/ppermute | solution.py:10
  543.6 5.2 collective-permute-start.2
  588.6 6.2 collective-permute-start.2
  634.7 6.2 collective-permute-start.2
  (1032 shorter events, 426.5 us)
Async XLA Ops:
  0.0 24.2 %collective-permute-start.4 = (f32[8,64,256]{2,1,0:T(8,128)}, f32[8,64,256]{2,1,0:T(8,128)S(1)}, u32[]{:S(2)}, u32[]{:S(2)}) collective-permute-start(f32[8,64,256]{2,1,0:T(8,128)} %param.15), channel_id=1, source_target_pairs={{0,14},{1,15},{2,0},{3,1},{4,2},{5,3},{6,4},{7,5},{8,6},{9,7},{10,... | collective-permute-start | bytes 1572872 | tf_op jit(solution)/shard_map/ppermute | solution.py:10
  15.2 16.2 %collective-permute-start.8 = (f32[2,4,64,256]{3,2,1,0:T(8,128)S(1)}, f32[2,4,64,256]{3,2,1,0:T(8,128)}, u32[]{:S(2)}, u32[]{:S(2)}) collective-permute-start(f32[2,4,64,256]{3,2,1,0:T(8,128)S(1)} %maximum_select_fusion), channel_id=1, source_target_pairs={{0,112},{16,0},{32,16},{48,32},{64,48},{80,64},{96,80},{112,96},{1... | collective-permute-start | bytes 1572872 | tf_op jit(solution)/shard_map/ppermute | solution.py:10
  38.1 21.8 %collective-permute-start.6 = (f32[8,64,256]{2,1,0:T(8,128)S(1)}, f32[8,64,256]{2,1,0:T(8,128)}, u32[]{:S(2)}, u32[]{:S(2)}) collective-permute-start(f32[8,64,256]{2,1,0:T(8,128)S(1)} %broadcast_select_fusion.9), channel_id=1, source_target_pairs={{0,8},{1,9},{2,10},{3,11},{4,12},{5,13},{6,14},{7,15},{8,0},{9,1},... | collective-permute-start | bytes 1572872 | tf_op jit(solution)/shard_map/ppermute | solution.py:10
  46.3 20.8 %collective-permute-start.10 = (f32[2,4,64,256]{3,2,1,0:T(8,128)S(1)}, f32[2,4,64,256]{3,2,1,0:T(8,128)S(1)}, u32[]{:S(2)}, u32[]{:S(2)}) collective-permute-start(f32[2,4,64,256]{3,2,1,0:T(8,128)S(1)} %broadcast_select_fusion.5), channel_id=1, source_target_pairs={{0,64},{16,80},{32,96},{48,112},{64,0},{80,16},{96,32},{112,48},{1... | collective-permute-start | bytes 1572872 | tf_op jit(solution)/shard_map/ppermute | solution.py:10
  69.0 30.1 %collective-permute-start.1 = (f32[4,64,256]{2,1,0:T(8,128)}, f32[4,64,256]{2,1,0:T(8,128)}, u32[]{:S(2)}, u32[]{:S(2)}) collective-permute-start(f32[4,64,256]{2,1,0:T(8,128)} %get-tuple-element.956), channel_id=1, source_target_pairs={{0,112},{16,0},{32,16},{48,32},{64,48},{80,64},{96,80},{112,96},{1... | collective-permute-start | bytes 786440 | tf_op jit(solution)/shard_map/while/body/eval_jaxpr/ppermute | solution.py:10
  69.3 30.9 %collective-permute-start = (f32[8,64,256]{2,1,0:T(8,128)S(1)}, f32[8,64,256]{2,1,0:T(8,128)S(1)}, u32[]{:S(2)}, u32[]{:S(2)}) collective-permute-start(f32[8,64,256]{2,1,0:T(8,128)S(1)} %copy.76), channel_id=1, source_target_pairs={{0,15},{1,0},{2,1},{3,2},{4,3},{5,4},{6,5},{7,6},{8,7},{9,8},{10,9... | collective-permute-start | bytes 1572872 | tf_op jit(solution)/shard_map/while/body/eval_jaxpr/ppermute | solution.py:10
  101.2 16.4 %collective-permute-start = (f32[8,64,256]{2,1,0:T(8,128)S(1)}, f32[8,64,256]{2,1,0:T(8,128)S(1)}, u32[]{:S(2)}, u32[]{:S(2)}) collective-permute-start(f32[8,64,256]{2,1,0:T(8,128)S(1)} %copy.76), channel_id=1, source_target_pairs={{0,15},{1,0},{2,1},{3,2},{4,3},{5,4},{6,5},{7,6},{8,7},{9,8},{10,9... | collective-permute-start | bytes 1572872 | tf_op jit(solution)/shard_map/while/body/eval_jaxpr/ppermute | solution.py:10
  118.5 16.2 %collective-permute-start.1 = (f32[4,64,256]{2,1,0:T(8,128)}, f32[4,64,256]{2,1,0:T(8,128)}, u32[]{:S(2)}, u32[]{:S(2)}) collective-permute-start(f32[4,64,256]{2,1,0:T(8,128)} %get-tuple-element.956), channel_id=1, source_target_pairs={{0,112},{16,0},{32,16},{48,32},{64,48},{80,64},{96,80},{112,96},{1... | collective-permute-start | bytes 786440 | tf_op jit(solution)/shard_map/while/body/eval_jaxpr/ppermute | solution.py:10
  136.9 16.7 %collective-permute-start.1 = (f32[4,64,256]{2,1,0:T(8,128)}, f32[4,64,256]{2,1,0:T(8,128)}, u32[]{:S(2)}, u32[]{:S(2)}) collective-permute-start(f32[4,64,256]{2,1,0:T(8,128)} %get-tuple-element.956), channel_id=1, source_target_pairs={{0,112},{16,0},{32,16},{48,32},{64,48},{80,64},{96,80},{112,96},{1... | collective-permute-start | bytes 786440 | tf_op jit(solution)/shard_map/while/body/eval_jaxpr/ppermute | solution.py:10
  136.9 17.9 %collective-permute-start = (f32[8,64,256]{2,1,0:T(8,128)S(1)}, f32[8,64,256]{2,1,0:T(8,128)S(1)}, u32[]{:S(2)}, u32[]{:S(2)}) collective-permute-start(f32[8,64,256]{2,1,0:T(8,128)S(1)} %copy.76), channel_id=1, source_target_pairs={{0,15},{1,0},{2,1},{3,2},{4,3},{5,4},{6,5},{7,6},{8,7},{9,8},{10,9... | collective-permute-start | bytes 1572872 | tf_op jit(solution)/shard_map/while/body/eval_jaxpr/ppermute | solution.py:10
  155.7 16.0 %collective-permute-start = (f32[8,64,256]{2,1,0:T(8,128)S(1)}, f32[8,64,256]{2,1,0:T(8,128)S(1)}, u32[]{:S(2)}, u32[]{:S(2)}) collective-permute-start(f32[8,64,256]{2,1,0:T(8,128)S(1)} %copy.76), channel_id=1, source_target_pairs={{0,15},{1,0},{2,1},{3,2},{4,3},{5,4},{6,5},{7,6},{8,7},{9,8},{10,9... | collective-permute-start | bytes 1572872 | tf_op jit(solution)/shard_map/while/body/eval_jaxpr/ppermute | solution.py:10
  172.7 15.7 %collective-permute-start.1 = (f32[4,64,256]{2,1,0:T(8,128)}, f32[4,64,256]{2,1,0:T(8,128)}, u32[]{:S(2)}, u32[]{:S(2)}) collective-permute-start(f32[4,64,256]{2,1,0:T(8,128)} %get-tuple-element.956), channel_id=1, source_target_pairs={{0,112},{16,0},{32,16},{48,32},{64,48},{80,64},{96,80},{112,96},{1... | collective-permute-start | bytes 786440 | tf_op jit(solution)/shard_map/while/body/eval_jaxpr/ppermute | solution.py:10
  172.7 16.9 %collective-permute-start = (f32[8,64,256]{2,1,0:T(8,128)S(1)}, f32[8,64,256]{2,1,0:T(8,128)S(1)}, u32[]{:S(2)}, u32[]{:S(2)}) collective-permute-start(f32[8,64,256]{2,1,0:T(8,128)S(1)} %copy.76), channel_id=1, source_target_pairs={{0,15},{1,0},{2,1},{3,2},{4,3},{5,4},{6,5},{7,6},{8,7},{9,8},{10,9... | collective-permute-start | bytes 1572872 | tf_op jit(solution)/shard_map/while/body/eval_jaxpr/ppermute | solution.py:10
  190.5 15.7 %collective-permute-start.1 = (f32[4,64,256]{2,1,0:T(8,128)}, f32[4,64,256]{2,1,0:T(8,128)}, u32[]{:S(2)}, u32[]{:S(2)}) collective-permute-start(f32[4,64,256]{2,1,0:T(8,128)} %get-tuple-element.956), channel_id=1, source_target_pairs={{0,112},{16,0},{32,16},{48,32},{64,48},{80,64},{96,80},{112,96},{1... | collective-permute-start | bytes 786440 | tf_op jit(solution)/shard_map/while/body/eval_jaxpr/ppermute | solution.py:10
  190.6 16.9 %collective-permute-start = (f32[8,64,256]{2,1,0:T(8,128)S(1)}, f32[8,64,256]{2,1,0:T(8,128)S(1)}, u32[]{:S(2)}, u32[]{:S(2)}) collective-permute-start(f32[8,64,256]{2,1,0:T(8,128)S(1)} %copy.76), channel_id=1, source_target_pairs={{0,15},{1,0},{2,1},{3,2},{4,3},{5,4},{6,5},{7,6},{8,7},{9,8},{10,9... | collective-permute-start | bytes 1572872 | tf_op jit(solution)/shard_map/while/body/eval_jaxpr/ppermute | solution.py:10
  208.3 15.7 %collective-permute-start.1 = (f32[4,64,256]{2,1,0:T(8,128)}, f32[4,64,256]{2,1,0:T(8,128)}, u32[]{:S(2)}, u32[]{:S(2)}) collective-permute-start(f32[4,64,256]{2,1,0:T(8,128)} %get-tuple-element.956), channel_id=1, source_target_pairs={{0,112},{16,0},{32,16},{48,32},{64,48},{80,64},{96,80},{112,96},{1... | collective-permute-start | bytes 786440 | tf_op jit(solution)/shard_map/while/body/eval_jaxpr/ppermute | solution.py:10
  208.4 16.9 %collective-permute-start = (f32[8,64,256]{2,1,0:T(8,128)S(1)}, f32[8,64,256]{2,1,0:T(8,128)S(1)}, u32[]{:S(2)}, u32[]{:S(2)}) collective-permute-start(f32[8,64,256]{2,1,0:T(8,128)S(1)} %copy.76), channel_id=1, source_target_pairs={{0,15},{1,0},{2,1},{3,2},{4,3},{5,4},{6,5},{7,6},{8,7},{9,8},{10,9... | collective-permute-start | bytes 1572872 | tf_op jit(solution)/shard_map/while/body/eval_jaxpr/ppermute | solution.py:10
  226.2 15.8 %collective-permute-start.1 = (f32[4,64,256]{2,1,0:T(8,128)}, f32[4,64,256]{2,1,0:T(8,128)}, u32[]{:S(2)}, u32[]{:S(2)}) collective-permute-start(f32[4,64,256]{2,1,0:T(8,128)} %get-tuple-element.956), channel_id=1, source_target_pairs={{0,112},{16,0},{32,16},{48,32},{64,48},{80,64},{96,80},{112,96},{1... | collective-permute-start | bytes 786440 | tf_op jit(solution)/shard_map/while/body/eval_jaxpr/ppermute | solution.py:10
  226.2 16.9 %collective-permute-start = (f32[8,64,256]{2,1,0:T(8,128)S(1)}, f32[8,64,256]{2,1,0:T(8,128)S(1)}, u32[]{:S(2)}, u32[]{:S(2)}) collective-permute-start(f32[8,64,256]{2,1,0:T(8,128)S(1)} %copy.76), channel_id=1, source_target_pairs={{0,15},{1,0},{2,1},{3,2},{4,3},{5,4},{6,5},{7,6},{8,7},{9,8},{10,9... | collective-permute-start | bytes 1572872 | tf_op jit(solution)/shard_map/while/body/eval_jaxpr/ppermute | solution.py:10
  244.1 16.9 %collective-permute-start = (f32[8,64,256]{2,1,0:T(8,128)S(1)}, f32[8,64,256]{2,1,0:T(8,128)S(1)}, u32[]{:S(2)}, u32[]{:S(2)}) collective-permute-start(f32[8,64,256]{2,1,0:T(8,128)S(1)} %copy.76), channel_id=1, source_target_pairs={{0,15},{1,0},{2,1},{3,2},{4,3},{5,4},{6,5},{7,6},{8,7},{9,8},{10,9... | collective-permute-start | bytes 1572872 | tf_op jit(solution)/shard_map/while/body/eval_jaxpr/ppermute | solution.py:10
  261.9 15.7 %collective-permute-start.1 = (f32[4,64,256]{2,1,0:T(8,128)}, f32[4,64,256]{2,1,0:T(8,128)}, u32[]{:S(2)}, u32[]{:S(2)}) collective-permute-start(f32[4,64,256]{2,1,0:T(8,128)} %get-tuple-element.956), channel_id=1, source_target_pairs={{0,112},{16,0},{32,16},{48,32},{64,48},{80,64},{96,80},{112,96},{1... | collective-permute-start | bytes 786440 | tf_op jit(solution)/shard_map/while/body/eval_jaxpr/ppermute | solution.py:10
  261.9 16.9 %collective-permute-start = (f32[8,64,256]{2,1,0:T(8,128)S(1)}, f32[8,64,256]{2,1,0:T(8,128)S(1)}, u32[]{:S(2)}, u32[]{:S(2)}) collective-permute-start(f32[8,64,256]{2,1,0:T(8,128)S(1)} %copy.76), channel_id=1, source_target_pairs={{0,15},{1,0},{2,1},{3,2},{4,3},{5,4},{6,5},{7,6},{8,7},{9,8},{10,9... | collective-permute-start | bytes 1572872 | tf_op jit(solution)/shard_map/while/body/eval_jaxpr/ppermute | solution.py:10
  279.7 15.8 %collective-permute-start.1 = (f32[4,64,256]{2,1,0:T(8,128)}, f32[4,64,256]{2,1,0:T(8,128)}, u32[]{:S(2)}, u32[]{:S(2)}) collective-permute-start(f32[4,64,256]{2,1,0:T(8,128)} %get-tuple-element.956), channel_id=1, source_target_pairs={{0,112},{16,0},{32,16},{48,32},{64,48},{80,64},{96,80},{112,96},{1... | collective-permute-start | bytes 786440 | tf_op jit(solution)/shard_map/while/body/eval_jaxpr/ppermute | solution.py:10
  279.7 16.9 %collective-permute-start = (f32[8,64,256]{2,1,0:T(8,128)S(1)}, f32[8,64,256]{2,1,0:T(8,128)S(1)}, u32[]{:S(2)}, u32[]{:S(2)}) collective-permute-start(f32[8,64,256]{2,1,0:T(8,128)S(1)} %copy.76), channel_id=1, source_target_pairs={{0,15},{1,0},{2,1},{3,2},{4,3},{5,4},{6,5},{7,6},{8,7},{9,8},{10,9... | collective-permute-start | bytes 1572872 | tf_op jit(solution)/shard_map/while/body/eval_jaxpr/ppermute | solution.py:10
  297.6 16.9 %collective-permute-start = (f32[8,64,256]{2,1,0:T(8,128)S(1)}, f32[8,64,256]{2,1,0:T(8,128)S(1)}, u32[]{:S(2)}, u32[]{:S(2)}) collective-permute-start(f32[8,64,256]{2,1,0:T(8,128)S(1)} %copy.76), channel_id=1, source_target_pairs={{0,15},{1,0},{2,1},{3,2},{4,3},{5,4},{6,5},{7,6},{8,7},{9,8},{10,9... | collective-permute-start | bytes 1572872 | tf_op jit(solution)/shard_map/while/body/eval_jaxpr/ppermute | solution.py:10
  315.4 15.8 %collective-permute-start.1 = (f32[4,64,256]{2,1,0:T(8,128)}, f32[4,64,256]{2,1,0:T(8,128)}, u32[]{:S(2)}, u32[]{:S(2)}) collective-permute-start(f32[4,64,256]{2,1,0:T(8,128)} %get-tuple-element.956), channel_id=1, source_target_pairs={{0,112},{16,0},{32,16},{48,32},{64,48},{80,64},{96,80},{112,96},{1... | collective-permute-start | bytes 786440 | tf_op jit(solution)/shard_map/while/body/eval_jaxpr/ppermute | solution.py:10
  315.4 16.9 %collective-permute-start = (f32[8,64,256]{2,1,0:T(8,128)S(1)}, f32[8,64,256]{2,1,0:T(8,128)S(1)}, u32[]{:S(2)}, u32[]{:S(2)}) collective-permute-start(f32[8,64,256]{2,1,0:T(8,128)S(1)} %copy.76), channel_id=1, source_target_pairs={{0,15},{1,0},{2,1},{3,2},{4,3},{5,4},{6,5},{7,6},{8,7},{9,8},{10,9... | collective-permute-start | bytes 1572872 | tf_op jit(solution)/shard_map/while/body/eval_jaxpr/ppermute | solution.py:10
  333.3 16.9 %collective-permute-start = (f32[8,64,256]{2,1,0:T(8,128)S(1)}, f32[8,64,256]{2,1,0:T(8,128)S(1)}, u32[]{:S(2)}, u32[]{:S(2)}) collective-permute-start(f32[8,64,256]{2,1,0:T(8,128)S(1)} %copy.76), channel_id=1, source_target_pairs={{0,15},{1,0},{2,1},{3,2},{4,3},{5,4},{6,5},{7,6},{8,7},{9,8},{10,9... | collective-permute-start | bytes 1572872 | tf_op jit(solution)/shard_map/while/body/eval_jaxpr/ppermute | solution.py:10
  407.2 28.1 %collective-permute-start.3 = (f32[4,64,256]{2,1,0:T(8,128)}, f32[4,64,256]{2,1,0:T(8,128)}, u32[]{:S(2)}, u32[]{:S(2)}) collective-permute-start(f32[4,64,256]{2,1,0:T(8,128)} %get-tuple-element.969), channel_id=1, source_target_pairs={{0,112},{16,0},{32,16},{48,32},{64,48},{80,64},{96,80},{112,96},{1... | collective-permute-start | bytes 786440 | tf_op jit(solution)/shard_map/while/body/eval_jaxpr/ppermute | solution.py:10
  413.9 22.5 %collective-permute-start.2 = (f32[8,64,256]{2,1,0:T(8,128)S(1)}, f32[8,64,256]{2,1,0:T(8,128)S(1)}, u32[]{:S(2)}, u32[]{:S(2)}) collective-permute-start(f32[8,64,256]{2,1,0:T(8,128)S(1)} %copy.88), channel_id=1, source_target_pairs={{0,15},{1,0},{2,1},{3,2},{4,3},{5,4},{6,5},{7,6},{8,7},{9,8},{10,9... | collective-permute-start | bytes 1572872 | tf_op jit(solution)/shard_map/while/body/eval_jaxpr/ppermute | solution.py:10
  588.6 16.2 %collective-permute-start.2 = (f32[8,64,256]{2,1,0:T(8,128)S(1)}, f32[8,64,256]{2,1,0:T(8,128)S(1)}, u32[]{:S(2)}, u32[]{:S(2)}) collective-permute-start(f32[8,64,256]{2,1,0:T(8,128)S(1)} %copy.88), channel_id=1, source_target_pairs={{0,15},{1,0},{2,1},{3,2},{4,3},{5,4},{6,5},{7,6},{8,7},{9,8},{10,9... | collective-permute-start | bytes 1572872 | tf_op jit(solution)/shard_map/while/body/eval_jaxpr/ppermute | solution.py:10
  634.7 16.2 %collective-permute-start.2 = (f32[8,64,256]{2,1,0:T(8,128)S(1)}, f32[8,64,256]{2,1,0:T(8,128)S(1)}, u32[]{:S(2)}, u32[]{:S(2)}) collective-permute-start(f32[8,64,256]{2,1,0:T(8,128)S(1)} %copy.88), channel_id=1, source_target_pairs={{0,15},{1,0},{2,1},{3,2},{4,3},{5,4},{6,5},{7,6},{8,7},{9,8},{10,9... | collective-permute-start | bytes 1572872 | tf_op jit(solution)/shard_map/while/body/eval_jaxpr/ppermute | solution.py:10
  (147 other events, 670.3 us)
where the time goes:
time: 667 us; the launch traced here: 659 us
  starting transfers between devices  226 us (34%)
  local copies, waits for them, and re-layouts  183 us (27%)
  other arithmetic  92.5 us (14%)
  matrix products  82 us (12%)
  waiting for transfers between devices  70.7 us (11%)
    ppermute x71, starting transfers between devices, from_behind(): return lax.ppermute(value, axis, pairs)  226 us
    ppermute x71, waiting for transfers between devices, from_behind(): return lax.ppermute(value, axis, pairs)  70.7 us
    dot_general x64, matrix products, spread_blocks(): jnp.einsum('rman,raj->rmjn', blocks, onehot, precision=lax.Precision.HIGH...  54.4 us
    gather x31, local copies, waits for them, and re-layouts, local_product(): pattern_counts[right_rows]  40.8 us
    concatenate x30, other arithmetic, rotate_lanes(): return jnp.concatenate([lane_stack[1:], incoming[None]], axis=0)  31.5 us
    slice x32, local copies, waits for them, and re-layouts, rotate_lanes(): return jnp.concatenate([lane_stack[1:], incoming[None]], axis=0)  27.7 us
    while x210, local copies, waits for them, and re-layouts  25.5 us
    dot_general x32, matrix products, local_product(): jnp.dot(left_dense.reshape(row_count * block_size, dense_width), right_de...  25.4 us
  transfers between devices with their start and end apart: 71, of which 10 were waited for; matrix products, arithmetic and copies ran while one was open for 44% of the time, Pallas kernels for 0%

commit v1 on v0

v1 whole, which is shorter than its diff:
```python
import jax
import jax.numpy as jnp
from jax import lax
from jax.experimental import pallas as pl
from jax.experimental.pallas import tpu as pltpu
from jax.sharding import PartitionSpec as P

ROWS = 8
BS = 64
SHORT = 3
REST = ROWS - SHORT
RING = 4
SIDES = 8
VMEM = pl.BlockSpec(memory_space=pltpu.VMEM)
SMEM = pl.BlockSpec(memory_space=pltpu.SMEM)
BF16 = jnp.bfloat16
F32 = jnp.float32


def is_near(row, chip):
    ahead = (chip - row + SIDES) % SIDES
    return (ahead <= 1) | (ahead == SIDES - 1)


def chip_moves(along_row, flip, shift, near_only):
    pairs = []
    for row in range(SIDES):
        for chip in range(SIDES):
            if near_only and not is_near(row, chip):
                continue
            place = chip if along_row else row
            half, at = divmod(place, RING)
            place = (half ^ flip) * RING + (at + shift) % RING
            target = (row, place) if along_row else (place, chip)
            for core in range(2):
                pairs.append(((row * SIDES + chip) * 2 + core, (target[0] * SIDES + target[1]) * 2 + core))
    return pairs


def move(value, along_row, flip, shift, near_only=False):
    return lax.ppermute(value, ("row", "col"), chip_moves(along_row, flip, shift, near_only))


def other_core(value):
    return lax.ppermute(value, "col", [(c, c ^ 1) for c in range(2 * SIDES)])


def read_code(code):
    return [(code >> (2 * a)) & 3 for a in range(4)], code >> 8


def low_lanes():
    return lax.broadcasted_iota(jnp.int32, (1, 128), 1) < BS


def lane_mask(low, when_low, when_high):
    return jnp.where(low, when_low.astype(jnp.int32), when_high.astype(jnp.int32)) != 0


def turned(half):
    return pltpu.roll(half, BS, 1)


def spread_row(tile, code):
    cols, count = read_code(code)
    low = low_lanes()
    first, second = tile[:, :128], tile[:, 128:]
    views = [(first, 0, 1), (turned(first), 1, 0), (second, 2, 3), (turned(second), 3, 2)]
    halves = []
    for t in range(2):
        dense = jnp.zeros((BS, 128), F32)
        for view, a, b in views:
            mask = lane_mask(low, (cols[a] == 2 * t) & (count > a), (cols[b] == 2 * t + 1) & (count > b))
            dense = jnp.where(mask, view, dense)
        halves.append(dense)
    return halves


def collect_row(tile, code):
    cols, count = read_code(code)
    low = low_lanes()
    first, second = tile[:, :128], tile[:, 128:]
    views = [(first, 0, 1), (turned(first), 1, 0), (second, 2, 3), (turned(second), 3, 2)]
    halves = []
    for u in range(2):
        slots = jnp.zeros((BS, 128), F32)
        for view, j, k in views:
            mask = lane_mask(
                low, (cols[2 * u] == j) & (count > 2 * u), (cols[2 * u + 1] == k) & (count > 2 * u + 1)
            )
            slots = jnp.where(mask, view, slots)
        halves.append(slots)
    return halves


def full_row(code_ref, row, panel):
    at = jnp.int32(0)
    for i in range(ROWS):
        at = jnp.where((code_ref[row * ROWS + i, panel] >> 8) > 1, i, at)
    return at


def pack(read, out_ref, code_ref, row, chip, panel):
    near = is_near(row, chip)

    @pl.when(near)
    def _():
        for i in range(ROWS):
            out_ref[i] = read(i)

    @pl.when(jnp.logical_not(near))
    def _():
        low = low_lanes()
        for g in range(2):
            for h in range(2):
                i = 4 * g + 2 * h
                out_ref[g, :, 128 * h : 128 * h + 128] = jnp.where(
                    low, read(i)[:, :128], turned(read(i + 1)[:, :128])
                )
        out_ref[2] = read(full_row(code_ref, row, panel))
        for i in range(SHORT, ROWS):
            out_ref[i] = jnp.zeros((BS, 256), F32)


def put(halves, hi_ref, lo_ref, at, i):
    rows = pl.ds(pl.multiple_of(i * BS, BS), BS)
    for t in range(2):
        hi = halves[t].astype(BF16)
        hi_ref[at, rows, 128 * t : 128 * t + 128] = hi
        lo_ref[at, rows, 128 * t : 128 * t + 128] = (halves[t] - hi.astype(F32)).astype(BF16)


def unpack(short_ref, short_at, rest_ref, rest_at, code_ref, row, panel, hi_ref, lo_ref, at):
    near = is_near(row, panel // 2)

    @pl.when(near)
    def _():
        @pl.loop(0, SHORT)
        def _(i):
            put(spread_row(short_ref[short_at + i], code_ref[row * ROWS + i, panel]), hi_ref, lo_ref, at, i)

        @pl.loop(SHORT, ROWS)
        def _(i):
            put(spread_row(rest_ref[rest_at + i - SHORT], code_ref[row * ROWS + i, panel]), hi_ref, lo_ref, at, i)

    @pl.when(jnp.logical_not(near))
    def _():
        low = low_lanes()
        for i in range(ROWS):
            code = code_ref[row * ROWS + i, panel]
            col, used = code & 3, (code >> 8) > 0
            h = (i % 4) // 2
            view = short_ref[short_at + i // 4, :, 128 * h : 128 * h + 128]
            other = turned(view)
            if i % 2 == 1:
                view, other = other, view
            halves = []
            for t in range(2):
                dense = jnp.where(lane_mask(low, (col == 2 * t) & used, jnp.bool_(False)), view, 0.0)
                dense = jnp.where(lane_mask(low, jnp.bool_(False), (col == 2 * t + 1) & used), other, dense)
                halves.append(dense)
            put(halves, hi_ref, lo_ref, at, i)
        full = full_row(code_ref, row, panel)
        put(spread_row(short_ref[short_at + 2], code_ref[row * ROWS + full, panel]), hi_ref, lo_ref, at, full)


def position():
    row = lax.axis_index("row")
    panel = lax.axis_index("col")
    return row, panel // 2, panel % 2, panel


def unpack_ring(parts, along_row, core, code_ref, hi_ref, lo_ref):
    row, chip, _, panel = position()
    place = chip if along_row else row
    half, spot = place // RING, place % RING
    for s, (short_ref, both_ref) in enumerate(parts):
        for flip in range(2):
            source = (half if flip == 0 else 1 - half) * RING + (spot - s + RING) % RING
            from_row, from_panel = (row, 2 * source + core) if along_row else (source, panel)
            unpack(
                short_ref if flip == 0 else both_ref,
                0,
                both_ref,
                SHORT,
                code_ref,
                from_row,
                from_panel,
                hi_ref,
                lo_ref,
                from_panel if along_row else from_row,
            )


def multiply(left_hi, left_lo, right_hi, right_lo, total):
    total[...] = jnp.zeros_like(total)

    @pl.loop(0, SIDES)
    def _(k):
        acc = total[...]
        for p in range(2):
            rows = pl.ds(256 * p, 256)
            a_hi, a_lo = left_hi[2 * k + p], left_lo[2 * k + p]
            b_hi, b_lo = right_hi[k, rows, :], right_lo[k, rows, :]
            acc += jnp.dot(a_hi, b_hi, preferred_element_type=F32)
            acc += jnp.dot(a_lo, b_hi, preferred_element_type=F32)
            acc += jnp.dot(a_hi, b_lo, preferred_element_type=F32)
        total[...] = acc


def pack_kernel(code_ref, matrix_ref, out_ref):
    row, chip, _, panel = position()
    pack(lambda i: matrix_ref[i], out_ref, code_ref, row, chip, panel)


def left_kernel(code_ref, *refs):
    mine = [(refs[2 * s], refs[2 * s + 1]) for s in range(RING)]
    others = [(refs[8 + 2 * s], refs[8 + 2 * s + 1]) for s in range(RING)]
    hi_ref, lo_ref = refs[16:]
    core = position()[2]
    unpack_ring(mine, True, core, code_ref, hi_ref, lo_ref)
    unpack_ring(others, True, 1 - core, code_ref, hi_ref, lo_ref)


def square_kernel(code_ref, left_hi, left_lo, *refs):
    parts = [(refs[2 * s], refs[2 * s + 1]) for s in range(RING)]
    out_ref, right_hi, right_lo, total, slots = refs[8:]
    row, chip, _, panel = position()
    unpack_ring(parts, False, None, code_ref, right_hi, right_lo)
    multiply(left_hi, left_lo, right_hi, right_lo, total)

    @pl.loop(0, ROWS)
    def _(i):
        tile = total[pl.ds(pl.multiple_of(i * BS, BS), BS), :]
        at_row = (row * ROWS + i) * BS + lax.broadcasted_iota(jnp.int32, (BS, 256), 0)
        at_col = panel * 256 + lax.broadcasted_iota(jnp.int32, (BS, 256), 1)
        tile = jnp.where(at_row == at_col, 3.0, 0.0) - tile
        first, second = collect_row(tile, code_ref[row * ROWS + i, panel])
        slots[i, :, :128] = first
        slots[i, :, 128:] = second

    pack(lambda i: slots[i], out_ref, code_ref, row, chip, panel)


def result_kernel(code_ref, left_hi, left_lo, *refs):
    parts = [(refs[2 * s], refs[2 * s + 1]) for s in range(RING)]
    out_ref, right_hi, right_lo, total = refs[8:]
    row, chip, _, panel = position()
    unpack_ring(parts, False, None, code_ref, right_hi, right_lo)
    multiply(left_hi, left_lo, right_hi, right_lo, total)

    @pl.loop(0, ROWS)
    def _(i):
        tile = 0.5 * total[pl.ds(pl.multiple_of(i * BS, BS), BS), :]
        first, second = collect_row(tile, code_ref[row * ROWS + i, panel])
        out_ref[i, :, :128] = first
        out_ref[i, :, 128:] = second


def call(kernel, inputs, outs, scratch=(), flops=0, nbytes=0):
    return pl.pallas_call(
        kernel,
        out_shape=outs,
        in_specs=[SMEM] + [VMEM] * (len(inputs) - 1),
        out_specs=jax.tree.map(lambda _: VMEM, outs),
        scratch_shapes=list(scratch),
        compiler_params=pltpu.CompilerParams(vmem_limit_bytes=48 * 2**20),
        cost_estimate=pl.CostEstimate(flops=flops, bytes_accessed=nbytes, transcendentals=0),
    )(*inputs)


def gather(packed, along_row, near):
    short, rest = packed[:SHORT], packed[SHORT:]
    flip_short = move(short, along_row, 1, 0)
    flip_rest = move(rest, along_row, 1, 0, near_only=True)
    shorts = [packed] + [move(short, along_row, 0, s) for s in (1, 2, 3)]
    both = jnp.concatenate([flip_short, jnp.where(near, rest, flip_rest)], axis=0)
    boths = [both] + [move(both, along_row, 0, s) for s in (1, 2, 3)]
    return [part for pair in zip(shorts, boths) for part in pair]


def per_device(matrix, pattern_cols, pattern_counts):
    row, panel = lax.axis_index("row"), lax.axis_index("col")
    near = is_near(row, panel // 2)
    weights = jnp.array([1, 4, 16, 64], jnp.int32)
    code = jnp.sum(pattern_cols * weights, axis=2) + pattern_counts * 256
    packed_shape = jax.ShapeDtypeStruct((ROWS, BS, 256), F32)
    packed = call(pack_kernel, [code, matrix], packed_shape)

    left = gather(packed, True, near)
    left = left + [other_core(part) for part in left]
    right = gather(packed, False, near)
    dense_shape = jax.ShapeDtypeStruct((2 * SIDES, ROWS * BS, 256), BF16)
    left_hi, left_lo = call(left_kernel, [code] + left, [dense_shape, dense_shape])

    right_scratch = [pltpu.VMEM((SIDES, ROWS * BS, 256), BF16)] * 2 + [pltpu.VMEM((ROWS * BS, 256), F32)]
    shifted = call(
        square_kernel,
        [code, left_hi, left_lo] + right,
        packed_shape,
        right_scratch + [pltpu.VMEM((ROWS, BS, 256), F32)],
    )
    right = gather(shifted, False, near)
    return call(result_kernel, [code, left_hi, left_lo] + right, packed_shape, right_scratch)


def solution(mesh):
    return jax.shard_map(
        per_device,
        mesh=mesh,
        in_specs=(P("row", None, "col"), P(), P()),
        out_specs=P("row", None, "col"),
        check_vma=False,
    )
```

time: 667 us -> 180 us (0.27)
  the two profiles are of different devices: /device:TPU:8 before, /device:TPU:16 now
where the time goes in v1:
time: 180 us
  waiting for transfers between devices  98.1 us (54%)
  starting transfers between devices  40.6 us (23%)
  Pallas kernels  37.9 us (21%)
  local copies, waits for them, and re-layouts  1.98 us (1%)
    ppermute x24, waiting for transfers between devices, move(): lax.ppermute(value, ('row', 'col'), chip_moves(along_row, flip, shift, ne...  97.1 us
    ppermute x24, starting transfers between devices, move(): lax.ppermute(value, ('row', 'col'), chip_moves(along_row, flip, shift, ne...  39.4 us
    pallas_call x4, Pallas kernels, call(): pl.pallas_call(kernel, out_shape=outs, in_specs=[SMEM] + [VMEM] * (len(in...  37.9 us
  transfers between devices with their start and end apart: 32, of which 15 were waited for; matrix products, arithmetic and copies ran while one was open for 0% of the time, Pallas kernels for 6%

profile of v1, /device:TPU:16, one launch (start us, length us, event | category | flops | bytes accessed | tf_op | source)
XLA Modules:
  0.0 179.8 jit_solution(3227957823590450576)
XLA Ops:
  4.0 1.3 collective-permute-start.1
  6.6 3.2 %collective-permute-start = (f32[3,64,256]{2,1,0:T(8,128)S(1)}, f32[3,64,256]{2,1,0:T(8,128)S(1)}, u32[]{:S(2)}, u32[]{:S(2)}) collective-permute-start(f32[3,64,256]{2,1,0:T(8,128)S(1)} %slice.18), channel_id=1, source_target_pairs={{0,8},{1,9},{2,10},{3,11},{4,12},{5,13},{6,14},{7,15},{8,0},{9,1},... | collective-permute-start | bytes 589832 | tf_op jit(solution)/shard_map/ppermute | solution.py:41
  9.9 1.5 collective-permute-start.2
  11.3 1.6 collective-permute-start.4
  12.9 3.6 %collective-permute-done.1 = f32[5,64,256]{2,1,0:T(8,128)S(1)} collective-permute-done((f32[5,64,256]{2,1,0:T(8,128)S(1)}, f32[5,64,256]{2,1,0:T(8,128)S(1)}, u32[]{:S(2)}, u32[]{:S(2)}) %collective-permute-start.1) | collective-permute-done | bytes 327712 | tf_op jit(solution)/shard_map/ppermute | solution.py:41
  16.5 6.9 %collective-permute-done.17 = f32[5,64,256]{2,1,0:T(8,128)S(1)} collective-permute-done((f32[5,64,256]{2,1,0:T(8,128)S(1)}, f32[5,64,256]{2,1,0:T(8,128)S(1)}, u32[]{:S(2)}, u32[]{:S(2)}) %collective-permute-start.17) | collective-permute-done | bytes 327712 | tf_op jit(solution)/shard_map/ppermute | solution.py:41
  23.5 3.1 %collective-permute-done = f32[3,64,256]{2,1,0:T(8,128)S(1)} collective-permute-done((f32[3,64,256]{2,1,0:T(8,128)S(1)}, f32[3,64,256]{2,1,0:T(8,128)S(1)}, u32[]{:S(2)}, u32[]{:S(2)}) %collective-permute-start) | collective-permute-done | bytes 196640 | tf_op jit(solution)/shard_map/ppermute | solution.py:41
  26.6 1.6 collective-permute-start.3
  28.2 1.7 collective-permute-start.6
  29.9 1.9 %collective-permute-start.18 = (f32[3,64,256]{2,1,0:T(8,128)S(1)}, f32[3,64,256]{2,1,0:T(8,128)S(1)}, u32[]{:S(2)}, u32[]{:S(2)}) collective-permute-start(f32[3,64,256]{2,1,0:T(8,128)S(1)} %slice.18), channel_id=1, source_target_pairs={{0,16},{1,17},{2,18},{3,19},{4,20},{5,21},{6,22},{7,23},{8,24},{9,... | collective-permute-start | bytes 589832 | tf_op jit(solution)/shard_map/ppermute | solution.py:41
  31.9 2.0 %collective-permute-done.6.refs_6_ = f32[3,64,256]{2,1,0:T(8,128)S(1)} collective-permute-done((f32[3,64,256]{2,1,0:T(8,128)S(1)}, f32[3,64,256]{2,1,0:T(8,128)S(1)}, u32[]{:S(2)}, u32[]{:S(2)}) %collective-permute-start.6) | collective-permute-done | bytes 196640 | tf_op jit(solution)/shard_map/ppermute | solution.py:41
  33.9 3.2 %collective-permute-done.16 = f32[3,64,256]{2,1,0:T(8,128)S(1)} collective-permute-done((f32[3,64,256]{2,1,0:T(8,128)S(1)}, f32[3,64,256]{2,1,0:T(8,128)S(1)}, u32[]{:S(2)}, u32[]{:S(2)}) %collective-permute-start.16) | collective-permute-done | bytes 196640 | tf_op jit(solution)/shard_map/ppermute | solution.py:41
  38.0 2.1 %collective-permute-start.7 = (f32[8,64,256]{2,1,0:T(8,128)S(1)}, f32[8,64,256]{2,1,0:T(8,128)S(1)}, u32[]{:S(2)}, u32[]{:S(2)}) collective-permute-start(f32[8,64,256]{2,1,0:T(8,128)S(1)} %pad_maximum_fusion.refs_1_), channel_id=1, source_target_pairs={{0,6},{1,7},{2,0},{3,1},{4,2},{5,3},{6,4},{7,5},{8,14},{9,15},{10,... | collective-permute-start | bytes 1572872 | tf_op jit(solution)/shard_map/ppermute | solution.py:41
  41.6 10.3 %collective-permute-done.3.refs_3_ = f32[8,64,256]{2,1,0:T(8,128)S(1)} collective-permute-done((f32[8,64,256]{2,1,0:T(8,128)S(1)}, f32[8,64,256]{2,1,0:T(8,128)S(1)}, u32[]{:S(2)}, u32[]{:S(2)}) %collective-permute-start.3) | collective-permute-done | bytes 524320 | tf_op jit(solution)/shard_map/ppermute | solution.py:41
  52.4 8.8 %collective-permute-done.7.refs_7_ = f32[8,64,256]{2,1,0:T(8,128)S(1)} collective-permute-done((f32[8,64,256]{2,1,0:T(8,128)S(1)}, f32[8,64,256]{2,1,0:T(8,128)S(1)}, u32[]{:S(2)}, u32[]{:S(2)}) %collective-permute-start.7) | collective-permute-done | bytes 524320 | tf_op jit(solution)/shard_map/ppermute | solution.py:41
  61.3 2.0 %collective-permute-start.19 = (f32[8,64,256]{2,1,0:T(8,128)S(1)}, f32[8,64,256]{2,1,0:T(8,128)S(1)}, u32[]{:S(2)}, u32[]{:S(2)}) collective-permute-start(f32[8,64,256]{2,1,0:T(8,128)S(1)} %pad_maximum_fusion.1.refs_1_), channel_id=1, source_target_pairs={{0,16},{1,17},{2,18},{3,19},{4,20},{5,21},{6,22},{7,23},{8,24},{9,... | collective-permute-start | bytes 1572872 | tf_op jit(solution)/shard_map/ppermute | solution.py:41
  63.3 3.3 %collective-permute-start.21 = (f32[8,64,256]{2,1,0:T(8,128)S(1)}, f32[8,64,256]{2,1,0:T(8,128)S(1)}, u32[]{:S(2)}, u32[]{:S(2)}) collective-permute-start(f32[8,64,256]{2,1,0:T(8,128)S(1)} %pad_maximum_fusion.1.refs_1_), channel_id=1, source_target_pairs={{0,32},{1,33},{2,34},{3,35},{4,36},{5,37},{6,38},{7,39},{8,40},{9,... | collective-permute-start | bytes 1572872 | tf_op jit(solution)/shard_map/ppermute | solution.py:41
  68.2 3.1 %collective-permute-start.22 = (f32[3,64,256]{2,1,0:T(8,128)S(1)}, f32[3,64,256]{2,1,0:T(8,128)S(1)}, u32[]{:S(2)}, u32[]{:S(2)}) collective-permute-start(f32[3,64,256]{2,1,0:T(8,128)S(1)} %slice.18), channel_id=1, source_target_pairs={{0,48},{1,49},{2,50},{3,51},{4,52},{5,53},{6,54},{7,55},{8,56},{9,... | collective-permute-start | bytes 589832 | tf_op jit(solution)/shard_map/ppermute | solution.py:41
  71.3 11.4 %shard_map.47 = (bf16[16,512,256]{2,1,0:T(8,128)(2,1)}, bf16[16,512,256]{2,1,0:T(8,128)(2,1)}) custom-call(s32[64,16]{1,0:T(8,128)S(1)} %multiply_add_fusion.code_ref, f32[8,64,256]{2,1,0:T(8,128)S(1)} %shard_map.46.refs_0_, f32[8,64,256]{2,1,0:T(8,128)S(1)} %pad_maximum_fusion.refs_1_, f32[3,64,256]{2,1,0:T(8,128)S(1)} %collective-permute-done.2.refs_2_, ...), custom_call_target="tpu_custom_call" | custom-call | tf_op jit(solution)/shard_map/pallas_call | solution.py:261
  82.7 11.7 %collective-permute-done.20.refs_4_ = f32[3,64,256]{2,1,0:T(8,128)S(1)} collective-permute-done((f32[3,64,256]{2,1,0:T(8,128)S(1)}, f32[3,64,256]{2,1,0:T(8,128)S(1)}, u32[]{:S(2)}, u32[]{:S(2)}) %collective-permute-start.20) | collective-permute-done | bytes 196640 | tf_op jit(solution)/shard_map/ppermute | solution.py:41
  94.3 3.8 %collective-permute-done.22.refs_6_ = f32[3,64,256]{2,1,0:T(8,128)S(1)} collective-permute-done((f32[3,64,256]{2,1,0:T(8,128)S(1)}, f32[3,64,256]{2,1,0:T(8,128)S(1)}, u32[]{:S(2)}, u32[]{:S(2)}) %collective-permute-start.22) | collective-permute-done | bytes 196640 | tf_op jit(solution)/shard_map/ppermute | solution.py:41
  98.2 12.4 %shard_map.48.refs_0_ = f32[8,64,256]{2,1,0:T(8,128)S(1)} custom-call(s32[64,16]{1,0:T(8,128)S(1)} %multiply_add_fusion.code_ref, bf16[16,512,256]{2,1,0:T(8,128)(2,1)} %get-tuple-element.7.left_hi, bf16[16,512,256]{2,1,0:T(8,128)(2,1)} %get-tuple-element.8.left_lo, f32[8,64,256]{2,1,0:T(8,128)S(1)} %shard_map.46.refs_0_, ...), custom_call_target="tpu_custom_call" | custom-call | tf_op jit(solution)/shard_map/pallas_call | solution.py:261
  110.5 1.3 collective-permute-start.25
  111.9 4.2 %collective-permute-start.24 = (f32[3,64,256]{2,1,0:T(8,128)S(1)}, f32[3,64,256]{2,1,0:T(8,128)S(1)}, u32[]{:S(2)}, u32[]{:S(2)}) collective-permute-start(f32[3,64,256]{2,1,0:T(8,128)S(1)} %slice.20), channel_id=1, source_target_pairs={{0,64},{1,65},{2,66},{3,67},{4,68},{5,69},{6,70},{7,71},{8,72},{9,... | collective-permute-start | bytes 589832 | tf_op jit(solution)/shard_map/ppermute | solution.py:41
  116.1 8.4 %collective-permute-done.25 = f32[5,64,256]{2,1,0:T(8,128)S(1)} collective-permute-done((f32[5,64,256]{2,1,0:T(8,128)S(1)}, f32[5,64,256]{2,1,0:T(8,128)S(1)}, u32[]{:S(2)}, u32[]{:S(2)}) %collective-permute-start.25) | collective-permute-done | bytes 327712 | tf_op jit(solution)/shard_map/ppermute | solution.py:41
  124.6 2.9 %collective-permute-done.24 = f32[3,64,256]{2,1,0:T(8,128)S(1)} collective-permute-done((f32[3,64,256]{2,1,0:T(8,128)S(1)}, f32[3,64,256]{2,1,0:T(8,128)S(1)}, u32[]{:S(2)}, u32[]{:S(2)}) %collective-permute-start.24) | collective-permute-done | bytes 196640 | tf_op jit(solution)/shard_map/ppermute | solution.py:41
  127.5 1.7 collective-permute-start.27
  129.3 2.8 %collective-permute-start.31 = (f32[8,64,256]{2,1,0:T(8,128)S(1)}, f32[8,64,256]{2,1,0:T(8,128)S(1)}, u32[]{:S(2)}, u32[]{:S(2)}) collective-permute-start(f32[8,64,256]{2,1,0:T(8,128)S(1)} %pad_maximum_fusion.2.refs_1_), channel_id=1, source_target_pairs={{0,48},{1,49},{2,50},{3,51},{4,52},{5,53},{6,54},{7,55},{8,56},{9,... | collective-permute-start | bytes 1572872 | tf_op jit(solution)/shard_map/ppermute | solution.py:41
  132.0 2.8 %collective-permute-start.28 = (f32[3,64,256]{2,1,0:T(8,128)S(1)}, f32[3,64,256]{2,1,0:T(8,128)S(1)}, u32[]{:S(2)}, u32[]{:S(2)}) collective-permute-start(f32[3,64,256]{2,1,0:T(8,128)S(1)} %slice.20), channel_id=1, source_target_pairs={{0,32},{1,33},{2,34},{3,35},{4,36},{5,37},{6,38},{7,39},{8,40},{9,... | collective-permute-start | bytes 589832 | tf_op jit(solution)/shard_map/ppermute | solution.py:41
  134.8 26.3 %collective-permute-done.26.refs_2_ = f32[3,64,256]{2,1,0:T(8,128)S(1)} collective-permute-done((f32[3,64,256]{2,1,0:T(8,128)S(1)}, f32[3,64,256]{2,1,0:T(8,128)S(1)}, u32[]{:S(2)}, u32[]{:S(2)}) %collective-permute-start.26) | collective-permute-done | bytes 196640 | tf_op jit(solution)/shard_map/ppermute | solution.py:41
  161.2 5.7 %collective-permute-done.30.refs_6_ = f32[3,64,256]{2,1,0:T(8,128)S(1)} collective-permute-done((f32[3,64,256]{2,1,0:T(8,128)S(1)}, f32[3,64,256]{2,1,0:T(8,128)S(1)}, u32[]{:S(2)}, u32[]{:S(2)}) %collective-permute-start.30) | collective-permute-done | bytes 196640 | tf_op jit(solution)/shard_map/ppermute | solution.py:41
  166.8 13.0 %shard_map.49 = f32[8,64,256]{2,1,0:T(8,128)} custom-call(s32[64,16]{1,0:T(8,128)S(1)} %multiply_add_fusion.code_ref, bf16[16,512,256]{2,1,0:T(8,128)(2,1)} %get-tuple-element.7.left_hi, bf16[16,512,256]{2,1,0:T(8,128)(2,1)} %get-tuple-element.8.left_lo, f32[8,64,256]{2,1,0:T(8,128)S(1)} %shard_map.48.refs_0_, f32[8,64,256]{2,1,0:T(8,128)S(1)} %pad_maximum_fusion.2.refs_1_, ...), custom_call_target="tpu_custom_call" | custom-call | tf_op jit(solution)/shard_map/pallas_call | solution.py:261
  (53 shorter events, 10.1 us)
Async XLA Ops:
  4.0 12.5 %collective-permute-start.1 = (f32[5,64,256]{2,1,0:T(8,128)S(1)}, f32[5,64,256]{2,1,0:T(8,128)S(1)}, u32[]{:S(2)}, u32[]{:S(2)}) collective-permute-start(f32[5,64,256]{2,1,0:T(8,128)S(1)} %slice.19), channel_id=1, source_target_pairs={{0,8},{1,9},{2,10},{3,11},{14,6},{15,7},{16,24},{17,25},{18,26},{1... | collective-permute-start | bytes 983048 | tf_op jit(solution)/shard_map/ppermute | solution.py:41
  5.3 18.1 %collective-permute-start.17 = (f32[5,64,256]{2,1,0:T(8,128)S(1)}, f32[5,64,256]{2,1,0:T(8,128)S(1)}, u32[]{:S(2)}, u32[]{:S(2)}) collective-permute-start(f32[5,64,256]{2,1,0:T(8,128)S(1)} %slice.19), channel_id=1, source_target_pairs={{0,64},{1,65},{2,66},{3,67},{14,78},{15,79},{16,80},{17,81},{18,82... | collective-permute-start | bytes 983048 | tf_op jit(solution)/shard_map/ppermute | solution.py:41
  6.6 20.0 %collective-permute-start = (f32[3,64,256]{2,1,0:T(8,128)S(1)}, f32[3,64,256]{2,1,0:T(8,128)S(1)}, u32[]{:S(2)}, u32[]{:S(2)}) collective-permute-start(f32[3,64,256]{2,1,0:T(8,128)S(1)} %slice.18), channel_id=1, source_target_pairs={{0,8},{1,9},{2,10},{3,11},{4,12},{5,13},{6,14},{7,15},{8,0},{9,1},... | collective-permute-start | bytes 589832 | tf_op jit(solution)/shard_map/ppermute | solution.py:41
  9.9 20.1 %collective-permute-start.2 = (f32[3,64,256]{2,1,0:T(8,128)S(1)}, f32[3,64,256]{2,1,0:T(8,128)S(1)}, u32[]{:S(2)}, u32[]{:S(2)}) collective-permute-start(f32[3,64,256]{2,1,0:T(8,128)S(1)} %slice.18), channel_id=1, source_target_pairs={{0,2},{1,3},{2,4},{3,5},{4,6},{5,7},{6,0},{7,1},{8,10},{9,11},{10,... | collective-permute-start | bytes 589832 | tf_op jit(solution)/shard_map/ppermute | solution.py:41
  11.3 20.5 %collective-permute-start.4 = (f32[3,64,256]{2,1,0:T(8,128)S(1)}, f32[3,64,256]{2,1,0:T(8,128)S(1)}, u32[]{:S(2)}, u32[]{:S(2)}) collective-permute-start(f32[3,64,256]{2,1,0:T(8,128)S(1)} %slice.18), channel_id=1, source_target_pairs={{0,4},{1,5},{2,6},{3,7},{4,0},{5,1},{6,2},{7,3},{8,12},{9,13},{10,... | collective-permute-start | bytes 589832 | tf_op jit(solution)/shard_map/ppermute | solution.py:41
  26.6 25.3 %collective-permute-start.3 = (f32[8,64,256]{2,1,0:T(8,128)S(1)}, f32[8,64,256]{2,1,0:T(8,128)S(1)}, u32[]{:S(2)}, u32[]{:S(2)}) collective-permute-start(f32[8,64,256]{2,1,0:T(8,128)S(1)} %pad_maximum_fusion.refs_1_), channel_id=1, source_target_pairs={{0,2},{1,3},{2,4},{3,5},{4,6},{5,7},{6,0},{7,1},{8,10},{9,11},{10,... | collective-permute-start | bytes 1572872 | tf_op jit(solution)/shard_map/ppermute | solution.py:41
  28.2 5.7 %collective-permute-start.6 = (f32[3,64,256]{2,1,0:T(8,128)S(1)}, f32[3,64,256]{2,1,0:T(8,128)S(1)}, u32[]{:S(2)}, u32[]{:S(2)}) collective-permute-start(f32[3,64,256]{2,1,0:T(8,128)S(1)} %slice.18), channel_id=1, source_target_pairs={{0,6},{1,7},{2,0},{3,1},{4,2},{5,3},{6,4},{7,5},{8,14},{9,15},{10,... | collective-permute-start | bytes 589832 | tf_op jit(solution)/shard_map/ppermute | solution.py:41
  29.9 7.2 %collective-permute-start.16 = (f32[3,64,256]{2,1,0:T(8,128)S(1)}, f32[3,64,256]{2,1,0:T(8,128)S(1)}, u32[]{:S(2)}, u32[]{:S(2)}) collective-permute-start(f32[3,64,256]{2,1,0:T(8,128)S(1)} %slice.18), channel_id=1, source_target_pairs={{0,64},{1,65},{2,66},{3,67},{4,68},{5,69},{6,70},{7,71},{8,72},{9,... | collective-permute-start | bytes 589832 | tf_op jit(solution)/shard_map/ppermute | solution.py:41
  29.9 8.0 %collective-permute-start.18 = (f32[3,64,256]{2,1,0:T(8,128)S(1)}, f32[3,64,256]{2,1,0:T(8,128)S(1)}, u32[]{:S(2)}, u32[]{:S(2)}) collective-permute-start(f32[3,64,256]{2,1,0:T(8,128)S(1)} %slice.18), channel_id=1, source_target_pairs={{0,16},{1,17},{2,18},{3,19},{4,20},{5,21},{6,22},{7,23},{8,24},{9,... | collective-permute-start | bytes 589832 | tf_op jit(solution)/shard_map/ppermute | solution.py:41
  31.9 8.2 %collective-permute-start.10 = (f32[3,64,256]{2,1,0:T(8,128)S(1)}, f32[3,64,256]{2,1,0:T(8,128)S(1)}, u32[]{:S(2)}, u32[]{:S(2)}) collective-permute-start(f32[3,64,256]{2,1,0:T(8,128)S(1)} %collective-permute-done.2.refs_2_), channel_id=1, source_target_pairs={{0,1},{1,0},{2,3},{3,2},{4,5},{5,4},{6,7},{7,6},{8,9},{9,8},{10,11... | collective-permute-start | bytes 589832 | tf_op jit(solution)/shard_map/ppermute | solution.py:45
  33.9 6.2 %collective-permute-start.12 = (f32[3,64,256]{2,1,0:T(8,128)S(1)}, f32[3,64,256]{2,1,0:T(8,128)S(1)}, u32[]{:S(2)}, u32[]{:S(2)}) collective-permute-start(f32[3,64,256]{2,1,0:T(8,128)S(1)} %collective-permute-done.4.refs_4_), channel_id=1, source_target_pairs={{0,1},{1,0},{2,3},{3,2},{4,5},{5,4},{6,7},{7,6},{8,9},{9,8},{10,11... | collective-permute-start | bytes 589832 | tf_op jit(solution)/shard_map/ppermute | solution.py:45
  37.1 14.8 %collective-permute-start.5 = (f32[8,64,256]{2,1,0:T(8,128)S(1)}, f32[8,64,256]{2,1,0:T(8,128)S(1)}, u32[]{:S(2)}, u32[]{:S(2)}) collective-permute-start(f32[8,64,256]{2,1,0:T(8,128)S(1)} %pad_maximum_fusion.refs_1_), channel_id=1, source_target_pairs={{0,4},{1,5},{2,6},{3,7},{4,0},{5,1},{6,2},{7,3},{8,12},{9,13},{10,... | collective-permute-start | bytes 1572872 | tf_op jit(solution)/shard_map/ppermute | solution.py:41
  38.0 23.3 %collective-permute-start.7 = (f32[8,64,256]{2,1,0:T(8,128)S(1)}, f32[8,64,256]{2,1,0:T(8,128)S(1)}, u32[]{:S(2)}, u32[]{:S(2)}) collective-permute-start(f32[8,64,256]{2,1,0:T(8,128)S(1)} %pad_maximum_fusion.refs_1_), channel_id=1, source_target_pairs={{0,6},{1,7},{2,0},{3,1},{4,2},{5,3},{6,4},{7,5},{8,14},{9,15},{10,... | collective-permute-start | bytes 1572872 | tf_op jit(solution)/shard_map/ppermute | solution.py:41
  40.1 1.4 collective-permute-start.14
  40.1 21.2 %collective-permute-start.8 = (f32[8,64,256]{2,1,0:T(8,128)S(1)}, f32[8,64,256]{2,1,0:T(8,128)S(1)}, u32[]{:S(2)}, u32[]{:S(2)}) collective-permute-start(f32[8,64,256]{2,1,0:T(8,128)S(1)} %shard_map.46.refs_0_), channel_id=1, source_target_pairs={{0,1},{1,0},{2,3},{3,2},{4,5},{5,4},{6,7},{7,6},{8,9},{9,8},{10,11... | collective-permute-start | bytes 1572872 | tf_op jit(solution)/shard_map/ppermute | solution.py:45
  41.5 21.8 %collective-permute-start.9 = (f32[8,64,256]{2,1,0:T(8,128)S(1)}, f32[8,64,256]{2,1,0:T(8,128)S(1)}, u32[]{:S(2)}, u32[]{:S(2)}) collective-permute-start(f32[8,64,256]{2,1,0:T(8,128)S(1)} %pad_maximum_fusion.refs_1_), channel_id=1, source_target_pairs={{0,1},{1,0},{2,3},{3,2},{4,5},{5,4},{6,7},{7,6},{8,9},{9,8},{10,11... | collective-permute-start | bytes 1572872 | tf_op jit(solution)/shard_map/ppermute | solution.py:45
  51.9 14.7 %collective-permute-start.11 = (f32[8,64,256]{2,1,0:T(8,128)S(1)}, f32[8,64,256]{2,1,0:T(8,128)S(1)}, u32[]{:S(2)}, u32[]{:S(2)}) collective-permute-start(f32[8,64,256]{2,1,0:T(8,128)S(1)} %collective-permute-done.3.refs_3_), channel_id=1, source_target_pairs={{0,1},{1,0},{2,3},{3,2},{4,5},{5,4},{6,7},{7,6},{8,9},{9,8},{10,11... | collective-permute-start | bytes 1572872 | tf_op jit(solution)/shard_map/ppermute | solution.py:45
  51.9 15.7 %collective-permute-start.13 = (f32[8,64,256]{2,1,0:T(8,128)S(1)}, f32[8,64,256]{2,1,0:T(8,128)S(1)}, u32[]{:S(2)}, u32[]{:S(2)}) collective-permute-start(f32[8,64,256]{2,1,0:T(8,128)S(1)} %collective-permute-done.5.refs_5_), channel_id=1, source_target_pairs={{0,1},{1,0},{2,3},{3,2},{4,5},{5,4},{6,7},{7,6},{8,9},{9,8},{10,11... | collective-permute-start | bytes 1572872 | tf_op jit(solution)/shard_map/ppermute | solution.py:45
  61.3 6.9 %collective-permute-start.15 = (f32[8,64,256]{2,1,0:T(8,128)S(1)}, f32[8,64,256]{2,1,0:T(8,128)S(1)}, u32[]{:S(2)}, u32[]{:S(2)}) collective-permute-start(f32[8,64,256]{2,1,0:T(8,128)S(1)} %collective-permute-done.7.refs_7_), channel_id=1, source_target_pairs={{0,1},{1,0},{2,3},{3,2},{4,5},{5,4},{6,7},{7,6},{8,9},{9,8},{10,11... | collective-permute-start | bytes 1572872 | tf_op jit(solution)/shard_map/ppermute | solution.py:45
  61.3 36.8 %collective-permute-start.19 = (f32[8,64,256]{2,1,0:T(8,128)S(1)}, f32[8,64,256]{2,1,0:T(8,128)S(1)}, u32[]{:S(2)}, u32[]{:S(2)}) collective-permute-start(f32[8,64,256]{2,1,0:T(8,128)S(1)} %pad_maximum_fusion.1.refs_1_), channel_id=1, source_target_pairs={{0,16},{1,17},{2,18},{3,19},{4,20},{5,21},{6,22},{7,23},{8,24},{9,... | collective-permute-start | bytes 1572872 | tf_op jit(solution)/shard_map/ppermute | solution.py:41
  63.3 34.8 %collective-permute-start.21 = (f32[8,64,256]{2,1,0:T(8,128)S(1)}, f32[8,64,256]{2,1,0:T(8,128)S(1)}, u32[]{:S(2)}, u32[]{:S(2)}) collective-permute-start(f32[8,64,256]{2,1,0:T(8,128)S(1)} %pad_maximum_fusion.1.refs_1_), channel_id=1, source_target_pairs={{0,32},{1,33},{2,34},{3,35},{4,36},{5,37},{6,38},{7,39},{8,40},{9,... | collective-permute-start | bytes 1572872 | tf_op jit(solution)/shard_map/ppermute | solution.py:41
  66.6 31.6 %collective-permute-start.23 = (f32[8,64,256]{2,1,0:T(8,128)S(1)}, f32[8,64,256]{2,1,0:T(8,128)S(1)}, u32[]{:S(2)}, u32[]{:S(2)}) collective-permute-start(f32[8,64,256]{2,1,0:T(8,128)S(1)} %pad_maximum_fusion.1.refs_1_), channel_id=1, source_target_pairs={{0,48},{1,49},{2,50},{3,51},{4,52},{5,53},{6,54},{7,55},{8,56},{9,... | collective-permute-start | bytes 1572872 | tf_op jit(solution)/shard_map/ppermute | solution.py:41
  67.6 26.7 %collective-permute-start.20 = (f32[3,64,256]{2,1,0:T(8,128)S(1)}, f32[3,64,256]{2,1,0:T(8,128)S(1)}, u32[]{:S(2)}, u32[]{:S(2)}) collective-permute-start(f32[3,64,256]{2,1,0:T(8,128)S(1)} %slice.18), channel_id=1, source_target_pairs={{0,32},{1,33},{2,34},{3,35},{4,36},{5,37},{6,38},{7,39},{8,40},{9,... | collective-permute-start | bytes 589832 | tf_op jit(solution)/shard_map/ppermute | solution.py:41
  68.2 30.0 %collective-permute-start.22 = (f32[3,64,256]{2,1,0:T(8,128)S(1)}, f32[3,64,256]{2,1,0:T(8,128)S(1)}, u32[]{:S(2)}, u32[]{:S(2)}) collective-permute-start(f32[3,64,256]{2,1,0:T(8,128)S(1)} %slice.18), channel_id=1, source_target_pairs={{0,48},{1,49},{2,50},{3,51},{4,52},{5,53},{6,54},{7,55},{8,56},{9,... | collective-permute-start | bytes 589832 | tf_op jit(solution)/shard_map/ppermute | solution.py:41
  110.5 14.0 %collective-permute-start.25 = (f32[5,64,256]{2,1,0:T(8,128)S(1)}, f32[5,64,256]{2,1,0:T(8,128)S(1)}, u32[]{:S(2)}, u32[]{:S(2)}) collective-permute-start(f32[5,64,256]{2,1,0:T(8,128)S(1)} %slice.21), channel_id=1, source_target_pairs={{0,64},{1,65},{2,66},{3,67},{14,78},{15,79},{16,80},{17,81},{18,82... | collective-permute-start | bytes 983048 | tf_op jit(solution)/shard_map/ppermute | solution.py:41
  111.9 15.6 %collective-permute-start.24 = (f32[3,64,256]{2,1,0:T(8,128)S(1)}, f32[3,64,256]{2,1,0:T(8,128)S(1)}, u32[]{:S(2)}, u32[]{:S(2)}) collective-permute-start(f32[3,64,256]{2,1,0:T(8,128)S(1)} %slice.20), channel_id=1, source_target_pairs={{0,64},{1,65},{2,66},{3,67},{4,68},{5,69},{6,70},{7,71},{8,72},{9,... | collective-permute-start | bytes 589832 | tf_op jit(solution)/shard_map/ppermute | solution.py:41
  127.5 39.3 %collective-permute-start.27 = (f32[8,64,256]{2,1,0:T(8,128)S(1)}, f32[8,64,256]{2,1,0:T(8,128)S(1)}, u32[]{:S(2)}, u32[]{:S(2)}) collective-permute-start(f32[8,64,256]{2,1,0:T(8,128)S(1)} %pad_maximum_fusion.2.refs_1_), channel_id=1, source_target_pairs={{0,16},{1,17},{2,18},{3,19},{4,20},{5,21},{6,22},{7,23},{8,24},{9,... | collective-permute-start | bytes 1572872 | tf_op jit(solution)/shard_map/ppermute | solution.py:41
  129.3 37.6 %collective-permute-start.29 = (f32[8,64,256]{2,1,0:T(8,128)S(1)}, f32[8,64,256]{2,1,0:T(8,128)S(1)}, u32[]{:S(2)}, u32[]{:S(2)}) collective-permute-start(f32[8,64,256]{2,1,0:T(8,128)S(1)} %pad_maximum_fusion.2.refs_1_), channel_id=1, source_target_pairs={{0,32},{1,33},{2,34},{3,35},{4,36},{5,37},{6,38},{7,39},{8,40},{9,... | collective-permute-start | bytes 1572872 | tf_op jit(solution)/shard_map/ppermute | solution.py:41
  129.3 37.6 %collective-permute-start.31 = (f32[8,64,256]{2,1,0:T(8,128)S(1)}, f32[8,64,256]{2,1,0:T(8,128)S(1)}, u32[]{:S(2)}, u32[]{:S(2)}) collective-permute-start(f32[8,64,256]{2,1,0:T(8,128)S(1)} %pad_maximum_fusion.2.refs_1_), channel_id=1, source_target_pairs={{0,48},{1,49},{2,50},{3,51},{4,52},{5,53},{6,54},{7,55},{8,56},{9,... | collective-permute-start | bytes 1572872 | tf_op jit(solution)/shard_map/ppermute | solution.py:41
  132.0 29.1 %collective-permute-start.26 = (f32[3,64,256]{2,1,0:T(8,128)S(1)}, f32[3,64,256]{2,1,0:T(8,128)S(1)}, u32[]{:S(2)}, u32[]{:S(2)}) collective-permute-start(f32[3,64,256]{2,1,0:T(8,128)S(1)} %slice.20), channel_id=1, source_target_pairs={{0,16},{1,17},{2,18},{3,19},{4,20},{5,21},{6,22},{7,23},{8,24},{9,... | collective-permute-start | bytes 589832 | tf_op jit(solution)/shard_map/ppermute | solution.py:41
  132.0 29.1 %collective-permute-start.28 = (f32[3,64,256]{2,1,0:T(8,128)S(1)}, f32[3,64,256]{2,1,0:T(8,128)S(1)}, u32[]{:S(2)}, u32[]{:S(2)}) collective-permute-start(f32[3,64,256]{2,1,0:T(8,128)S(1)} %slice.20), channel_id=1, source_target_pairs={{0,32},{1,33},{2,34},{3,35},{4,36},{5,37},{6,38},{7,39},{8,40},{9,... | collective-permute-start | bytes 589832 | tf_op jit(solution)/shard_map/ppermute | solution.py:41
  161.1 5.7 %collective-permute-start.30 = (f32[3,64,256]{2,1,0:T(8,128)S(1)}, f32[3,64,256]{2,1,0:T(8,128)S(1)}, u32[]{:S(2)}, u32[]{:S(2)}) collective-permute-start(f32[3,64,256]{2,1,0:T(8,128)S(1)} %slice.20), channel_id=1, source_target_pairs={{0,48},{1,49},{2,50},{3,51},{4,52},{5,53},{6,54},{7,55},{8,56},{9,... | collective-permute-start | bytes 589832 | tf_op jit(solution)/shard_map/ppermute | solution.py:41
  (2 other events, 4.2 us)

commit v2 on v0

v2 whole, which is shorter than its diff:
```python
import jax
import jax.numpy as jnp
from jax import lax
from jax.experimental import pallas as pl
from jax.experimental.pallas import tpu as pltpu
from jax.sharding import PartitionSpec as P

ROWS = 8
HALF = ROWS // 2
BS = 64
RING = 4
SIDES = 8
VMEM = pl.BlockSpec(memory_space=pltpu.VMEM)
SMEM = pl.BlockSpec(memory_space=pltpu.SMEM)
BF16 = jnp.bfloat16
F32 = jnp.float32


def move(value, along_row, flip, shift):
    pairs = []
    for row in range(SIDES):
        for chip in range(SIDES):
            half, at = divmod(chip if along_row else row, RING)
            place = (half ^ flip) * RING + (at + shift) % RING
            target = (row, place) if along_row else (place, chip)
            for core in range(2):
                pairs.append(((row * SIDES + chip) * 2 + core, (target[0] * SIDES + target[1]) * 2 + core))
    return lax.ppermute(value, ("row", "col"), pairs)


def other_core(value):
    return lax.ppermute(value, "col", [(c, c ^ 1) for c in range(2 * SIDES)])


def gather_two_stages(value, along_row):
    one, three, two, across = [move(value, along_row, f, s) for f, s in ((0, 1), (0, 3), (0, 2), (1, 0))]
    near = [(value, 0, 0), (one, 0, 1), (three, 0, 3), (two, 0, 2)]
    far = [
        (across, 1, 0),
        (move(across, along_row, 0, 1), 1, 1),
        (move(across, along_row, 0, 3), 1, 3),
        (move(two, along_row, 1, 0), 1, 2),
    ]
    return [[([(a, 0, ROWS, 0)], f, s) for a, f, s in part] for part in (near, far)]


def gather_by_halves(value, along_row):
    across, one, three = [move(value, along_row, f, s) for f, s in ((1, 0), (0, 1), (0, 3))]
    low, high = move(one[:HALF], along_row, 0, 1), move(three[HALF:], along_row, 0, 3)
    near = [([(a, 0, ROWS, 0)], 0, s) for a, s in ((value, 0), (one, 1), (three, 3))]
    near.append(([(low, 0, HALF, 0), (high, 0, HALF, HALF)], 0, 2))
    far = [
        ([(a, 0, ROWS, 0)], 1, s)
        for a, s in ((across, 0), (move(across, along_row, 0, 1), 1), (move(across, along_row, 0, 3), 3))
    ]
    far.append(([(move(low, along_row, 1, 0), 0, HALF, 0), (move(high, along_row, 1, 0), 0, HALF, HALF)], 1, 2))
    return near, far


def turned(half):
    return pltpu.roll(half, BS, 1)


VIEWS = ((0, 1), (1, 0), (2, 3), (3, 2))


def views_of(tile):
    first, second = tile[:, :128], tile[:, 128:]
    return first, turned(first), second, turned(second)


def slot_cols(code):
    return [jnp.where((code >> 8) > a, (code >> (2 * a)) & 3, 7) for a in range(4)]


def spread_masks(code):
    cols = slot_cols(code)
    low = lax.broadcasted_iota(jnp.int32, (16, 128), 1) < BS
    high = jnp.where(low, 0, 1)
    found = [jnp.where(low, cols[a], cols[b]) for a, b in VIEWS]
    return [[f == high + 2 * t for f in found] for t in range(2)]


def collect_masks(code):
    cols = slot_cols(code)
    low = lax.broadcasted_iota(jnp.int32, (16, 128), 1) < BS
    wanted = [jnp.where(low, cols[2 * u], cols[2 * u + 1]) for u in range(2)]
    return [[w == jnp.where(low, j, k) for j, k in VIEWS] for w in wanted]


def choose(masks, views):
    out = jnp.zeros((16, 128), F32)
    for mask, view in zip(masks, views):
        out = jnp.where(mask, view, out)
    return out


def position():
    panel = lax.axis_index("col")
    return lax.axis_index("row"), panel // 2, panel % 2


def put(tile, masks, hi_ref, lo_ref, at, first_row, first_col):
    for g in range(BS // 16):
        rows = slice(first_row + 16 * g, first_row + 16 * g + 16)
        views = views_of(tile[16 * g : 16 * g + 16, :])
        for t in range(2):
            cols = slice(first_col + 128 * t, first_col + 128 * t + 128)
            dense = choose(masks[t], views)
            hi = dense.astype(BF16)
            hi_ref[at, rows, cols] = hi
            lo_ref[at, rows, cols] = (dense - hi.astype(F32)).astype(BF16)


def source_of(place, flip, shift):
    half, spot = place // RING, place % RING
    return (half if flip == 0 else 1 - half) * RING + (spot - shift + RING) % RING


def unpack_left(shards, refs, code_ref, hi_ref, lo_ref):
    row, chip, core = position()
    for pieces, flip, shift in shards:
        source = source_of(chip, flip, shift)
        for at, first, count, start in pieces:
            for n in range(count):
                i = start + n
                masks = spread_masks(code_ref[row * ROWS + i, 2 * source + core])
                put(refs[at][first + n], masks, hi_ref, lo_ref, source, BS * i, 0)


def unpack_right(shards, refs, code_ref, hi_ref, lo_ref):
    row, chip, core = position()
    for pieces, flip, shift in shards:
        source = source_of(row, flip, shift)
        for at, first, count, start in pieces:
            for n in range(count):
                part, i = divmod(start + n, HALF)
                panel = 2 * chip + (core if part == 0 else 1 - core)
                masks = spread_masks(code_ref[source * ROWS + HALF * core + i, panel])
                put(refs[at][first + n], masks, hi_ref, lo_ref, source, BS * i, 256 * part)


def multiply(left_hi, left_lo, right_hi, right_lo, total):
    lefts, rights = [], []
    for k in range(SIDES):
        lefts += [left_hi[k], left_lo[k], left_hi[k]]
        rights += [right_hi[k], right_hi[k], right_lo[k]]
    total[...] = jnp.dot(
        jnp.concatenate(lefts, axis=1), jnp.concatenate(rights, axis=0), preferred_element_type=F32
    )


def flatten(shards):
    arrays, placed = [], []
    for pieces, flip, shift in shards:
        placed.append(([(len(arrays) + n, *piece[1:]) for n, piece in enumerate(pieces)], flip, shift))
        arrays += [piece[0] for piece in pieces]
    return arrays, placed


ANYWHERE = pl.BlockSpec(memory_space=pl.ANY)
LEFT = jax.ShapeDtypeStruct((SIDES, ROWS * BS, 256), BF16)
RIGHT = jax.ShapeDtypeStruct((SIDES, HALF * BS, 512), BF16)
SLOTS = jax.ShapeDtypeStruct((ROWS, BS, 256), F32)


def product(code, left_shards, left_dense, right_shards, last):
    left_arrays, left_plan = flatten(left_shards)
    right_arrays, right_plan = flatten(right_shards)
    n_left, n_right = len(left_arrays), len(right_arrays)

    def kernel(code_ref, *refs):
        left_refs, refs = refs[:n_left], refs[n_left:]
        right_refs, refs = refs[:n_right], refs[n_right:]
        if last:
            hbm, (mine_ref, other_ref), refs = refs[:2], refs[2:4], refs[4:]
        else:
            (mine_ref, other_ref), hbm, refs = refs[:2], refs[2:4], refs[4:]
        left_hi, left_lo, right_hi, right_lo, total, sems = refs
        row, chip, core = position()
        moves = []
        for n, (far, here) in enumerate(zip(hbm, (left_hi, left_lo))):
            ends = (far, here) if last else (here, far)
            moves.append(pltpu.make_async_copy(*ends, sems.at[n]))
        unpack_left(left_plan, left_refs, code_ref, left_hi, left_lo)
        for m in moves:
            m.start()
        unpack_right(right_plan, right_refs, code_ref, right_hi, right_lo)
        if last:
            for m in moves:
                m.wait()
        multiply(left_hi, left_lo, right_hi, right_lo, total)

        for part in range(2):
            panel = 2 * chip + (core if part == 0 else 1 - core)
            for n in range(ROWS):
                if last:
                    i, out_ref, at = n, (mine_ref, other_ref)[part], n
                elif n < HALF:
                    i, out_ref, at = HALF * core + n, mine_ref, HALF * part + n
                else:
                    i, out_ref, at = HALF * (1 - core) + n - HALF, other_ref, HALF * (1 - part) + n - HALF
                masks = collect_masks(code_ref[row * ROWS + i, panel])
                for g in range(BS // 16):
                    first = i * BS + 16 * g
                    rows = pl.ds(first if last else pl.multiple_of(first, 16), 16)
                    tile = total[rows, 256 * part : 256 * part + 256]
                    if last:
                        tile = 0.5 * tile
                    elif n < HALF:
                        at_row = row * ROWS * BS + first + lax.broadcasted_iota(jnp.int32, (16, 256), 0)
                        at_col = panel * 256 + lax.broadcasted_iota(jnp.int32, (16, 256), 1)
                        tile = jnp.where(at_row == at_col, 3.0, 0.0) - tile
                    else:
                        tile = -tile
                    views = views_of(tile)
                    for u in range(2):
                        out_ref[at, 16 * g : 16 * g + 16, 128 * u : 128 * u + 128] = choose(masks[u], views)

        if not last:
            for m in moves:
                m.wait()

    return pl.pallas_call(
        kernel,
        out_shape=[SLOTS, SLOTS] if last else [SLOTS, SLOTS, LEFT, LEFT],
        in_specs=[SMEM] + [VMEM] * (n_left + n_right) + [ANYWHERE] * len(left_dense),
        out_specs=[VMEM, VMEM] if last else [VMEM, VMEM, ANYWHERE, ANYWHERE],
        scratch_shapes=[
            *[pltpu.VMEM(LEFT.shape, BF16)] * 2,
            *[pltpu.VMEM(RIGHT.shape, BF16)] * 2,
            pltpu.VMEM((ROWS * BS, 512), F32),
            pltpu.SemaphoreType.DMA((2,)),
        ],
        compiler_params=pltpu.CompilerParams(vmem_limit_bytes=20 * 2**20),
        cost_estimate=pl.CostEstimate(flops=3 * 2**30, bytes_accessed=2**24, transcendentals=0),
    )(code, *left_arrays, *right_arrays, *left_dense)


def per_device(matrix, pattern_cols, pattern_counts):
    weights = jnp.array([1, 4, 16, 64], jnp.int32)
    code = jnp.sum(pattern_cols * weights, axis=2) + pattern_counts * 256
    core = lax.axis_index("col") % 2

    keep = lax.dynamic_slice_in_dim(matrix, HALF * core, HALF, 0)
    send = lax.dynamic_slice_in_dim(matrix, HALF * (1 - core), HALF, 0)
    halves = jnp.concatenate([keep, other_core(send)], axis=0)
    left = sum(gather_two_stages(matrix, True), [])
    right = sum(gather_two_stages(halves, False), [])
    mine, other, *left = product(code, left, [], right, False)

    right = sum(gather_by_halves(mine + other_core(other), False), [])
    mine, other = product(code, [], left, right, True)
    return mine + other_core(other)


def solution(mesh):
    return jax.shard_map(
        per_device,
        mesh=mesh,
        in_specs=(P("row", None, "col"), P(), P()),
        out_specs=P("row", None, "col"),
        check_vma=False,
    )
```

time: 667 us -> 125 us (0.19)
  the two profiles are of different devices: /device:TPU:8 before, /device:TPU:1 now
where the time goes in v2:
time: 125 us; the launch traced here: 124 us
  starting transfers between devices  50.9 us (41%)
  waiting for transfers between devices  49.8 us (40%)
  Pallas kernels  15.7 us (13%)
  local copies, waits for them, and re-layouts  6.82 us (5%)
    ppermute x23, waiting for transfers between devices, move(): return lax.ppermute(value, ('row', 'col'), pairs)  45.5 us
    ppermute x23, starting transfers between devices, move(): return lax.ppermute(value, ('row', 'col'), pairs)  45 us
    pallas_call x2, Pallas kernels, product(): pl.pallas_call(kernel, out_shape=[SLOTS, SLOTS] if last else [SLOTS, SLOT...  15.7 us
    ppermute x3, starting transfers between devices, other_core(): return lax.ppermute(value, 'col', [(c, c ^ 1) for c in range(2 * SIDES)])  5.98 us
    unnamed x21, local copies, waits for them, and re-layouts  5.64 us
    ppermute x3, waiting for transfers between devices, other_core(): return lax.ppermute(value, 'col', [(c, c ^ 1) for c in range(2 * SIDES)])  4.24 us
  transfers between devices with their start and end apart: 26, of which 15 were waited for; matrix products, arithmetic and copies ran while one was open for 1% of the time, Pallas kernels for 0%

profile of v2, /device:TPU:1, one launch (start us, length us, event | category | flops | bytes accessed | tf_op | source)
XLA Modules:
  0.0 124.5 jit_solution(17359817758949075367)
XLA Ops:
  0.0 2.2 %collective-permute-start.3 = (f32[8,64,256]{2,1,0:T(8,128)}, f32[8,64,256]{2,1,0:T(8,128)S(1)}, u32[]{:S(2)}, u32[]{:S(2)}) collective-permute-start(f32[8,64,256]{2,1,0:T(8,128)} %refs_0_.1), channel_id=1, source_target_pairs={{0,8},{1,9},{2,10},{3,11},{4,12},{5,13},{6,14},{7,15},{8,0},{9,1},... | collective-permute-start | bytes 1572872 | tf_op jit(solution)/shard_map/ppermute | solution.py:28
  2.2 2.7 %collective-permute-start.2 = (f32[8,64,256]{2,1,0:T(8,128)}, f32[8,64,256]{2,1,0:T(8,128)S(1)}, u32[]{:S(2)}, u32[]{:S(2)}) collective-permute-start(f32[8,64,256]{2,1,0:T(8,128)} %refs_0_.1), channel_id=1, source_target_pairs={{0,4},{1,5},{2,6},{3,7},{4,0},{5,1},{6,2},{7,3},{8,12},{9,13},{10,... | collective-permute-start | bytes 1572872 | tf_op jit(solution)/shard_map/ppermute | solution.py:28
  7.5 1.9 %collective-permute-start.7 = (f32[4,64,256]{2,1,0:T(8,128)S(1)}, f32[4,64,256]{2,1,0:T(8,128)S(1)}, u32[]{:S(2)}, u32[]{:S(2)}) collective-permute-start(f32[4,64,256]{2,1,0:T(8,128)S(1)} %get-tuple-element.18), channel_id=1, source_target_pairs={{0,1},{1,0},{2,3},{3,2},{4,5},{5,4},{6,7},{7,6},{8,9},{9,8},{10,11... | collective-permute-start | bytes 786440 | tf_op jit(solution)/shard_map/ppermute | solution.py:32
  9.4 1.2 collective-permute-done.7
  10.6 2.7 %collective-permute-start.11 = (f32[8,64,256]{2,1,0:T(8,128)S(1)}, f32[8,64,256]{2,1,0:T(8,128)}, u32[]{:S(2)}, u32[]{:S(2)}) collective-permute-start(f32[8,64,256]{2,1,0:T(8,128)S(1)} %pad_maximum_fusion.refs_8_), channel_id=1, source_target_pairs={{0,64},{1,65},{2,66},{3,67},{4,68},{5,69},{6,70},{7,71},{8,72},{9,... | collective-permute-start | bytes 1572872 | tf_op jit(solution)/shard_map/ppermute | solution.py:28
  13.7 3.8 %collective-permute-start.10 = (f32[8,64,256]{2,1,0:T(8,128)S(1)}, f32[8,64,256]{2,1,0:T(8,128)}, u32[]{:S(2)}, u32[]{:S(2)}) collective-permute-start(f32[8,64,256]{2,1,0:T(8,128)S(1)} %pad_maximum_fusion.refs_8_), channel_id=1, source_target_pairs={{0,32},{1,33},{2,34},{3,35},{4,36},{5,37},{6,38},{7,39},{8,40},{9,... | collective-permute-start | bytes 1572872 | tf_op jit(solution)/shard_map/ppermute | solution.py:28
  17.5 2.7 %collective-permute-start.9 = (f32[8,64,256]{2,1,0:T(8,128)S(1)}, f32[8,64,256]{2,1,0:T(8,128)S(1)}, u32[]{:S(2)}, u32[]{:S(2)}) collective-permute-start(f32[8,64,256]{2,1,0:T(8,128)S(1)} %pad_maximum_fusion.refs_8_), channel_id=1, source_target_pairs={{0,48},{1,49},{2,50},{3,51},{4,52},{5,53},{6,54},{7,55},{8,56},{9,... | collective-permute-start | bytes 1572872 | tf_op jit(solution)/shard_map/ppermute | solution.py:28
  20.2 8.0 %collective-permute-done.1.refs_2_ = f32[8,64,256]{2,1,0:T(8,128)S(1)} collective-permute-done((f32[8,64,256]{2,1,0:T(8,128)}, f32[8,64,256]{2,1,0:T(8,128)S(1)}, u32[]{:S(2)}, u32[]{:S(2)}) %collective-permute-start.1) | collective-permute-done | bytes 524320 | tf_op jit(solution)/shard_map/ppermute | solution.py:28
  28.2 1.6 %collective-permute-start.8 = (f32[8,64,256]{2,1,0:T(8,128)S(1)}, f32[8,64,256]{2,1,0:T(8,128)S(1)}, u32[]{:S(2)}, u32[]{:S(2)}) collective-permute-start(f32[8,64,256]{2,1,0:T(8,128)S(1)} %pad_maximum_fusion.refs_8_), channel_id=1, source_target_pairs={{0,16},{1,17},{2,18},{3,19},{4,20},{5,21},{6,22},{7,23},{8,24},{9,... | collective-permute-start | bytes 1572872 | tf_op jit(solution)/shard_map/ppermute | solution.py:28
  29.8 3.3 %collective-permute-start.5 = (f32[8,64,256]{2,1,0:T(8,128)S(1)}, f32[8,64,256]{2,1,0:T(8,128)S(1)}, u32[]{:S(2)}, u32[]{:S(2)}) collective-permute-start(f32[8,64,256]{2,1,0:T(8,128)S(1)} %collective-permute-done.3.refs_4_), channel_id=1, source_target_pairs={{0,6},{1,7},{2,0},{3,1},{4,2},{5,3},{6,4},{7,5},{8,14},{9,15},{10,... | collective-permute-start | bytes 1572872 | tf_op jit(solution)/shard_map/ppermute | solution.py:28
  33.4 7.5 %collective-permute-done.9.refs_10_ = f32[8,64,256]{2,1,0:T(8,128)S(1)} collective-permute-done((f32[8,64,256]{2,1,0:T(8,128)S(1)}, f32[8,64,256]{2,1,0:T(8,128)S(1)}, u32[]{:S(2)}, u32[]{:S(2)}) %collective-permute-start.9) | collective-permute-done | bytes 524320 | tf_op jit(solution)/shard_map/ppermute | solution.py:28
  41.7 3.5 %collective-permute-start.13 = (f32[8,64,256]{2,1,0:T(8,128)}, f32[8,64,256]{2,1,0:T(8,128)}, u32[]{:S(2)}, u32[]{:S(2)}) collective-permute-start(f32[8,64,256]{2,1,0:T(8,128)} %collective-permute-done.11.refs_12_), channel_id=1, source_target_pairs={{0,48},{1,49},{2,50},{3,51},{4,52},{5,53},{6,54},{7,55},{8,56},{9,... | collective-permute-start | bytes 1572872 | tf_op jit(solution)/shard_map/ppermute | solution.py:28
  46.8 2.9 %collective-permute-start.14 = (f32[8,64,256]{2,1,0:T(8,128)}, f32[8,64,256]{2,1,0:T(8,128)}, u32[]{:S(2)}, u32[]{:S(2)}) collective-permute-start(f32[8,64,256]{2,1,0:T(8,128)} %collective-permute-done.10.refs_11_), channel_id=1, source_target_pairs={{0,64},{1,65},{2,66},{3,67},{4,68},{5,69},{6,70},{7,71},{8,72},{9,... | collective-permute-start | bytes 1572872 | tf_op jit(solution)/shard_map/ppermute | solution.py:28
  50.0 6.4 %collective-permute-done.13.refs_14_ = f32[8,64,256]{2,1,0:T(8,128)} collective-permute-done((f32[8,64,256]{2,1,0:T(8,128)}, f32[8,64,256]{2,1,0:T(8,128)}, u32[]{:S(2)}, u32[]{:S(2)}) %collective-permute-start.13) | collective-permute-done | bytes 524320 | tf_op jit(solution)/shard_map/ppermute | solution.py:28
  56.4 3.9 %collective-permute-done.12.refs_13_ = f32[8,64,256]{2,1,0:T(8,128)} collective-permute-done((f32[8,64,256]{2,1,0:T(8,128)}, f32[8,64,256]{2,1,0:T(8,128)}, u32[]{:S(2)}, u32[]{:S(2)}) %collective-permute-start.12) | collective-permute-done | bytes 524320 | tf_op jit(solution)/shard_map/ppermute | solution.py:28
  60.3 1.1 collective-permute-done.14.refs_15_
  64.6 9.3 %shard_map.46 = (f32[8,64,256]{2,1,0:T(8,128)S(1)}, f32[8,64,256]{2,1,0:T(8,128)S(1)}, bf16[8,512,256]{2,1,0:T(8,128)(2,1)S(1)}, bf16[8,512,256]{2,1,0:T(8,128)(2,1)S(1)}) custom-call(s32[64,16]{1,0:T(8,128)S(1)} %multiply_add_fusion.code_ref, f32[8,64,256]{2,1,0:T(8,128)S(1)} %copy-done, f32[8,64,256]{2,1,0:T(8,128)S(1)} %collective-permute-done.refs_1_, ...), custom_call_target="tpu_custom_call" | custom-call | flops 3221225472 | bytes 16777216 | tf_op jit(solution)/shard_map/pallas_call | solution.py:224
  73.8 1.6 %collective-permute-start.15 = (f32[8,64,256]{2,1,0:T(8,128)S(1)}, f32[8,64,256]{2,1,0:T(8,128)S(1)}, u32[]{:S(2)}, u32[]{:S(2)}) collective-permute-start(f32[8,64,256]{2,1,0:T(8,128)S(1)} %get-tuple-element.12), channel_id=1, source_target_pairs={{0,1},{1,0},{2,3},{3,2},{4,5},{5,4},{6,7},{7,6},{8,9},{9,8},{10,11... | collective-permute-start | bytes 1572872 | tf_op jit(solution)/shard_map/ppermute | solution.py:32
  75.5 1.5 %collective-permute-done.15 = f32[8,64,256]{2,1,0:T(8,128)S(1)} collective-permute-done((f32[8,64,256]{2,1,0:T(8,128)S(1)}, f32[8,64,256]{2,1,0:T(8,128)S(1)}, u32[]{:S(2)}, u32[]{:S(2)}) %collective-permute-start.15) | collective-permute-done | bytes 524320 | tf_op jit(solution)/shard_map/ppermute | solution.py:32
  77.1 2.7 %collective-permute-start.17 = (f32[8,64,256]{2,1,0:T(8,128)S(1)}, f32[8,64,256]{2,1,0:T(8,128)S(1)}, u32[]{:S(2)}, u32[]{:S(2)}) collective-permute-start(f32[8,64,256]{2,1,0:T(8,128)S(1)} %add.23.refs_0_), channel_id=1, source_target_pairs={{0,48},{1,49},{2,50},{3,51},{4,52},{5,53},{6,54},{7,55},{8,56},{9,... | collective-permute-start | bytes 1572872 | tf_op jit(solution)/shard_map/ppermute | solution.py:28
  79.8 2.9 %collective-permute-start.20 = (f32[8,64,256]{2,1,0:T(8,128)S(1)}, f32[8,64,256]{2,1,0:T(8,128)S(1)}, u32[]{:S(2)}, u32[]{:S(2)}) collective-permute-start(f32[8,64,256]{2,1,0:T(8,128)S(1)} %add.23.refs_0_), channel_id=1, source_target_pairs={{0,64},{1,65},{2,66},{3,67},{4,68},{5,69},{6,70},{7,71},{8,72},{9,... | collective-permute-start | bytes 1572872 | tf_op jit(solution)/shard_map/ppermute | solution.py:28
  82.7 8.0 %collective-permute-done.17.refs_2_ = f32[8,64,256]{2,1,0:T(8,128)S(1)} collective-permute-done((f32[8,64,256]{2,1,0:T(8,128)S(1)}, f32[8,64,256]{2,1,0:T(8,128)S(1)}, u32[]{:S(2)}, u32[]{:S(2)}) %collective-permute-start.17) | collective-permute-done | bytes 524320 | tf_op jit(solution)/shard_map/ppermute | solution.py:28
  90.8 3.5 %collective-permute-start.19 = (f32[4,64,256]{2,1,0:T(8,128)S(1)}, f32[4,64,256]{2,1,0:T(8,128)S(1)}, u32[]{:S(2)}, u32[]{:S(2)}) collective-permute-start(f32[4,64,256]{2,1,0:T(8,128)S(1)} %slice.9), channel_id=1, source_target_pairs={{0,48},{1,49},{2,50},{3,51},{4,52},{5,53},{6,54},{7,55},{8,56},{9,... | collective-permute-start | bytes 786440 | tf_op jit(solution)/shard_map/ppermute | solution.py:28
  94.4 2.7 %collective-permute-start.22 = (f32[8,64,256]{2,1,0:T(8,128)S(1)}, f32[8,64,256]{2,1,0:T(8,128)S(1)}, u32[]{:S(2)}, u32[]{:S(2)}) collective-permute-start(f32[8,64,256]{2,1,0:T(8,128)S(1)} %collective-permute-done.20.refs_5_), channel_id=1, source_target_pairs={{0,48},{1,49},{2,50},{3,51},{4,52},{5,53},{6,54},{7,55},{8,56},{9,... | collective-permute-start | bytes 1572872 | tf_op jit(solution)/shard_map/ppermute | solution.py:28
  97.0 1.6 %collective-permute-done.19.refs_4_ = f32[4,64,256]{2,1,0:T(8,128)S(1)} collective-permute-done((f32[4,64,256]{2,1,0:T(8,128)S(1)}, f32[4,64,256]{2,1,0:T(8,128)S(1)}, u32[]{:S(2)}, u32[]{:S(2)}) %collective-permute-start.19) | collective-permute-done | bytes 262176 | tf_op jit(solution)/shard_map/ppermute | solution.py:28
  98.7 2.9 %collective-permute-start.24 = (f32[4,64,256]{2,1,0:T(8,128)S(1)}, f32[4,64,256]{2,1,0:T(8,128)S(1)}, u32[]{:S(2)}, u32[]{:S(2)}) collective-permute-start(f32[4,64,256]{2,1,0:T(8,128)S(1)} %collective-permute-done.19.refs_4_), channel_id=1, source_target_pairs={{0,64},{1,65},{2,66},{3,67},{4,68},{5,69},{6,70},{7,71},{8,72},{9,... | collective-permute-start | bytes 786440 | tf_op jit(solution)/shard_map/ppermute | solution.py:28
  101.9 2.9 %collective-permute-start.23 = (f32[4,64,256]{2,1,0:T(8,128)S(1)}, f32[4,64,256]{2,1,0:T(8,128)S(1)}, u32[]{:S(2)}, u32[]{:S(2)}) collective-permute-start(f32[4,64,256]{2,1,0:T(8,128)S(1)} %collective-permute-done.18.refs_3_), channel_id=1, source_target_pairs={{0,64},{1,65},{2,66},{3,67},{4,68},{5,69},{6,70},{7,71},{8,72},{9,... | collective-permute-start | bytes 786440 | tf_op jit(solution)/shard_map/ppermute | solution.py:28
  105.4 5.2 %collective-permute-done.23.refs_8_ = f32[4,64,256]{2,1,0:T(8,128)S(1)} collective-permute-done((f32[4,64,256]{2,1,0:T(8,128)S(1)}, f32[4,64,256]{2,1,0:T(8,128)S(1)}, u32[]{:S(2)}, u32[]{:S(2)}) %collective-permute-start.23) | collective-permute-done | bytes 262176 | tf_op jit(solution)/shard_map/ppermute | solution.py:28
  110.6 2.5 %collective-permute-done.21.refs_6_ = f32[8,64,256]{2,1,0:T(8,128)S(1)} collective-permute-done((f32[8,64,256]{2,1,0:T(8,128)S(1)}, f32[8,64,256]{2,1,0:T(8,128)S(1)}, u32[]{:S(2)}, u32[]{:S(2)}) %collective-permute-start.21) | collective-permute-done | bytes 524320 | tf_op jit(solution)/shard_map/ppermute | solution.py:28
  113.1 6.5 %shard_map.47 = (f32[8,64,256]{2,1,0:T(8,128)S(1)}, f32[8,64,256]{2,1,0:T(8,128)S(1)}) custom-call(s32[64,16]{1,0:T(8,128)S(1)} %multiply_add_fusion.code_ref, f32[8,64,256]{2,1,0:T(8,128)S(1)} %add.23.refs_0_, f32[8,64,256]{2,1,0:T(8,128)S(1)} %collective-permute-done.16.refs_1_, f32[8,64,256]{2,1,0:T(8,128)S(1)} %collective-permute-done.17.refs_2_, ...), custom_call_target="tpu_custom_call" | custom-call | flops 3221225472 | bytes 16777216 | tf_op jit(solution)/shard_map/pallas_call | solution.py:224
  119.6 2.5 %collective-permute-start.25 = (f32[8,64,256]{2,1,0:T(8,128)S(1)}, f32[8,64,256]{2,1,0:T(8,128)S(1)}, u32[]{:S(2)}, u32[]{:S(2)}) collective-permute-start(f32[8,64,256]{2,1,0:T(8,128)S(1)} %get-tuple-element.16), channel_id=1, source_target_pairs={{0,1},{1,0},{2,3},{3,2},{4,5},{5,4},{6,7},{7,6},{8,9},{9,8},{10,11... | collective-permute-start | bytes 1572872 | tf_op jit(solution)/shard_map/ppermute | solution.py:32
  122.1 1.5 %collective-permute-done.25 = f32[8,64,256]{2,1,0:T(8,128)S(1)} collective-permute-done((f32[8,64,256]{2,1,0:T(8,128)S(1)}, f32[8,64,256]{2,1,0:T(8,128)S(1)}, u32[]{:S(2)}, u32[]{:S(2)}) %collective-permute-start.25) | collective-permute-done | bytes 524320 | tf_op jit(solution)/shard_map/ppermute | solution.py:32
  (52 shorter events, 11.0 us)
Async XLA Ops:
  0.0 49.7 %copy-start.9 = (s32[4]{0:T(128)S(1)}, s32[4]{0:T(128)}, u32[]{:S(2)}) copy-start(s32[4]{0:T(128)} %constant.27.clone) | copy-start | bytes 52
  0.0 61.4 %copy-start = (f32[8,64,256]{2,1,0:T(8,128)S(1)}, f32[8,64,256]{2,1,0:T(8,128)}, u32[]{:S(2)}) copy-start(f32[8,64,256]{2,1,0:T(8,128)} %refs_0_.1) | copy-start | bytes 1572868
  0.0 49.7 %copy-start.7 = (s32[64,16,4]{0,2,1:T(4,128)S(1)}, s32[64,16,4]{0,2,1:T(4,128)}, u32[]{:S(2)}) copy-start(s32[64,16,4]{0,2,1:T(4,128)} %param.5) | copy-start | bytes 49156
  0.0 49.9 %copy-start.8 = (s32[64,16]{0,1:T(8,128)S(1)}, s32[64,16]{0,1:T(8,128)}, u32[]{:S(2)}) copy-start(s32[64,16]{0,1:T(8,128)} %param.6) | copy-start | bytes 12292
  0.0 13.7 %collective-permute-start.3 = (f32[8,64,256]{2,1,0:T(8,128)}, f32[8,64,256]{2,1,0:T(8,128)S(1)}, u32[]{:S(2)}, u32[]{:S(2)}) collective-permute-start(f32[8,64,256]{2,1,0:T(8,128)} %refs_0_.1), channel_id=1, source_target_pairs={{0,8},{1,9},{2,10},{3,11},{4,12},{5,13},{6,14},{7,15},{8,0},{9,1},... | collective-permute-start | bytes 1572872 | tf_op jit(solution)/shard_map/ppermute | solution.py:28
  2.2 15.3 %collective-permute-start.2 = (f32[8,64,256]{2,1,0:T(8,128)}, f32[8,64,256]{2,1,0:T(8,128)S(1)}, u32[]{:S(2)}, u32[]{:S(2)}) collective-permute-start(f32[8,64,256]{2,1,0:T(8,128)} %refs_0_.1), channel_id=1, source_target_pairs={{0,4},{1,5},{2,6},{3,7},{4,0},{5,1},{6,2},{7,3},{8,12},{9,13},{10,... | collective-permute-start | bytes 1572872 | tf_op jit(solution)/shard_map/ppermute | solution.py:28
  5.0 23.2 %collective-permute-start.1 = (f32[8,64,256]{2,1,0:T(8,128)}, f32[8,64,256]{2,1,0:T(8,128)S(1)}, u32[]{:S(2)}, u32[]{:S(2)}) collective-permute-start(f32[8,64,256]{2,1,0:T(8,128)} %refs_0_.1), channel_id=1, source_target_pairs={{0,6},{1,7},{2,0},{3,1},{4,2},{5,3},{6,4},{7,5},{8,14},{9,15},{10,... | collective-permute-start | bytes 1572872 | tf_op jit(solution)/shard_map/ppermute | solution.py:28
  5.8 24.0 %collective-permute-start = (f32[8,64,256]{2,1,0:T(8,128)}, f32[8,64,256]{2,1,0:T(8,128)S(1)}, u32[]{:S(2)}, u32[]{:S(2)}) collective-permute-start(f32[8,64,256]{2,1,0:T(8,128)} %refs_0_.1), channel_id=1, source_target_pairs={{0,2},{1,3},{2,4},{3,5},{4,6},{5,7},{6,0},{7,1},{8,10},{9,11},{10,... | collective-permute-start | bytes 1572872 | tf_op jit(solution)/shard_map/ppermute | solution.py:28
  7.5 3.0 %collective-permute-start.7 = (f32[4,64,256]{2,1,0:T(8,128)S(1)}, f32[4,64,256]{2,1,0:T(8,128)S(1)}, u32[]{:S(2)}, u32[]{:S(2)}) collective-permute-start(f32[4,64,256]{2,1,0:T(8,128)S(1)} %get-tuple-element.18), channel_id=1, source_target_pairs={{0,1},{1,0},{2,3},{3,2},{4,5},{5,4},{6,7},{7,6},{8,9},{9,8},{10,11... | collective-permute-start | bytes 786440 | tf_op jit(solution)/shard_map/ppermute | solution.py:32
  10.6 22.6 %collective-permute-start.11 = (f32[8,64,256]{2,1,0:T(8,128)S(1)}, f32[8,64,256]{2,1,0:T(8,128)}, u32[]{:S(2)}, u32[]{:S(2)}) collective-permute-start(f32[8,64,256]{2,1,0:T(8,128)S(1)} %pad_maximum_fusion.refs_8_), channel_id=1, source_target_pairs={{0,64},{1,65},{2,66},{3,67},{4,68},{5,69},{6,70},{7,71},{8,72},{9,... | collective-permute-start | bytes 1572872 | tf_op jit(solution)/shard_map/ppermute | solution.py:28
  13.7 19.5 %collective-permute-start.10 = (f32[8,64,256]{2,1,0:T(8,128)S(1)}, f32[8,64,256]{2,1,0:T(8,128)}, u32[]{:S(2)}, u32[]{:S(2)}) collective-permute-start(f32[8,64,256]{2,1,0:T(8,128)S(1)} %pad_maximum_fusion.refs_8_), channel_id=1, source_target_pairs={{0,32},{1,33},{2,34},{3,35},{4,36},{5,37},{6,38},{7,39},{8,40},{9,... | collective-permute-start | bytes 1572872 | tf_op jit(solution)/shard_map/ppermute | solution.py:28
  17.5 23.3 %collective-permute-start.9 = (f32[8,64,256]{2,1,0:T(8,128)S(1)}, f32[8,64,256]{2,1,0:T(8,128)S(1)}, u32[]{:S(2)}, u32[]{:S(2)}) collective-permute-start(f32[8,64,256]{2,1,0:T(8,128)S(1)} %pad_maximum_fusion.refs_8_), channel_id=1, source_target_pairs={{0,48},{1,49},{2,50},{3,51},{4,52},{5,53},{6,54},{7,55},{8,56},{9,... | collective-permute-start | bytes 1572872 | tf_op jit(solution)/shard_map/ppermute | solution.py:28
  28.2 17.0 %collective-permute-start.8 = (f32[8,64,256]{2,1,0:T(8,128)S(1)}, f32[8,64,256]{2,1,0:T(8,128)S(1)}, u32[]{:S(2)}, u32[]{:S(2)}) collective-permute-start(f32[8,64,256]{2,1,0:T(8,128)S(1)} %pad_maximum_fusion.refs_8_), channel_id=1, source_target_pairs={{0,16},{1,17},{2,18},{3,19},{4,20},{5,21},{6,22},{7,23},{8,24},{9,... | collective-permute-start | bytes 1572872 | tf_op jit(solution)/shard_map/ppermute | solution.py:28
  29.8 16.2 %collective-permute-start.5 = (f32[8,64,256]{2,1,0:T(8,128)S(1)}, f32[8,64,256]{2,1,0:T(8,128)S(1)}, u32[]{:S(2)}, u32[]{:S(2)}) collective-permute-start(f32[8,64,256]{2,1,0:T(8,128)S(1)} %collective-permute-done.3.refs_4_), channel_id=1, source_target_pairs={{0,6},{1,7},{2,0},{3,1},{4,2},{5,3},{6,4},{7,5},{8,14},{9,15},{10,... | collective-permute-start | bytes 1572872 | tf_op jit(solution)/shard_map/ppermute | solution.py:28
  33.1 16.9 %collective-permute-start.4 = (f32[8,64,256]{2,1,0:T(8,128)S(1)}, f32[8,64,256]{2,1,0:T(8,128)}, u32[]{:S(2)}, u32[]{:S(2)}) collective-permute-start(f32[8,64,256]{2,1,0:T(8,128)S(1)} %collective-permute-done.3.refs_4_), channel_id=1, source_target_pairs={{0,2},{1,3},{2,4},{3,5},{4,6},{5,7},{6,0},{7,1},{8,10},{9,11},{10,... | collective-permute-start | bytes 1572872 | tf_op jit(solution)/shard_map/ppermute | solution.py:28
  33.2 16.9 %collective-permute-start.6 = (f32[8,64,256]{2,1,0:T(8,128)S(1)}, f32[8,64,256]{2,1,0:T(8,128)}, u32[]{:S(2)}, u32[]{:S(2)}) collective-permute-start(f32[8,64,256]{2,1,0:T(8,128)S(1)} %collective-permute-done.2.refs_3_), channel_id=1, source_target_pairs={{0,8},{1,9},{2,10},{3,11},{4,12},{5,13},{6,14},{7,15},{8,0},{9,1},... | collective-permute-start | bytes 1572872 | tf_op jit(solution)/shard_map/ppermute | solution.py:28
  41.7 14.7 %collective-permute-start.13 = (f32[8,64,256]{2,1,0:T(8,128)}, f32[8,64,256]{2,1,0:T(8,128)}, u32[]{:S(2)}, u32[]{:S(2)}) collective-permute-start(f32[8,64,256]{2,1,0:T(8,128)} %collective-permute-done.11.refs_12_), channel_id=1, source_target_pairs={{0,48},{1,49},{2,50},{3,51},{4,52},{5,53},{6,54},{7,55},{8,56},{9,... | collective-permute-start | bytes 1572872 | tf_op jit(solution)/shard_map/ppermute | solution.py:28
  46.0 14.3 %collective-permute-start.12 = (f32[8,64,256]{2,1,0:T(8,128)}, f32[8,64,256]{2,1,0:T(8,128)}, u32[]{:S(2)}, u32[]{:S(2)}) collective-permute-start(f32[8,64,256]{2,1,0:T(8,128)} %collective-permute-done.11.refs_12_), channel_id=1, source_target_pairs={{0,16},{1,17},{2,18},{3,19},{4,20},{5,21},{6,22},{7,23},{8,24},{9,... | collective-permute-start | bytes 1572872 | tf_op jit(solution)/shard_map/ppermute | solution.py:28
  46.8 14.6 %collective-permute-start.14 = (f32[8,64,256]{2,1,0:T(8,128)}, f32[8,64,256]{2,1,0:T(8,128)}, u32[]{:S(2)}, u32[]{:S(2)}) collective-permute-start(f32[8,64,256]{2,1,0:T(8,128)} %collective-permute-done.10.refs_11_), channel_id=1, source_target_pairs={{0,64},{1,65},{2,66},{3,67},{4,68},{5,69},{6,70},{7,71},{8,72},{9,... | collective-permute-start | bytes 1572872 | tf_op jit(solution)/shard_map/ppermute | solution.py:28
  61.4 1.0 copy-start.2
  62.5 1.0 copy-start.4
  73.8 3.2 %collective-permute-start.15 = (f32[8,64,256]{2,1,0:T(8,128)S(1)}, f32[8,64,256]{2,1,0:T(8,128)S(1)}, u32[]{:S(2)}, u32[]{:S(2)}) collective-permute-start(f32[8,64,256]{2,1,0:T(8,128)S(1)} %get-tuple-element.12), channel_id=1, source_target_pairs={{0,1},{1,0},{2,3},{3,2},{4,5},{5,4},{6,7},{7,6},{8,9},{9,8},{10,11... | collective-permute-start | bytes 1572872 | tf_op jit(solution)/shard_map/ppermute | solution.py:32
  77.1 13.7 %collective-permute-start.17 = (f32[8,64,256]{2,1,0:T(8,128)S(1)}, f32[8,64,256]{2,1,0:T(8,128)S(1)}, u32[]{:S(2)}, u32[]{:S(2)}) collective-permute-start(f32[8,64,256]{2,1,0:T(8,128)S(1)} %add.23.refs_0_), channel_id=1, source_target_pairs={{0,48},{1,49},{2,50},{3,51},{4,52},{5,53},{6,54},{7,55},{8,56},{9,... | collective-permute-start | bytes 1572872 | tf_op jit(solution)/shard_map/ppermute | solution.py:28
  79.8 14.4 %collective-permute-start.16 = (f32[8,64,256]{2,1,0:T(8,128)S(1)}, f32[8,64,256]{2,1,0:T(8,128)S(1)}, u32[]{:S(2)}, u32[]{:S(2)}) collective-permute-start(f32[8,64,256]{2,1,0:T(8,128)S(1)} %add.23.refs_0_), channel_id=1, source_target_pairs={{0,16},{1,17},{2,18},{3,19},{4,20},{5,21},{6,22},{7,23},{8,24},{9,... | collective-permute-start | bytes 1572872 | tf_op jit(solution)/shard_map/ppermute | solution.py:28
  79.8 14.5 %collective-permute-start.20 = (f32[8,64,256]{2,1,0:T(8,128)S(1)}, f32[8,64,256]{2,1,0:T(8,128)S(1)}, u32[]{:S(2)}, u32[]{:S(2)}) collective-permute-start(f32[8,64,256]{2,1,0:T(8,128)S(1)} %add.23.refs_0_), channel_id=1, source_target_pairs={{0,64},{1,65},{2,66},{3,67},{4,68},{5,69},{6,70},{7,71},{8,72},{9,... | collective-permute-start | bytes 1572872 | tf_op jit(solution)/shard_map/ppermute | solution.py:28
  90.8 7.9 %collective-permute-start.19 = (f32[4,64,256]{2,1,0:T(8,128)S(1)}, f32[4,64,256]{2,1,0:T(8,128)S(1)}, u32[]{:S(2)}, u32[]{:S(2)}) collective-permute-start(f32[4,64,256]{2,1,0:T(8,128)S(1)} %slice.9), channel_id=1, source_target_pairs={{0,48},{1,49},{2,50},{3,51},{4,52},{5,53},{6,54},{7,55},{8,56},{9,... | collective-permute-start | bytes 786440 | tf_op jit(solution)/shard_map/ppermute | solution.py:28
  94.3 7.6 %collective-permute-start.18 = (f32[4,64,256]{2,1,0:T(8,128)S(1)}, f32[4,64,256]{2,1,0:T(8,128)S(1)}, u32[]{:S(2)}, u32[]{:S(2)}) collective-permute-start(f32[4,64,256]{2,1,0:T(8,128)S(1)} %slice.8), channel_id=1, source_target_pairs={{0,16},{1,17},{2,18},{3,19},{4,20},{5,21},{6,22},{7,23},{8,24},{9,... | collective-permute-start | bytes 786440 | tf_op jit(solution)/shard_map/ppermute | solution.py:28
  94.4 16.2 %collective-permute-start.22 = (f32[8,64,256]{2,1,0:T(8,128)S(1)}, f32[8,64,256]{2,1,0:T(8,128)S(1)}, u32[]{:S(2)}, u32[]{:S(2)}) collective-permute-start(f32[8,64,256]{2,1,0:T(8,128)S(1)} %collective-permute-done.20.refs_5_), channel_id=1, source_target_pairs={{0,48},{1,49},{2,50},{3,51},{4,52},{5,53},{6,54},{7,55},{8,56},{9,... | collective-permute-start | bytes 1572872 | tf_op jit(solution)/shard_map/ppermute | solution.py:28
  97.0 16.1 %collective-permute-start.21 = (f32[8,64,256]{2,1,0:T(8,128)S(1)}, f32[8,64,256]{2,1,0:T(8,128)S(1)}, u32[]{:S(2)}, u32[]{:S(2)}) collective-permute-start(f32[8,64,256]{2,1,0:T(8,128)S(1)} %collective-permute-done.20.refs_5_), channel_id=1, source_target_pairs={{0,16},{1,17},{2,18},{3,19},{4,20},{5,21},{6,22},{7,23},{8,24},{9,... | collective-permute-start | bytes 1572872 | tf_op jit(solution)/shard_map/ppermute | solution.py:28
  98.7 6.7 %collective-permute-start.24 = (f32[4,64,256]{2,1,0:T(8,128)S(1)}, f32[4,64,256]{2,1,0:T(8,128)S(1)}, u32[]{:S(2)}, u32[]{:S(2)}) collective-permute-start(f32[4,64,256]{2,1,0:T(8,128)S(1)} %collective-permute-done.19.refs_4_), channel_id=1, source_target_pairs={{0,64},{1,65},{2,66},{3,67},{4,68},{5,69},{6,70},{7,71},{8,72},{9,... | collective-permute-start | bytes 786440 | tf_op jit(solution)/shard_map/ppermute | solution.py:28
  101.9 8.7 %collective-permute-start.23 = (f32[4,64,256]{2,1,0:T(8,128)S(1)}, f32[4,64,256]{2,1,0:T(8,128)S(1)}, u32[]{:S(2)}, u32[]{:S(2)}) collective-permute-start(f32[4,64,256]{2,1,0:T(8,128)S(1)} %collective-permute-done.18.refs_3_), channel_id=1, source_target_pairs={{0,64},{1,65},{2,66},{3,67},{4,68},{5,69},{6,70},{7,71},{8,72},{9,... | collective-permute-start | bytes 786440 | tf_op jit(solution)/shard_map/ppermute | solution.py:28
  119.6 4.0 %collective-permute-start.25 = (f32[8,64,256]{2,1,0:T(8,128)S(1)}, f32[8,64,256]{2,1,0:T(8,128)S(1)}, u32[]{:S(2)}, u32[]{:S(2)}) collective-permute-start(f32[8,64,256]{2,1,0:T(8,128)S(1)} %get-tuple-element.16), channel_id=1, source_target_pairs={{0,1},{1,0},{2,3},{3,2},{4,5},{5,4},{6,7},{7,6},{8,9},{9,8},{10,11... | collective-permute-start | bytes 1572872 | tf_op jit(solution)/shard_map/ppermute | solution.py:32
  (4 other events, 3.5 us)

commit v3 on v2

v3 whole, which is shorter than its diff:
```python
import jax
import jax.numpy as jnp
from jax import lax
from jax.experimental import pallas as pl
from jax.experimental.pallas import tpu as pltpu
from jax.sharding import PartitionSpec as P

ROWS = 8
HALF = ROWS // 2
BS = 64
RING = 4
KINDS = ("M", "M", "M")
TIE = False
SIDES = 8
VMEM = pl.BlockSpec(memory_space=pltpu.VMEM)
SMEM = pl.BlockSpec(memory_space=pltpu.SMEM)
BF16 = jnp.bfloat16
F32 = jnp.float32


def move(value, along_row, flip, shift):
    pairs = []
    for row in range(SIDES):
        for chip in range(SIDES):
            half, at = divmod(chip if along_row else row, RING)
            place = (half ^ flip) * RING + (at + shift) % RING
            target = (row, place) if along_row else (place, chip)
            for core in range(2):
                pairs.append(((row * SIDES + chip) * 2 + core, (target[0] * SIDES + target[1]) * 2 + core))
    return lax.ppermute(value, ("row", "col"), pairs)


def other_core(value):
    return lax.ppermute(value, "col", [(c, c ^ 1) for c in range(2 * SIDES)])


def whole(array, flip, shift):
    return [(array, 0, ROWS, 0)], flip, shift


def by_half(low, high, flip, first=(0, 0)):
    return [(low, first[0], HALF, 0), (high, first[1], HALF, HALF)], flip, 2


def gather(value, along_row, kind, use_early=None):
    step = lambda v, flip, shift: move(v, along_row, flip, shift)
    across, one, three = step(value, 1, 0), step(value, 0, 1), step(value, 0, 3)
    low = high = two = None
    if kind in ("P", "L7", "L8"):
        two = step(value, 0, 2)
        own_two = whole(two, 0, 2)
    elif kind == "W":
        two = step(one, 0, 1)
        own_two = whole(two, 0, 2)
    else:
        low, high = step(one[:HALF], 0, 1), step(three[HALF:], 0, 3)
        own_two = by_half(low, high, 0)
    early = [whole(value, 0, 0), whole(one, 0, 1), whole(three, 0, 3), own_two, whole(across, 1, 0)]
    used = None
    if use_early:
        used = list(use_early(early))
        if TIE and two is not None and kind in ("P", "W"):
            two, used[0] = lax.optimization_barrier((two, used[0]))
    g1, g3 = step(across, 0, 1), step(across, 0, 3)
    if kind in ("P", "W"):
        far_two = whole(step(two, 1, 0), 1, 2)
    elif kind == "F":
        far_two = by_half(step(low, 1, 0), step(high, 1, 0), 1)
    elif kind == "M":
        both = step(jnp.concatenate([low, high], axis=0), 1, 0)
        far_two = whole(both, 1, 2)
    elif kind == "L7":
        far_two = whole(step(g1, 0, 1), 1, 2)
    else:
        far_two = by_half(step(g1[:HALF], 0, 1), step(g3[HALF:], 0, 3), 1)
    late = [whole(g1, 1, 1), whole(g3, 1, 3), far_two]
    return early, used, late


def turned(half):
    return pltpu.roll(half, BS, 1)


VIEWS = ((0, 1), (1, 0), (2, 3), (3, 2))


def views_of(tile):
    first, second = tile[:, :128], tile[:, 128:]
    return first, turned(first), second, turned(second)


def slot_cols(code):
    return [jnp.where((code >> 8) > a, (code >> (2 * a)) & 3, 7) for a in range(4)]


def spread_masks(code):
    cols = slot_cols(code)
    low = lax.broadcasted_iota(jnp.int32, (16, 128), 1) < BS
    high = jnp.where(low, 0, 1)
    found = [jnp.where(low, cols[a], cols[b]) for a, b in VIEWS]
    return [[f == high + 2 * t for f in found] for t in range(2)]


def collect_masks(code):
    cols = slot_cols(code)
    low = lax.broadcasted_iota(jnp.int32, (16, 128), 1) < BS
    wanted = [jnp.where(low, cols[2 * u], cols[2 * u + 1]) for u in range(2)]
    return [[w == jnp.where(low, j, k) for j, k in VIEWS] for w in wanted]


def choose(masks, views):
    out = jnp.zeros((16, 128), F32)
    for mask, view in zip(masks, views):
        out = jnp.where(mask, view, out)
    return out


def position():
    panel = lax.axis_index("col")
    return lax.axis_index("row"), panel // 2, panel % 2


def put(tile, masks, hi_ref, lo_ref, at, first_row, first_col):
    for g in range(BS // 16):
        rows = slice(first_row + 16 * g, first_row + 16 * g + 16)
        views = views_of(tile[16 * g : 16 * g + 16, :])
        for t in range(2):
            cols = slice(first_col + 128 * t, first_col + 128 * t + 128)
            dense = choose(masks[t], views)
            hi = dense.astype(BF16)
            hi_ref[at, rows, cols] = hi
            lo_ref[at, rows, cols] = (dense - hi.astype(F32)).astype(BF16)


def source_of(place, flip, shift):
    half, spot = place // RING, place % RING
    return (half if flip == 0 else 1 - half) * RING + (spot - shift + RING) % RING


def unpack_left(shards, refs, code_ref, hi_ref, lo_ref, by_source):
    row, chip, core = position()
    for place, (pieces, flip, shift) in enumerate(shards):
        source = source_of(chip, flip, shift)
        for at, first, count, start in pieces:
            for n in range(count):
                i = start + n
                masks = spread_masks(code_ref[row * ROWS + i, 2 * source + core])
                put(refs[at][first + n], masks, hi_ref, lo_ref, source if by_source else place, BS * i, 0)


def unpack_right(shards, refs, code_ref, hi_ref, lo_ref, by_source):
    row, chip, core = position()
    for place, (pieces, flip, shift) in enumerate(shards):
        source = source_of(row, flip, shift)
        for at, first, count, start in pieces:
            for n in range(count):
                part, i = divmod(start + n, HALF)
                panel = 2 * chip + (core if part == 0 else 1 - core)
                masks = spread_masks(code_ref[source * ROWS + HALF * core + i, panel])
                at_place = source if by_source else place
                put(refs[at][first + n], masks, hi_ref, lo_ref, at_place, BS * i, 256 * part)


def multiply(left_hi, left_lo, right_hi, right_lo, count):
    lefts, rights = [], []
    for k in range(count):
        lefts += [left_hi[k], left_lo[k], left_hi[k]]
        rights += [right_hi[k], right_hi[k], right_lo[k]]
    return jnp.dot(jnp.concatenate(lefts, axis=1), jnp.concatenate(rights, axis=0), preferred_element_type=F32)


def collect(total, code_ref, part, i, finish, out_ref, at):
    row, chip, core = position()
    panel = 2 * chip + (core if part == 0 else 1 - core)
    masks = collect_masks(code_ref[row * ROWS + i, panel])
    for g in range(BS // 16):
        first = i * BS + 16 * g
        rows = pl.ds(first if isinstance(first, int) else pl.multiple_of(first, 16), 16)
        views = views_of(finish(total[rows, 256 * part : 256 * part + 256], row * ROWS * BS + first, panel * 256))
        for u in range(2):
            out_ref[at, 16 * g : 16 * g + 16, 128 * u : 128 * u + 128] = choose(masks[u], views)


def from_three(tile, first_row, first_col):
    at_row = first_row + lax.broadcasted_iota(jnp.int32, (16, 256), 0)
    at_col = first_col + lax.broadcasted_iota(jnp.int32, (16, 256), 1)
    return jnp.where(at_row == at_col, 3.0, 0.0) - tile


def flatten(shards):
    arrays, placed = [], []
    for pieces, flip, shift in shards:
        placed.append(([(len(arrays) + n, *piece[1:]) for n, piece in enumerate(pieces)], flip, shift))
        arrays += [piece[0] for piece in pieces]
    return arrays, placed


ANYWHERE = pl.BlockSpec(memory_space=pl.ANY)
SLOTS = jax.ShapeDtypeStruct((ROWS, BS, 256), F32)


def left_shape(count):
    return (count, ROWS * BS, 256)


def right_shape(count):
    return (count, HALF * BS, 512)


def call(kernel, inputs, in_specs, outs, out_specs, scratch, megabytes, microseconds):
    return pl.pallas_call(
        kernel,
        out_shape=outs,
        in_specs=in_specs,
        out_specs=out_specs,
        scratch_shapes=scratch,
        compiler_params=pltpu.CompilerParams(vmem_limit_bytes=megabytes * 2**20),
        cost_estimate=pl.CostEstimate(flops=0, bytes_accessed=microseconds * 3_000_000, transcendentals=0),
    )(*inputs)


def make_dense(code, along_row, shards):
    arrays, plan = flatten(shards)
    unpack, shape = (unpack_left, left_shape) if along_row else (unpack_right, right_shape)

    def kernel(code_ref, *refs):
        unpack(plan, refs, code_ref, refs[-2], refs[-1], False)

    outs = [jax.ShapeDtypeStruct(shape(len(shards)), BF16)] * 2
    return call(kernel, [code, *arrays], [SMEM] + [VMEM] * len(arrays), outs, [VMEM] * 2, [], 8, 2)


def square(code, early, dense, left_shards, right_shards):
    left_arrays, left_plan = flatten(left_shards)
    right_arrays, right_plan = flatten(right_shards)
    n_left = len(left_arrays)
    n_in = n_left + len(right_arrays)
    places = [(flip, shift) for _, flip, shift in early]

    def kernel(code_ref, *refs):
        near, refs = refs[:4], refs[4:]
        left_refs, right_refs, refs = refs[:n_left], refs[n_left:n_in], refs[n_in:]
        keep_ref, send_ref, *stored = refs[:4]
        *sides, total, load_sems, store_sems = refs[4:]
        row, chip, core = position()
        loads = []
        for n, (there, here) in enumerate(zip(near, sides)):
            for k, (flip, shift) in enumerate(places):
                at = here.at[source_of(chip if n < 2 else row, flip, shift)]
                loads.append(pltpu.make_async_copy(there.at[k], at, load_sems.at[n * len(places) + k]))
        for m in loads:
            m.start()
        unpack_left(left_plan, left_refs, code_ref, sides[0], sides[1], True)
        unpack_right(right_plan, right_refs, code_ref, sides[2], sides[3], True)
        for m in loads:
            m.wait()
        stores = [pltpu.make_async_copy(sides[n], stored[n], store_sems.at[n]) for n in range(2)]
        for m in stores:
            m.start()
        total[...] = multiply(*sides, SIDES)
        for part in range(2):
            for n in range(HALF):
                collect(total, code_ref, part, HALF * core + n, from_three, keep_ref, HALF * part + n)
                collect(
                    total, code_ref, part, HALF * (1 - core) + n, lambda t, *_: -t, send_ref, HALF * (1 - part) + n
                )
        for m in stores:
            m.wait()

    left = jax.ShapeDtypeStruct(left_shape(SIDES), BF16)
    return call(
        kernel,
        [code, *dense, *left_arrays, *right_arrays],
        [SMEM] + [ANYWHERE] * 4 + [VMEM] * n_in,
        [SLOTS, SLOTS, left, left],
        [VMEM, VMEM, ANYWHERE, ANYWHERE],
        [
            *[pltpu.VMEM(left_shape(SIDES), BF16)] * 2,
            *[pltpu.VMEM(right_shape(SIDES), BF16)] * 2,
            pltpu.VMEM((ROWS * BS, 512), F32),
            pltpu.SemaphoreType.DMA((4 * len(places),)),
            pltpu.SemaphoreType.DMA((2,)),
        ],
        20,
        9,
    )


def times(code, left, right_shards, before=None):
    arrays, plan = flatten(right_shards)
    n_in, count = len(arrays), len(right_shards)
    extra = [] if before is None else [before]

    def kernel(code_ref, far_hi, far_lo, *refs):
        arrived, refs = refs[:n_in], refs[n_in:]
        before_ref, refs = refs[: len(extra)], refs[len(extra) :]
        outs, refs = refs[: 1 + len(extra)], refs[1 + len(extra) :]
        *sides, sems = refs
        row, _, _ = position()
        loads = []
        for k, (_, flip, shift) in enumerate(plan):
            source = source_of(row, flip, shift)
            for n, far in enumerate((far_hi, far_lo)):
                loads.append(pltpu.make_async_copy(far.at[source], sides[n].at[k], sems.at[2 * k + n]))
        for m in loads:
            m.start()
        unpack_right(plan, arrived, code_ref, sides[2], sides[3], False)
        for m in loads:
            m.wait()
        if not extra:
            outs[0][...] = multiply(*sides[:4], count)
            return
        total = sides[4]
        total[...] = before_ref[0][...] + multiply(*sides[:4], count)
        for part in range(2):
            for i in range(ROWS):
                collect(total, code_ref, part, i, lambda t, *_: 0.5 * t, outs[part], i)

    dense = jax.ShapeDtypeStruct((ROWS * BS, 512), F32)
    return call(
        kernel,
        [code, *left, *arrays, *extra],
        [SMEM] + [ANYWHERE] * 2 + [VMEM] * (n_in + len(extra)),
        [SLOTS, SLOTS] if extra else [dense],
        [VMEM, VMEM] if extra else [VMEM],
        [
            *[pltpu.VMEM(left_shape(count), BF16)] * 2,
            *[pltpu.VMEM(right_shape(count), BF16)] * 2,
            *([pltpu.VMEM((ROWS * BS, 512), F32)] if extra else []),
            pltpu.SemaphoreType.DMA((2 * count,)),
        ],
        14,
        4,
    )


def per_device(matrix, pattern_cols, pattern_counts):
    weights = jnp.array([1, 4, 16, 64], jnp.int32)
    code = jnp.sum(pattern_cols * weights, axis=2) + pattern_counts * 256
    core = lax.axis_index("col") % 2

    keep = lax.dynamic_slice_in_dim(matrix, HALF * core, HALF, 0)
    send = lax.dynamic_slice_in_dim(matrix, HALF * (1 - core), HALF, 0)
    halves = jnp.concatenate([keep, other_core(send)], axis=0)
    left_early, left_dense, left_late = gather(matrix, True, KINDS[0], lambda x: make_dense(code, True, x))
    right_early, right_dense, right_late = gather(halves, False, KINDS[1], lambda x: make_dense(code, False, x))
    keep, send, *left = square(code, left_early, left_dense + right_dense, left_late, right_late)

    early, _, late = gather(keep + other_core(send), False, KINDS[2])
    part = times(code, left, early)[0]
    mine, other = times(code, left, late, part)
    return mine + other_core(other)


def solution(mesh):
    return jax.shard_map(
        per_device,
        mesh=mesh,
        in_specs=(P("row", None, "col"), P(), P()),
        out_specs=P("row", None, "col"),
        check_vma=False,
    )
```

time: 125 us -> 117 us (0.936)
  waiting for transfers between devices: 49.8 us -> 44.4 us
  starting transfers between devices: 50.9 us -> 45.6 us
  Pallas kernels: 15.7 us -> 19.5 us
  local copies, waits for them, and re-layouts: 6.82 us -> 3.82 us
  other arithmetic: 1.07 us -> 2.93 us
    ppermute x23 -> x24, starting transfers between devices: 45 us -> 36.4 us  [move(): return lax.ppermute(value, ('row', 'col'), pairs)]
    ppermute x23 -> x24, waiting for transfers between devices: 45.5 us -> 41.3 us  [move(): return lax.ppermute(value, ('row', 'col'), pairs)]
    pallas_call x2 -> x5, Pallas kernels: 15.7 us -> 19.5 us  [call(): pl.pallas_call(kernel, out_shape=outs, in_specs=in_specs, out_specs=out_s...]
    ppermute x3, starting transfers between devices: 5.98 us -> 9.28 us  [other_core(): return lax.ppermute(value, 'col', [(c, c ^ 1) for c in range(2 * SIDES)])]
    unnamed x21 -> x25, local copies, waits for them, and re-layouts: 5.64 us -> 2.57 us
    concatenate x0 -> x3, other arithmetic: none -> 1.86 us  [gather(): both = step(jnp.concatenate([low, high], axis=0), 1, 0)]
  transfers between devices with their start and end apart: 26 -> 27, of which waited for: 15 -> 13; matrix products, arithmetic and copies ran while one was open for 1% -> 2% of each run, Pallas kernels for 0% -> 7%
where the time goes in v3:
time: 117 us
  starting transfers between devices  45.6 us (39%)
  waiting for transfers between devices  44.4 us (38%)
  Pallas kernels  19.5 us (17%)
  local copies, waits for them, and re-layouts  3.82 us (3%)
  other arithmetic  2.93 us (3%)
    ppermute x24, waiting for transfers between devices, move(): return lax.ppermute(value, ('row', 'col'), pairs)  41.3 us
    ppermute x24, starting transfers between devices, move(): return lax.ppermute(value, ('row', 'col'), pairs)  36.4 us
    pallas_call x5, Pallas kernels, call(): pl.pallas_call(kernel, out_shape=outs, in_specs=in_specs, out_specs=out_s...  19.5 us
    ppermute x3, starting transfers between devices, other_core(): return lax.ppermute(value, 'col', [(c, c ^ 1) for c in range(2 * SIDES)])  9.28 us
    ppermute x3, waiting for transfers between devices, other_core(): return lax.ppermute(value, 'col', [(c, c ^ 1) for c in range(2 * SIDES)])  3.08 us
    unnamed x25, local copies, waits for them, and re-layouts  2.57 us
  transfers between devices with their start and end apart: 27, of which 13 were waited for; matrix products, arithmetic and copies ran while one was open for 2% of the time, Pallas kernels for 7%

profile of v3, /device:TPU:1, one launch (start us, length us, event | category | flops | bytes accessed | tf_op | source)
XLA Modules:
  0.0 116.5 jit_solution(3610649963224075231)
XLA Ops:
  1.1 1.5 %collective-permute-start.5 = (f32[4,64,256]{2,1,0:T(8,128)S(1)}, f32[4,64,256]{2,1,0:T(8,128)S(1)}, u32[]{:S(2)}, u32[]{:S(2)}) collective-permute-start(f32[4,64,256]{2,1,0:T(8,128)S(1)} %get-tuple-element.26), channel_id=1, source_target_pairs={{0,1},{1,0},{2,3},{3,2},{4,5},{5,4},{6,7},{7,6},{8,9},{9,8},{10,11... | collective-permute-start | bytes 786440 | tf_op jit(solution)/shard_map/ppermute | solution.py:34
  2.6 2.6 %collective-permute-start.1 = (f32[8,64,256]{2,1,0:T(8,128)}, f32[8,64,256]{2,1,0:T(8,128)S(1)}, u32[]{:S(2)}, u32[]{:S(2)}) collective-permute-start(f32[8,64,256]{2,1,0:T(8,128)} %refs_0_.1), channel_id=1, source_target_pairs={{0,6},{1,7},{2,0},{3,1},{4,2},{5,3},{6,4},{7,5},{8,14},{9,15},{10,... | collective-permute-start | bytes 1572872 | tf_op jit(solution)/shard_map/ppermute | solution.py:30
  5.1 1.3 %collective-permute-start.4 = (f32[8,64,256]{2,1,0:T(8,128)}, f32[8,64,256]{2,1,0:T(8,128)}, u32[]{:S(2)}, u32[]{:S(2)}) collective-permute-start(f32[8,64,256]{2,1,0:T(8,128)} %refs_0_.1), channel_id=1, source_target_pairs={{0,8},{1,9},{2,10},{3,11},{4,12},{5,13},{6,14},{7,15},{8,0},{9,1},... | collective-permute-start | bytes 1572872 | tf_op jit(solution)/shard_map/ppermute | solution.py:30
  6.5 3.8 %collective-permute-start.7 = (f32[8,64,256]{2,1,0:T(8,128)S(1)}, f32[8,64,256]{2,1,0:T(8,128)S(1)}, u32[]{:S(2)}, u32[]{:S(2)}) collective-permute-start(f32[8,64,256]{2,1,0:T(8,128)S(1)} %pad_maximum_fusion.refs_0_), channel_id=1, source_target_pairs={{0,48},{1,49},{2,50},{3,51},{4,52},{5,53},{6,54},{7,55},{8,56},{9,... | collective-permute-start | bytes 1572872 | tf_op jit(solution)/shard_map/ppermute | solution.py:30
  10.3 6.4 %collective-permute-done.1.refs_2_ = f32[8,64,256]{2,1,0:T(8,128)S(1)} collective-permute-done((f32[8,64,256]{2,1,0:T(8,128)}, f32[8,64,256]{2,1,0:T(8,128)S(1)}, u32[]{:S(2)}, u32[]{:S(2)}) %collective-permute-start.1) | collective-permute-done | bytes 524320 | tf_op jit(solution)/shard_map/ppermute | solution.py:30
  16.7 2.9 %collective-permute-start.10 = (f32[8,64,256]{2,1,0:T(8,128)S(1)}, f32[8,64,256]{2,1,0:T(8,128)}, u32[]{:S(2)}, u32[]{:S(2)}) collective-permute-start(f32[8,64,256]{2,1,0:T(8,128)S(1)} %pad_maximum_fusion.refs_0_), channel_id=1, source_target_pairs={{0,64},{1,65},{2,66},{3,67},{4,68},{5,69},{6,70},{7,71},{8,72},{9,... | collective-permute-start | bytes 1572872 | tf_op jit(solution)/shard_map/ppermute | solution.py:30
  19.7 3.4 %collective-permute-start.3 = (f32[4,64,256]{2,1,0:T(8,128)S(1)}, f32[4,64,256]{2,1,0:T(8,128)S(1)}, u32[]{:S(2)}, u32[]{:S(2)}) collective-permute-start(f32[4,64,256]{2,1,0:T(8,128)S(1)} %slice.25), channel_id=1, source_target_pairs={{0,6},{1,7},{2,0},{3,1},{4,2},{5,3},{6,4},{7,5},{8,14},{9,15},{10,... | collective-permute-start | bytes 786440 | tf_op jit(solution)/shard_map/ppermute | solution.py:30
  23.2 1.4 %collective-permute-start.2 = (f32[4,64,256]{2,1,0:T(8,128)S(1)}, f32[4,64,256]{2,1,0:T(8,128)S(1)}, u32[]{:S(2)}, u32[]{:S(2)}) collective-permute-start(f32[4,64,256]{2,1,0:T(8,128)S(1)} %slice.24), channel_id=1, source_target_pairs={{0,2},{1,3},{2,4},{3,5},{4,6},{5,7},{6,0},{7,1},{8,10},{9,11},{10,... | collective-permute-start | bytes 786440 | tf_op jit(solution)/shard_map/ppermute | solution.py:30
  24.7 3.8 %collective-permute-start.9 = (f32[4,64,256]{2,1,0:T(8,128)S(1)}, f32[4,64,256]{2,1,0:T(8,128)S(1)}, u32[]{:S(2)}, u32[]{:S(2)}) collective-permute-start(f32[4,64,256]{2,1,0:T(8,128)S(1)} %slice.27), channel_id=1, source_target_pairs={{0,48},{1,49},{2,50},{3,51},{4,52},{5,53},{6,54},{7,55},{8,56},{9,... | collective-permute-start | bytes 786440 | tf_op jit(solution)/shard_map/ppermute | solution.py:30
  29.2 1.8 %collective-permute-done.2.refs_3_ = f32[4,64,256]{2,1,0:T(8,128)S(1)} collective-permute-done((f32[4,64,256]{2,1,0:T(8,128)S(1)}, f32[4,64,256]{2,1,0:T(8,128)S(1)}, u32[]{:S(2)}, u32[]{:S(2)}) %collective-permute-start.2) | collective-permute-done | bytes 262176 | tf_op jit(solution)/shard_map/ppermute | solution.py:30
  32.3 3.8 %collective-permute-start.15 = (f32[8,64,256]{2,1,0:T(8,128)}, f32[8,64,256]{2,1,0:T(8,128)}, u32[]{:S(2)}, u32[]{:S(2)}) collective-permute-start(f32[8,64,256]{2,1,0:T(8,128)} %collective-permute-done.10.refs_5_), channel_id=1, source_target_pairs={{0,48},{1,49},{2,50},{3,51},{4,52},{5,53},{6,54},{7,55},{8,56},{9,... | collective-permute-start | bytes 1572872 | tf_op jit(solution)/shard_map/ppermute | solution.py:30
  37.8 1.1 collective-permute-done.12.refs_5_
  39.7 1.4 %collective-permute-start.16 = (f32[8,64,256]{2,1,0:T(8,128)}, f32[8,64,256]{2,1,0:T(8,128)}, u32[]{:S(2)}, u32[]{:S(2)}) collective-permute-start(f32[8,64,256]{2,1,0:T(8,128)} %pad_maximum_fusion.2), channel_id=1, source_target_pairs={{0,64},{1,65},{2,66},{3,67},{4,68},{5,69},{6,70},{7,71},{8,72},{9,... | collective-permute-start | bytes 1572872 | tf_op jit(solution)/shard_map/ppermute | solution.py:30
  42.3 2.0 %shard_map.46 = (bf16[5,512,256]{2,1,0:T(8,128)(2,1)S(1)}, bf16[5,512,256]{2,1,0:T(8,128)(2,1)S(1)}) custom-call(s32[64,16]{1,0:T(8,128)S(1)} %multiply_add_fusion.code_ref, f32[8,64,256]{2,1,0:T(8,128)S(1)} %copy-done, f32[8,64,256]{2,1,0:T(8,128)S(1)} %collective-permute-done.refs_1_, f32[8,64,256]{2,1,0:T(8,128)S(1)} %collective-permute-done.1.refs_2_, ...), custom_call_target="tpu_custom_call" | custom-call | bytes 6000000 | tf_op jit(solution)/shard_map/pallas_call | solution.py:211
  44.3 2.0 %shard_map.47 = (bf16[5,256,512]{2,1,0:T(8,128)(2,1)S(1)}, bf16[5,256,512]{2,1,0:T(8,128)(2,1)S(1)}) custom-call(s32[64,16]{1,0:T(8,128)S(1)} %multiply_add_fusion.code_ref, f32[8,64,256]{2,1,0:T(8,128)S(1)} %pad_maximum_fusion.refs_0_, f32[8,64,256]{2,1,0:T(8,128)S(1)} %collective-permute-done.6.refs_1_, f32[8,64,256]{2,1,0:T(8,128)S(1)} %collective-permute-done.7.refs_2_, ...), custom_call_target="tpu_custom_call" | custom-call | bytes 6000000 | tf_op jit(solution)/shard_map/pallas_call | solution.py:211
  46.4 1.2 %collective-permute-done.14.refs_7_ = f32[8,64,256]{2,1,0:T(8,128)} collective-permute-done((f32[8,64,256]{2,1,0:T(8,128)}, f32[8,64,256]{2,1,0:T(8,128)}, u32[]{:S(2)}, u32[]{:S(2)}) %collective-permute-start.14) | collective-permute-done | bytes 524320 | tf_op jit(solution)/shard_map/ppermute | solution.py:30
  47.6 9.0 %collective-permute-done.16.refs_9_ = f32[8,64,256]{2,1,0:T(8,128)} collective-permute-done((f32[8,64,256]{2,1,0:T(8,128)}, f32[8,64,256]{2,1,0:T(8,128)}, u32[]{:S(2)}, u32[]{:S(2)}) %collective-permute-start.16) | collective-permute-done | bytes 524320 | tf_op jit(solution)/shard_map/ppermute | solution.py:30
  56.6 7.5 %shard_map.48 = (f32[8,64,256]{2,1,0:T(8,128)S(1)}, f32[8,64,256]{2,1,0:T(8,128)S(1)}, bf16[8,512,256]{2,1,0:T(8,128)(2,1)S(1)}, bf16[8,512,256]{2,1,0:T(8,128)(2,1)S(1)}) custom-call(s32[64,16]{1,0:T(8,128)S(1)} %multiply_add_fusion.code_ref, bf16[5,512,256]{2,1,0:T(8,128)(2,1)S(1)} %get-tuple-element.15.refs_0_, ...), custom_call_target="tpu_custom_call" | custom-call | bytes 27000000 | tf_op jit(solution)/shard_map/pallas_call | solution.py:211
  64.1 2.8 %collective-permute-start.17 = (f32[8,64,256]{2,1,0:T(8,128)S(1)}, f32[8,64,256]{2,1,0:T(8,128)S(1)}, u32[]{:S(2)}, u32[]{:S(2)}) collective-permute-start(f32[8,64,256]{2,1,0:T(8,128)S(1)} %get-tuple-element.22), channel_id=1, source_target_pairs={{0,1},{1,0},{2,3},{3,2},{4,5},{5,4},{6,7},{7,6},{8,9},{9,8},{10,11... | collective-permute-start | bytes 1572872 | tf_op jit(solution)/shard_map/ppermute | solution.py:34
  66.8 1.5 %collective-permute-done.17 = f32[8,64,256]{2,1,0:T(8,128)S(1)} collective-permute-done((f32[8,64,256]{2,1,0:T(8,128)S(1)}, f32[8,64,256]{2,1,0:T(8,128)S(1)}, u32[]{:S(2)}, u32[]{:S(2)}) %collective-permute-start.17) | collective-permute-done | bytes 524320 | tf_op jit(solution)/shard_map/ppermute | solution.py:34
  68.4 3.8 %collective-permute-start.23 = (f32[8,64,256]{2,1,0:T(8,128)S(1)}, f32[8,64,256]{2,1,0:T(8,128)S(1)}, u32[]{:S(2)}, u32[]{:S(2)}) collective-permute-start(f32[8,64,256]{2,1,0:T(8,128)S(1)} %add.23.refs_0_), channel_id=1, source_target_pairs={{0,48},{1,49},{2,50},{3,51},{4,52},{5,53},{6,54},{7,55},{8,56},{9,... | collective-permute-start | bytes 1572872 | tf_op jit(solution)/shard_map/ppermute | solution.py:30
  72.7 10.5 %collective-permute-done.23.refs_2_ = f32[8,64,256]{2,1,0:T(8,128)S(1)} collective-permute-done((f32[8,64,256]{2,1,0:T(8,128)S(1)}, f32[8,64,256]{2,1,0:T(8,128)S(1)}, u32[]{:S(2)}, u32[]{:S(2)}) %collective-permute-start.23) | collective-permute-done | bytes 524320 | tf_op jit(solution)/shard_map/ppermute | solution.py:30
  83.2 3.5 %collective-permute-start.24 = (f32[4,64,256]{2,1,0:T(8,128)S(1)}, f32[4,64,256]{2,1,0:T(8,128)S(1)}, u32[]{:S(2)}, u32[]{:S(2)}) collective-permute-start(f32[4,64,256]{2,1,0:T(8,128)S(1)} %slice.29), channel_id=1, source_target_pairs={{0,48},{1,49},{2,50},{3,51},{4,52},{5,53},{6,54},{7,55},{8,56},{9,... | collective-permute-start | bytes 786440 | tf_op jit(solution)/shard_map/ppermute | solution.py:30
  86.8 2.7 %collective-permute-start.20 = (f32[8,64,256]{2,1,0:T(8,128)S(1)}, f32[8,64,256]{2,1,0:T(8,128)S(1)}, u32[]{:S(2)}, u32[]{:S(2)}) collective-permute-start(f32[8,64,256]{2,1,0:T(8,128)S(1)} %collective-permute-done.18.refs_5_), channel_id=1, source_target_pairs={{0,48},{1,49},{2,50},{3,51},{4,52},{5,53},{6,54},{7,55},{8,56},{9,... | collective-permute-start | bytes 1572872 | tf_op jit(solution)/shard_map/ppermute | solution.py:30
  89.5 1.6 %collective-permute-done.24.refs_4_ = f32[4,64,256]{2,1,0:T(8,128)S(1)} collective-permute-done((f32[4,64,256]{2,1,0:T(8,128)S(1)}, f32[4,64,256]{2,1,0:T(8,128)S(1)}, u32[]{:S(2)}, u32[]{:S(2)}) %collective-permute-start.24) | collective-permute-done | bytes 262176 | tf_op jit(solution)/shard_map/ppermute | solution.py:30
  91.1 3.2 %collective-permute-done.22.refs_3_ = f32[4,64,256]{2,1,0:T(8,128)S(1)} collective-permute-done((f32[4,64,256]{2,1,0:T(8,128)S(1)}, f32[4,64,256]{2,1,0:T(8,128)S(1)}, u32[]{:S(2)}, u32[]{:S(2)}) %collective-permute-start.22) | collective-permute-done | bytes 262176 | tf_op jit(solution)/shard_map/ppermute | solution.py:30
  95.1 4.5 %shard_map.49.refs_3_ = f32[512,512]{1,0:T(8,128)S(1)} custom-call(s32[64,16]{1,0:T(8,128)S(1)} %multiply_add_fusion.code_ref, bf16[8,512,256]{2,1,0:T(8,128)(2,1)S(1)} %get-tuple-element.19.far_hi, bf16[8,512,256]{2,1,0:T(8,128)(2,1)S(1)} %get-tuple-element.20.far_lo, f32[8,64,256]{2,1,0:T(8,128)S(1)} %add.23.refs_0_, ...), custom_call_target="tpu_custom_call" | custom-call | bytes 12000000 | tf_op jit(solution)/shard_map/pallas_call | solution.py:211
  99.6 2.7 %collective-permute-done.20.refs_1_ = f32[8,64,256]{2,1,0:T(8,128)S(1)} collective-permute-done((f32[8,64,256]{2,1,0:T(8,128)S(1)}, f32[8,64,256]{2,1,0:T(8,128)S(1)}, u32[]{:S(2)}, u32[]{:S(2)}) %collective-permute-start.20) | collective-permute-done | bytes 524320 | tf_op jit(solution)/shard_map/ppermute | solution.py:30
  102.3 3.2 %collective-permute-done.19.refs_0_ = f32[8,64,256]{2,1,0:T(8,128)S(1)} collective-permute-done((f32[8,64,256]{2,1,0:T(8,128)S(1)}, f32[8,64,256]{2,1,0:T(8,128)S(1)}, u32[]{:S(2)}, u32[]{:S(2)}) %collective-permute-start.19) | collective-permute-done | bytes 524320 | tf_op jit(solution)/shard_map/ppermute | solution.py:30
  105.6 3.5 %shard_map.50 = (f32[8,64,256]{2,1,0:T(8,128)S(1)}, f32[8,64,256]{2,1,0:T(8,128)S(1)}) custom-call(s32[64,16]{1,0:T(8,128)S(1)} %multiply_add_fusion.code_ref, bf16[8,512,256]{2,1,0:T(8,128)(2,1)S(1)} %get-tuple-element.19.far_hi, bf16[8,512,256]{2,1,0:T(8,128)(2,1)S(1)} %get-tuple-element.20.far_lo, f32[8,64,256]{2,1,0:T(8,128)S(1)} %collective-permute-done.19.refs_0_, ...), custom_call_target="tpu_custom_call" | custom-call | bytes 12000000 | tf_op jit(solution)/shard_map/pallas_call | solution.py:211
  109.1 5.0 %collective-permute-start.26 = (f32[8,64,256]{2,1,0:T(8,128)S(1)}, f32[8,64,256]{2,1,0:T(8,128)S(1)}, u32[]{:S(2)}, u32[]{:S(2)}) collective-permute-start(f32[8,64,256]{2,1,0:T(8,128)S(1)} %get-tuple-element.24), channel_id=1, source_target_pairs={{0,1},{1,0},{2,3},{3,2},{4,5},{5,4},{6,7},{7,6},{8,9},{9,8},{10,11... | collective-permute-start | bytes 1572872 | tf_op jit(solution)/shard_map/ppermute | solution.py:34
  114.1 1.5 %collective-permute-done.26 = f32[8,64,256]{2,1,0:T(8,128)S(1)} collective-permute-done((f32[8,64,256]{2,1,0:T(8,128)S(1)}, f32[8,64,256]{2,1,0:T(8,128)S(1)}, u32[]{:S(2)}, u32[]{:S(2)}) %collective-permute-start.26) | collective-permute-done | bytes 524320 | tf_op jit(solution)/shard_map/ppermute | solution.py:34
  (68 shorter events, 9.2 us)
Async XLA Ops:
  1.1 5.4 %collective-permute-start.5 = (f32[4,64,256]{2,1,0:T(8,128)S(1)}, f32[4,64,256]{2,1,0:T(8,128)S(1)}, u32[]{:S(2)}, u32[]{:S(2)}) collective-permute-start(f32[4,64,256]{2,1,0:T(8,128)S(1)} %get-tuple-element.26), channel_id=1, source_target_pairs={{0,1},{1,0},{2,3},{3,2},{4,5},{5,4},{6,7},{7,6},{8,9},{9,8},{10,11... | collective-permute-start | bytes 786440 | tf_op jit(solution)/shard_map/ppermute | solution.py:34
  2.6 14.2 %collective-permute-start.1 = (f32[8,64,256]{2,1,0:T(8,128)}, f32[8,64,256]{2,1,0:T(8,128)S(1)}, u32[]{:S(2)}, u32[]{:S(2)}) collective-permute-start(f32[8,64,256]{2,1,0:T(8,128)} %refs_0_.1), channel_id=1, source_target_pairs={{0,6},{1,7},{2,0},{3,1},{4,2},{5,3},{6,4},{7,5},{8,14},{9,15},{10,... | collective-permute-start | bytes 1572872 | tf_op jit(solution)/shard_map/ppermute | solution.py:30
  5.1 14.5 %collective-permute-start.4 = (f32[8,64,256]{2,1,0:T(8,128)}, f32[8,64,256]{2,1,0:T(8,128)}, u32[]{:S(2)}, u32[]{:S(2)}) collective-permute-start(f32[8,64,256]{2,1,0:T(8,128)} %refs_0_.1), channel_id=1, source_target_pairs={{0,8},{1,9},{2,10},{3,11},{4,12},{5,13},{6,14},{7,15},{8,0},{9,1},... | collective-permute-start | bytes 1572872 | tf_op jit(solution)/shard_map/ppermute | solution.py:30
  6.4 16.6 %collective-permute-start = (f32[8,64,256]{2,1,0:T(8,128)}, f32[8,64,256]{2,1,0:T(8,128)S(1)}, u32[]{:S(2)}, u32[]{:S(2)}) collective-permute-start(f32[8,64,256]{2,1,0:T(8,128)} %refs_0_.1), channel_id=1, source_target_pairs={{0,2},{1,3},{2,4},{3,5},{4,6},{5,7},{6,0},{7,1},{8,10},{9,11},{10,... | collective-permute-start | bytes 1572872 | tf_op jit(solution)/shard_map/ppermute | solution.py:30
  6.5 16.7 %collective-permute-start.7 = (f32[8,64,256]{2,1,0:T(8,128)S(1)}, f32[8,64,256]{2,1,0:T(8,128)S(1)}, u32[]{:S(2)}, u32[]{:S(2)}) collective-permute-start(f32[8,64,256]{2,1,0:T(8,128)S(1)} %pad_maximum_fusion.refs_0_), channel_id=1, source_target_pairs={{0,48},{1,49},{2,50},{3,51},{4,52},{5,53},{6,54},{7,55},{8,56},{9,... | collective-permute-start | bytes 1572872 | tf_op jit(solution)/shard_map/ppermute | solution.py:30
  10.3 14.4 %collective-permute-start.6 = (f32[8,64,256]{2,1,0:T(8,128)S(1)}, f32[8,64,256]{2,1,0:T(8,128)S(1)}, u32[]{:S(2)}, u32[]{:S(2)}) collective-permute-start(f32[8,64,256]{2,1,0:T(8,128)S(1)} %pad_maximum_fusion.refs_0_), channel_id=1, source_target_pairs={{0,16},{1,17},{2,18},{3,19},{4,20},{5,21},{6,22},{7,23},{8,24},{9,... | collective-permute-start | bytes 1572872 | tf_op jit(solution)/shard_map/ppermute | solution.py:30
  16.7 15.6 %collective-permute-start.10 = (f32[8,64,256]{2,1,0:T(8,128)S(1)}, f32[8,64,256]{2,1,0:T(8,128)}, u32[]{:S(2)}, u32[]{:S(2)}) collective-permute-start(f32[8,64,256]{2,1,0:T(8,128)S(1)} %pad_maximum_fusion.refs_0_), channel_id=1, source_target_pairs={{0,64},{1,65},{2,66},{3,67},{4,68},{5,69},{6,70},{7,71},{8,72},{9,... | collective-permute-start | bytes 1572872 | tf_op jit(solution)/shard_map/ppermute | solution.py:30
  19.7 8.9 %collective-permute-start.3 = (f32[4,64,256]{2,1,0:T(8,128)S(1)}, f32[4,64,256]{2,1,0:T(8,128)S(1)}, u32[]{:S(2)}, u32[]{:S(2)}) collective-permute-start(f32[4,64,256]{2,1,0:T(8,128)S(1)} %slice.25), channel_id=1, source_target_pairs={{0,6},{1,7},{2,0},{3,1},{4,2},{5,3},{6,4},{7,5},{8,14},{9,15},{10,... | collective-permute-start | bytes 786440 | tf_op jit(solution)/shard_map/ppermute | solution.py:30
  23.1 15.8 %collective-permute-start.12 = (f32[8,64,256]{2,1,0:T(8,128)}, f32[8,64,256]{2,1,0:T(8,128)S(1)}, u32[]{:S(2)}, u32[]{:S(2)}) collective-permute-start(f32[8,64,256]{2,1,0:T(8,128)} %collective-permute-done.4.refs_5_), channel_id=1, source_target_pairs={{0,6},{1,7},{2,0},{3,1},{4,2},{5,3},{6,4},{7,5},{8,14},{9,15},{10,... | collective-permute-start | bytes 1572872 | tf_op jit(solution)/shard_map/ppermute | solution.py:30
  23.2 7.8 %collective-permute-start.2 = (f32[4,64,256]{2,1,0:T(8,128)S(1)}, f32[4,64,256]{2,1,0:T(8,128)S(1)}, u32[]{:S(2)}, u32[]{:S(2)}) collective-permute-start(f32[4,64,256]{2,1,0:T(8,128)S(1)} %slice.24), channel_id=1, source_target_pairs={{0,2},{1,3},{2,4},{3,5},{4,6},{5,7},{6,0},{7,1},{8,10},{9,11},{10,... | collective-permute-start | bytes 786440 | tf_op jit(solution)/shard_map/ppermute | solution.py:30
  24.7 16.4 %copy-start.9 = (s32[64,16,4]{0,2,1:T(4,128)S(1)}, s32[64,16,4]{0,2,1:T(4,128)}, u32[]{:S(2)}) copy-start(s32[64,16,4]{0,2,1:T(4,128)} %param.5) | copy-start | bytes 49156
  24.7 16.4 %copy-start.11 = (s32[4]{0:T(128)S(1)}, s32[4]{0:T(128)}, u32[]{:S(2)}) copy-start(s32[4]{0:T(128)} %constant.27.clone) | copy-start | bytes 52
  24.7 16.5 %copy-start.10 = (s32[64,16]{0,1:T(8,128)S(1)}, s32[64,16]{0,1:T(8,128)}, u32[]{:S(2)}) copy-start(s32[64,16]{0,1:T(8,128)} %param.6) | copy-start | bytes 12292
  24.7 16.6 %copy-start = (f32[8,64,256]{2,1,0:T(8,128)S(1)}, f32[8,64,256]{2,1,0:T(8,128)}, u32[]{:S(2)}) copy-start(f32[8,64,256]{2,1,0:T(8,128)} %refs_0_.1) | copy-start | bytes 1572868
  24.7 7.6 %collective-permute-start.9 = (f32[4,64,256]{2,1,0:T(8,128)S(1)}, f32[4,64,256]{2,1,0:T(8,128)S(1)}, u32[]{:S(2)}, u32[]{:S(2)}) collective-permute-start(f32[4,64,256]{2,1,0:T(8,128)S(1)} %slice.27), channel_id=1, source_target_pairs={{0,48},{1,49},{2,50},{3,51},{4,52},{5,53},{6,54},{7,55},{8,56},{9,... | collective-permute-start | bytes 786440 | tf_op jit(solution)/shard_map/ppermute | solution.py:30
  28.6 7.6 %collective-permute-start.8 = (f32[4,64,256]{2,1,0:T(8,128)S(1)}, f32[4,64,256]{2,1,0:T(8,128)S(1)}, u32[]{:S(2)}, u32[]{:S(2)}) collective-permute-start(f32[4,64,256]{2,1,0:T(8,128)S(1)} %slice.26), channel_id=1, source_target_pairs={{0,16},{1,17},{2,18},{3,19},{4,20},{5,21},{6,22},{7,23},{8,24},{9,... | collective-permute-start | bytes 786440 | tf_op jit(solution)/shard_map/ppermute | solution.py:30
  31.0 15.4 %collective-permute-start.11 = (f32[8,64,256]{2,1,0:T(8,128)}, f32[8,64,256]{2,1,0:T(8,128)}, u32[]{:S(2)}, u32[]{:S(2)}) collective-permute-start(f32[8,64,256]{2,1,0:T(8,128)} %collective-permute-done.4.refs_5_), channel_id=1, source_target_pairs={{0,2},{1,3},{2,4},{3,5},{4,6},{5,7},{6,0},{7,1},{8,10},{9,11},{10,... | collective-permute-start | bytes 1572872 | tf_op jit(solution)/shard_map/ppermute | solution.py:30
  32.3 15.3 %collective-permute-start.13 = (f32[8,64,256]{2,1,0:T(8,128)}, f32[8,64,256]{2,1,0:T(8,128)}, u32[]{:S(2)}, u32[]{:S(2)}) collective-permute-start(f32[8,64,256]{2,1,0:T(8,128)} %pad_maximum_fusion.1), channel_id=1, source_target_pairs={{0,8},{1,9},{2,10},{3,11},{4,12},{5,13},{6,14},{7,15},{8,0},{9,1},... | collective-permute-start | bytes 1572872 | tf_op jit(solution)/shard_map/ppermute | solution.py:30
  32.3 14.0 %collective-permute-start.15 = (f32[8,64,256]{2,1,0:T(8,128)}, f32[8,64,256]{2,1,0:T(8,128)}, u32[]{:S(2)}, u32[]{:S(2)}) collective-permute-start(f32[8,64,256]{2,1,0:T(8,128)} %collective-permute-done.10.refs_5_), channel_id=1, source_target_pairs={{0,48},{1,49},{2,50},{3,51},{4,52},{5,53},{6,54},{7,55},{8,56},{9,... | collective-permute-start | bytes 1572872 | tf_op jit(solution)/shard_map/ppermute | solution.py:30
  36.2 11.5 %collective-permute-start.14 = (f32[8,64,256]{2,1,0:T(8,128)}, f32[8,64,256]{2,1,0:T(8,128)}, u32[]{:S(2)}, u32[]{:S(2)}) collective-permute-start(f32[8,64,256]{2,1,0:T(8,128)} %collective-permute-done.10.refs_5_), channel_id=1, source_target_pairs={{0,16},{1,17},{2,18},{3,19},{4,20},{5,21},{6,22},{7,23},{8,24},{9,... | collective-permute-start | bytes 1572872 | tf_op jit(solution)/shard_map/ppermute | solution.py:30
  39.7 16.9 %collective-permute-start.16 = (f32[8,64,256]{2,1,0:T(8,128)}, f32[8,64,256]{2,1,0:T(8,128)}, u32[]{:S(2)}, u32[]{:S(2)}) collective-permute-start(f32[8,64,256]{2,1,0:T(8,128)} %pad_maximum_fusion.2), channel_id=1, source_target_pairs={{0,64},{1,65},{2,66},{3,67},{4,68},{5,69},{6,70},{7,71},{8,72},{9,... | collective-permute-start | bytes 1572872 | tf_op jit(solution)/shard_map/ppermute | solution.py:30
  44.3 12.3 %copy-start.8 = (f32[8,64,256]{2,1,0:T(8,128)S(1)}, f32[8,64,256]{2,1,0:T(8,128)}, u32[]{:S(2)}) copy-start(f32[8,64,256]{2,1,0:T(8,128)} %copy-done.7) | copy-start | bytes 1572868
  64.1 4.3 %collective-permute-start.17 = (f32[8,64,256]{2,1,0:T(8,128)S(1)}, f32[8,64,256]{2,1,0:T(8,128)S(1)}, u32[]{:S(2)}, u32[]{:S(2)}) collective-permute-start(f32[8,64,256]{2,1,0:T(8,128)S(1)} %get-tuple-element.22), channel_id=1, source_target_pairs={{0,1},{1,0},{2,3},{3,2},{4,5},{5,4},{6,7},{7,6},{8,9},{9,8},{10,11... | collective-permute-start | bytes 1572872 | tf_op jit(solution)/shard_map/ppermute | solution.py:34
  68.4 14.8 %collective-permute-start.23 = (f32[8,64,256]{2,1,0:T(8,128)S(1)}, f32[8,64,256]{2,1,0:T(8,128)S(1)}, u32[]{:S(2)}, u32[]{:S(2)}) collective-permute-start(f32[8,64,256]{2,1,0:T(8,128)S(1)} %add.23.refs_0_), channel_id=1, source_target_pairs={{0,48},{1,49},{2,50},{3,51},{4,52},{5,53},{6,54},{7,55},{8,56},{9,... | collective-permute-start | bytes 1572872 | tf_op jit(solution)/shard_map/ppermute | solution.py:30
  72.3 14.4 %collective-permute-start.21 = (f32[8,64,256]{2,1,0:T(8,128)S(1)}, f32[8,64,256]{2,1,0:T(8,128)S(1)}, u32[]{:S(2)}, u32[]{:S(2)}) collective-permute-start(f32[8,64,256]{2,1,0:T(8,128)S(1)} %add.23.refs_0_), channel_id=1, source_target_pairs={{0,16},{1,17},{2,18},{3,19},{4,20},{5,21},{6,22},{7,23},{8,24},{9,... | collective-permute-start | bytes 1572872 | tf_op jit(solution)/shard_map/ppermute | solution.py:30
  72.3 14.5 %collective-permute-start.18 = (f32[8,64,256]{2,1,0:T(8,128)S(1)}, f32[8,64,256]{2,1,0:T(8,128)S(1)}, u32[]{:S(2)}, u32[]{:S(2)}) collective-permute-start(f32[8,64,256]{2,1,0:T(8,128)S(1)} %add.23.refs_0_), channel_id=1, source_target_pairs={{0,64},{1,65},{2,66},{3,67},{4,68},{5,69},{6,70},{7,71},{8,72},{9,... | collective-permute-start | bytes 1572872 | tf_op jit(solution)/shard_map/ppermute | solution.py:30
  83.2 7.9 %collective-permute-start.24 = (f32[4,64,256]{2,1,0:T(8,128)S(1)}, f32[4,64,256]{2,1,0:T(8,128)S(1)}, u32[]{:S(2)}, u32[]{:S(2)}) collective-permute-start(f32[4,64,256]{2,1,0:T(8,128)S(1)} %slice.29), channel_id=1, source_target_pairs={{0,48},{1,49},{2,50},{3,51},{4,52},{5,53},{6,54},{7,55},{8,56},{9,... | collective-permute-start | bytes 786440 | tf_op jit(solution)/shard_map/ppermute | solution.py:30
  86.7 7.6 %collective-permute-start.22 = (f32[4,64,256]{2,1,0:T(8,128)S(1)}, f32[4,64,256]{2,1,0:T(8,128)S(1)}, u32[]{:S(2)}, u32[]{:S(2)}) collective-permute-start(f32[4,64,256]{2,1,0:T(8,128)S(1)} %slice.28), channel_id=1, source_target_pairs={{0,16},{1,17},{2,18},{3,19},{4,20},{5,21},{6,22},{7,23},{8,24},{9,... | collective-permute-start | bytes 786440 | tf_op jit(solution)/shard_map/ppermute | solution.py:30
  86.8 15.5 %collective-permute-start.20 = (f32[8,64,256]{2,1,0:T(8,128)S(1)}, f32[8,64,256]{2,1,0:T(8,128)S(1)}, u32[]{:S(2)}, u32[]{:S(2)}) collective-permute-start(f32[8,64,256]{2,1,0:T(8,128)S(1)} %collective-permute-done.18.refs_5_), channel_id=1, source_target_pairs={{0,48},{1,49},{2,50},{3,51},{4,52},{5,53},{6,54},{7,55},{8,56},{9,... | collective-permute-start | bytes 1572872 | tf_op jit(solution)/shard_map/ppermute | solution.py:30
  89.5 16.1 %collective-permute-start.19 = (f32[8,64,256]{2,1,0:T(8,128)S(1)}, f32[8,64,256]{2,1,0:T(8,128)S(1)}, u32[]{:S(2)}, u32[]{:S(2)}) collective-permute-start(f32[8,64,256]{2,1,0:T(8,128)S(1)} %collective-permute-done.18.refs_5_), channel_id=1, source_target_pairs={{0,16},{1,17},{2,18},{3,19},{4,20},{5,21},{6,22},{7,23},{8,24},{9,... | collective-permute-start | bytes 1572872 | tf_op jit(solution)/shard_map/ppermute | solution.py:30
  94.4 11.2 %collective-permute-start.25 = (f32[8,64,256]{2,1,0:T(8,128)S(1)}, f32[8,64,256]{2,1,0:T(8,128)S(1)}, u32[]{:S(2)}, u32[]{:S(2)}) collective-permute-start(f32[8,64,256]{2,1,0:T(8,128)S(1)} %pad_maximum_fusion.3), channel_id=1, source_target_pairs={{0,64},{1,65},{2,66},{3,67},{4,68},{5,69},{6,70},{7,71},{8,72},{9,... | collective-permute-start | bytes 1572872 | tf_op jit(solution)/shard_map/ppermute | solution.py:30
  109.1 6.6 %collective-permute-start.26 = (f32[8,64,256]{2,1,0:T(8,128)S(1)}, f32[8,64,256]{2,1,0:T(8,128)S(1)}, u32[]{:S(2)}, u32[]{:S(2)}) collective-permute-start(f32[8,64,256]{2,1,0:T(8,128)S(1)} %get-tuple-element.24), channel_id=1, source_target_pairs={{0,1},{1,0},{2,3},{3,2},{4,5},{5,4},{6,7},{7,6},{8,9},{9,8},{10,11... | collective-permute-start | bytes 1572872 | tf_op jit(solution)/shard_map/ppermute | solution.py:34
  (7 other events, 8.8 us)

commit v4 on v3

--- a/solution.py
+++ b/solution.py
@@ -9,7 +9,7 @@
 HALF = ROWS // 2
 BS = 64
 RING = 4
-KINDS = ("M", "M", "M")
+KINDS = ("M", "M", "F")
 TIE = False
 SIDES = 8
 VMEM = pl.BlockSpec(memory_space=pltpu.VMEM)
@@ -230,34 +230,42 @@
     return call(kernel, [code, *arrays], [SMEM] + [VMEM] * len(arrays), outs, [VMEM] * 2, [], 8, 2)
 
 
-def square(code, early, dense, left_shards, right_shards):
-    left_arrays, left_plan = flatten(left_shards)
+def square(code, left_shards, left_dense, right_early, right_dense, right_shards):
     right_arrays, right_plan = flatten(right_shards)
-    n_left = len(left_arrays)
-    n_in = n_left + len(right_arrays)
-    places = [(flip, shift) for _, flip, shift in early]
+    n_left, n_right = 2 * len(left_dense), len(right_arrays)
+    places = [(n, k, flip, shift) for n, part in enumerate(left_shards) for k, (_, flip, shift) in enumerate(part)]
 
     def kernel(code_ref, *refs):
-        near, refs = refs[:4], refs[4:]
-        left_refs, right_refs, refs = refs[:n_left], refs[n_left:n_in], refs[n_in:]
+        lefts, refs = refs[:n_left], refs[n_left:]
+        early, refs = refs[:2], refs[2:]
+        right_refs, refs = refs[:n_right], refs[n_right:]
         keep_ref, send_ref, *stored = refs[:4]
-        *sides, total, load_sems, store_sems = refs[4:]
+        right_hi, right_lo, total, load_sems, store_sems = refs[4:]
         row, chip, core = position()
         loads = []
-        for n, (there, here) in enumerate(zip(near, sides)):
-            for k, (flip, shift) in enumerate(places):
-                at = here.at[source_of(chip if n < 2 else row, flip, shift)]
-                loads.append(pltpu.make_async_copy(there.at[k], at, load_sems.at[n * len(places) + k]))
-        for m in loads:
+        for k, (_, flip, shift) in enumerate(right_early):
+            source = source_of(row, flip, shift)
+            for m, here in enumerate((right_hi, right_lo)):
+                loads.append(pltpu.make_async_copy(early[m].at[k], here.at[source], load_sems.at[2 * k + m]))
+        pairs, stores = [], []
+        for at, (n, k, flip, shift) in enumerate(places):
+            source = source_of(chip, flip, shift)
+            pairs.append((lefts[2 * n], lefts[2 * n + 1], k, source))
+            for m in range(2):
+                there = stored[m].at[source]
+                stores.append(pltpu.make_async_copy(lefts[2 * n + m].at[k], there, store_sems.at[2 * at + m]))
+        for m in loads + stores:
             m.start()
-        unpack_left(left_plan, left_refs, code_ref, sides[0], sides[1], True)
-        unpack_right(right_plan, right_refs, code_ref, sides[2], sides[3], True)
+        unpack_right(right_plan, right_refs, code_ref, right_hi, right_lo, True)
         for m in loads:
             m.wait()
-        stores = [pltpu.make_async_copy(sides[n], stored[n], store_sems.at[n]) for n in range(2)]
-        for m in stores:
-            m.start()
-        total[...] = multiply(*sides, SIDES)
+        ones, others = [], []
+        for left_hi, left_lo, k, source in pairs:
+            ones += [left_hi[k], left_lo[k], left_hi[k]]
+            others += [right_hi[source], right_hi[source], right_lo[source]]
+        total[...] = jnp.dot(
+            jnp.concatenate(ones, axis=1), jnp.concatenate(others, axis=0), preferred_element_type=F32
+        )
         for part in range(2):
             for n in range(HALF):
                 collect(total, code_ref, part, HALF * core + n, from_three, keep_ref, HALF * part + n)
@@ -270,19 +278,18 @@
     left = jax.ShapeDtypeStruct(left_shape(SIDES), BF16)
     return call(
         kernel,
-        [code, *dense, *left_arrays, *right_arrays],
-        [SMEM] + [ANYWHERE] * 4 + [VMEM] * n_in,
+        [code, *[a for pair in left_dense for a in pair], *right_dense, *right_arrays],
+        [SMEM] + [VMEM] * (n_left + 2 + n_right),
         [SLOTS, SLOTS, left, left],
         [VMEM, VMEM, ANYWHERE, ANYWHERE],
         [
-            *[pltpu.VMEM(left_shape(SIDES), BF16)] * 2,
             *[pltpu.VMEM(right_shape(SIDES), BF16)] * 2,
             pltpu.VMEM((ROWS * BS, 512), F32),
-            pltpu.SemaphoreType.DMA((4 * len(places),)),
-            pltpu.SemaphoreType.DMA((2,)),
+            pltpu.SemaphoreType.DMA((2 * len(right_early),)),
+            pltpu.SemaphoreType.DMA((2 * len(places),)),
         ],
         20,
-        9,
+        8,
     )
 
 
@@ -344,7 +351,10 @@
     halves = jnp.concatenate([keep, other_core(send)], axis=0)
     left_early, left_dense, left_late = gather(matrix, True, KINDS[0], lambda x: make_dense(code, True, x))
     right_early, right_dense, right_late = gather(halves, False, KINDS[1], lambda x: make_dense(code, False, x))
-    keep, send, *left = square(code, left_early, left_dense + right_dense, left_late, right_late)
+    left_last = make_dense(code, True, left_late)
+    keep, send, *left = square(
+        code, [left_early, left_late], [left_dense, left_last], right_early, right_dense, right_late
+    )
 
     early, _, late = gather(keep + other_core(send), False, KINDS[2])
     part = times(code, left, early)[0]

time: 117 us -> 113 us (0.966)
  starting transfers between devices: 45.6 us -> 43.2 us
  waiting for transfers between devices: 44.4 us -> 42.5 us
    ppermute x3, starting transfers between devices: 9.28 us -> 6.74 us  [other_core(): return lax.ppermute(value, 'col', [(c, c ^ 1) for c in range(2 * SIDES)])]
    ppermute x24 -> x25, waiting for transfers between devices: 41.3 us -> 39.4 us  [move(): return lax.ppermute(value, ('row', 'col'), pairs)]
    pallas_call x5 -> x6, Pallas kernels: 19.5 us -> 20.3 us  [call(): pl.pallas_call(kernel, out_shape=outs, in_specs=in_specs, out_specs=out_s...]
    ppermute x24 -> x25, starting transfers between devices: 36.4 us -> 36.5 us  [move(): return lax.ppermute(value, ('row', 'col'), pairs)]
  transfers between devices with their start and end apart: 27 -> 28, of which waited for: 13 -> 12; matrix products, arithmetic and copies ran while one was open for 2% -> 2% of each run, Pallas kernels for 7% -> 9%
where the time goes in v4:
time: 113 us
  starting transfers between devices  43.2 us (38%)
  waiting for transfers between devices  42.5 us (38%)
  Pallas kernels  20.3 us (18%)
  local copies, waits for them, and re-layouts  3.83 us (3%)
  other arithmetic  2.84 us (3%)
    ppermute x25, waiting for transfers between devices, move(): return lax.ppermute(value, ('row', 'col'), pairs)  39.4 us
    ppermute x25, starting transfers between devices, move(): return lax.ppermute(value, ('row', 'col'), pairs)  36.5 us
    pallas_call x6, Pallas kernels, call(): pl.pallas_call(kernel, out_shape=outs, in_specs=in_specs, out_specs=out_s...  20.3 us
    ppermute x3, starting transfers between devices, other_core(): return lax.ppermute(value, 'col', [(c, c ^ 1) for c in range(2 * SIDES)])  6.74 us
    ppermute x3, waiting for transfers between devices, other_core(): return lax.ppermute(value, 'col', [(c, c ^ 1) for c in range(2 * SIDES)])  3.08 us
    unnamed x25, local copies, waits for them, and re-layouts  2.57 us
  transfers between devices with their start and end apart: 28, of which 12 were waited for; matrix products, arithmetic and copies ran while one was open for 2% of the time, Pallas kernels for 9%

profile of v4, /device:TPU:1, one launch (start us, length us, event | category | flops | bytes accessed | tf_op | source)
XLA Modules:
  0.0 113.0 jit_solution(3199561783368792500)
XLA Ops:
  1.1 1.5 %collective-permute-start.8 = (f32[4,64,256]{2,1,0:T(8,128)S(1)}, f32[4,64,256]{2,1,0:T(8,128)S(1)}, u32[]{:S(2)}, u32[]{:S(2)}) collective-permute-start(f32[4,64,256]{2,1,0:T(8,128)S(1)} %get-tuple-element.30), channel_id=1, source_target_pairs={{0,1},{1,0},{2,3},{3,2},{4,5},{5,4},{6,7},{7,6},{8,9},{9,8},{10,11... | collective-permute-start | bytes 786440 | tf_op jit(solution)/shard_map/ppermute | solution.py:34
  2.6 2.6 %collective-permute-start.1 = (f32[8,64,256]{2,1,0:T(8,128)}, f32[8,64,256]{2,1,0:T(8,128)S(1)}, u32[]{:S(2)}, u32[]{:S(2)}) collective-permute-start(f32[8,64,256]{2,1,0:T(8,128)} %refs_0_.1), channel_id=1, source_target_pairs={{0,6},{1,7},{2,0},{3,1},{4,2},{5,3},{6,4},{7,5},{8,14},{9,15},{10,... | collective-permute-start | bytes 1572872 | tf_op jit(solution)/shard_map/ppermute | solution.py:30
  5.1 1.3 %collective-permute-start.4 = (f32[8,64,256]{2,1,0:T(8,128)}, f32[8,64,256]{2,1,0:T(8,128)}, u32[]{:S(2)}, u32[]{:S(2)}) collective-permute-start(f32[8,64,256]{2,1,0:T(8,128)} %refs_0_.1), channel_id=1, source_target_pairs={{0,8},{1,9},{2,10},{3,11},{4,12},{5,13},{6,14},{7,15},{8,0},{9,1},... | collective-permute-start | bytes 1572872 | tf_op jit(solution)/shard_map/ppermute | solution.py:30
  6.5 3.8 %collective-permute-start.10 = (f32[8,64,256]{2,1,0:T(8,128)S(1)}, f32[8,64,256]{2,1,0:T(8,128)S(1)}, u32[]{:S(2)}, u32[]{:S(2)}) collective-permute-start(f32[8,64,256]{2,1,0:T(8,128)S(1)} %pad_maximum_fusion.1.refs_0_), channel_id=1, source_target_pairs={{0,48},{1,49},{2,50},{3,51},{4,52},{5,53},{6,54},{7,55},{8,56},{9,... | collective-permute-start | bytes 1572872 | tf_op jit(solution)/shard_map/ppermute | solution.py:30
  10.3 6.4 %collective-permute-done.1.refs_2_ = f32[8,64,256]{2,1,0:T(8,128)S(1)} collective-permute-done((f32[8,64,256]{2,1,0:T(8,128)}, f32[8,64,256]{2,1,0:T(8,128)S(1)}, u32[]{:S(2)}, u32[]{:S(2)}) %collective-permute-start.1) | collective-permute-done | bytes 524320 | tf_op jit(solution)/shard_map/ppermute | solution.py:30
  16.7 2.9 %collective-permute-start.13 = (f32[8,64,256]{2,1,0:T(8,128)S(1)}, f32[8,64,256]{2,1,0:T(8,128)}, u32[]{:S(2)}, u32[]{:S(2)}) collective-permute-start(f32[8,64,256]{2,1,0:T(8,128)S(1)} %pad_maximum_fusion.1.refs_0_), channel_id=1, source_target_pairs={{0,64},{1,65},{2,66},{3,67},{4,68},{5,69},{6,70},{7,71},{8,72},{9,... | collective-permute-start | bytes 1572872 | tf_op jit(solution)/shard_map/ppermute | solution.py:30
  19.7 3.4 %collective-permute-start.3 = (f32[4,64,256]{2,1,0:T(8,128)S(1)}, f32[4,64,256]{2,1,0:T(8,128)S(1)}, u32[]{:S(2)}, u32[]{:S(2)}) collective-permute-start(f32[4,64,256]{2,1,0:T(8,128)S(1)} %slice.25), channel_id=1, source_target_pairs={{0,6},{1,7},{2,0},{3,1},{4,2},{5,3},{6,4},{7,5},{8,14},{9,15},{10,... | collective-permute-start | bytes 786440 | tf_op jit(solution)/shard_map/ppermute | solution.py:30
  23.2 1.4 %collective-permute-start.2 = (f32[4,64,256]{2,1,0:T(8,128)S(1)}, f32[4,64,256]{2,1,0:T(8,128)S(1)}, u32[]{:S(2)}, u32[]{:S(2)}) collective-permute-start(f32[4,64,256]{2,1,0:T(8,128)S(1)} %slice.24), channel_id=1, source_target_pairs={{0,2},{1,3},{2,4},{3,5},{4,6},{5,7},{6,0},{7,1},{8,10},{9,11},{10,... | collective-permute-start | bytes 786440 | tf_op jit(solution)/shard_map/ppermute | solution.py:30
  24.7 3.8 %collective-permute-start.12 = (f32[4,64,256]{2,1,0:T(8,128)S(1)}, f32[4,64,256]{2,1,0:T(8,128)S(1)}, u32[]{:S(2)}, u32[]{:S(2)}) collective-permute-start(f32[4,64,256]{2,1,0:T(8,128)S(1)} %slice.27), channel_id=1, source_target_pairs={{0,48},{1,49},{2,50},{3,51},{4,52},{5,53},{6,54},{7,55},{8,56},{9,... | collective-permute-start | bytes 786440 | tf_op jit(solution)/shard_map/ppermute | solution.py:30
  29.2 1.8 %collective-permute-done.2.refs_3_ = f32[4,64,256]{2,1,0:T(8,128)S(1)} collective-permute-done((f32[4,64,256]{2,1,0:T(8,128)S(1)}, f32[4,64,256]{2,1,0:T(8,128)S(1)}, u32[]{:S(2)}, u32[]{:S(2)}) %collective-permute-start.2) | collective-permute-done | bytes 262176 | tf_op jit(solution)/shard_map/ppermute | solution.py:30
  32.3 3.8 %collective-permute-start.15 = (f32[8,64,256]{2,1,0:T(8,128)}, f32[8,64,256]{2,1,0:T(8,128)}, u32[]{:S(2)}, u32[]{:S(2)}) collective-permute-start(f32[8,64,256]{2,1,0:T(8,128)} %collective-permute-done.13.refs_5_), channel_id=1, source_target_pairs={{0,48},{1,49},{2,50},{3,51},{4,52},{5,53},{6,54},{7,55},{8,56},{9,... | collective-permute-start | bytes 1572872 | tf_op jit(solution)/shard_map/ppermute | solution.py:30
  37.7 1.1 collective-permute-done.6.refs_1_
  39.7 1.4 %collective-permute-start.16 = (f32[8,64,256]{2,1,0:T(8,128)}, f32[8,64,256]{2,1,0:T(8,128)}, u32[]{:S(2)}, u32[]{:S(2)}) collective-permute-start(f32[8,64,256]{2,1,0:T(8,128)} %pad_maximum_fusion.2), channel_id=1, source_target_pairs={{0,64},{1,65},{2,66},{3,67},{4,68},{5,69},{6,70},{7,71},{8,72},{9,... | collective-permute-start | bytes 1572872 | tf_op jit(solution)/shard_map/ppermute | solution.py:30
  42.3 2.0 %shard_map.46 = (bf16[5,512,256]{2,1,0:T(8,128)(2,1)S(1)}, bf16[5,512,256]{2,1,0:T(8,128)(2,1)S(1)}) custom-call(s32[64,16]{1,0:T(8,128)S(1)} %multiply_add_fusion.code_ref, f32[8,64,256]{2,1,0:T(8,128)S(1)} %copy-done, f32[8,64,256]{2,1,0:T(8,128)S(1)} %collective-permute-done.refs_1_, f32[8,64,256]{2,1,0:T(8,128)S(1)} %collective-permute-done.1.refs_2_, ...), custom_call_target="tpu_custom_call" | custom-call | bytes 6000000 | tf_op jit(solution)/shard_map/pallas_call | solution.py:211
  44.3 2.0 %shard_map.48 = (bf16[5,256,512]{2,1,0:T(8,128)(2,1)S(1)}, bf16[5,256,512]{2,1,0:T(8,128)(2,1)S(1)}) custom-call(s32[64,16]{1,0:T(8,128)S(1)} %multiply_add_fusion.code_ref, f32[8,64,256]{2,1,0:T(8,128)S(1)} %pad_maximum_fusion.1.refs_0_, f32[8,64,256]{2,1,0:T(8,128)S(1)} %collective-permute-done.9.refs_1_, ...), custom_call_target="tpu_custom_call" | custom-call | bytes 6000000 | tf_op jit(solution)/shard_map/pallas_call | solution.py:211
  46.4 1.8 %shard_map.47 = (bf16[3,512,256]{2,1,0:T(8,128)(2,1)S(1)}, bf16[3,512,256]{2,1,0:T(8,128)(2,1)S(1)}) custom-call(s32[64,16]{1,0:T(8,128)S(1)} %multiply_add_fusion.code_ref, f32[8,64,256]{2,1,0:T(8,128)} %collective-permute-done.5.refs_0_, f32[8,64,256]{2,1,0:T(8,128)S(1)} %copy-done.8, f32[8,64,256]{2,1,0:T(8,128)} %collective-permute-done.7.refs_2_), custom_call_target="tpu_custom_call" | custom-call | bytes 6000000 | tf_op jit(solution)/shard_map/pallas_call | solution.py:211
  48.2 8.4 %collective-permute-done.16.refs_8_ = f32[8,64,256]{2,1,0:T(8,128)} collective-permute-done((f32[8,64,256]{2,1,0:T(8,128)}, f32[8,64,256]{2,1,0:T(8,128)}, u32[]{:S(2)}, u32[]{:S(2)}) %collective-permute-start.16) | collective-permute-done | bytes 524320 | tf_op jit(solution)/shard_map/ppermute | solution.py:30
  56.6 6.5 %shard_map.49 = (f32[8,64,256]{2,1,0:T(8,128)S(1)}, f32[8,64,256]{2,1,0:T(8,128)S(1)}, bf16[8,512,256]{2,1,0:T(8,128)(2,1)S(1)}, bf16[8,512,256]{2,1,0:T(8,128)(2,1)S(1)}) custom-call(s32[64,16]{1,0:T(8,128)S(1)} %multiply_add_fusion.code_ref, bf16[5,512,256]{2,1,0:T(8,128)(2,1)S(1)} %get-tuple-element.17.refs_0_, ...), custom_call_target="tpu_custom_call" | custom-call | bytes 24000000 | tf_op jit(solution)/shard_map/pallas_call | solution.py:211
  63.1 2.8 %collective-permute-start.17 = (f32[8,64,256]{2,1,0:T(8,128)S(1)}, f32[8,64,256]{2,1,0:T(8,128)S(1)}, u32[]{:S(2)}, u32[]{:S(2)}) collective-permute-start(f32[8,64,256]{2,1,0:T(8,128)S(1)} %get-tuple-element.26), channel_id=1, source_target_pairs={{0,1},{1,0},{2,3},{3,2},{4,5},{5,4},{6,7},{7,6},{8,9},{9,8},{10,11... | collective-permute-start | bytes 1572872 | tf_op jit(solution)/shard_map/ppermute | solution.py:34
  65.9 1.5 %collective-permute-done.17 = f32[8,64,256]{2,1,0:T(8,128)S(1)} collective-permute-done((f32[8,64,256]{2,1,0:T(8,128)S(1)}, f32[8,64,256]{2,1,0:T(8,128)S(1)}, u32[]{:S(2)}, u32[]{:S(2)}) %collective-permute-start.17) | collective-permute-done | bytes 524320 | tf_op jit(solution)/shard_map/ppermute | solution.py:34
  67.5 3.8 %collective-permute-start.24 = (f32[8,64,256]{2,1,0:T(8,128)S(1)}, f32[8,64,256]{2,1,0:T(8,128)S(1)}, u32[]{:S(2)}, u32[]{:S(2)}) collective-permute-start(f32[8,64,256]{2,1,0:T(8,128)S(1)} %add.23.refs_0_), channel_id=1, source_target_pairs={{0,48},{1,49},{2,50},{3,51},{4,52},{5,53},{6,54},{7,55},{8,56},{9,... | collective-permute-start | bytes 1572872 | tf_op jit(solution)/shard_map/ppermute | solution.py:30
  71.8 10.5 %collective-permute-done.24.refs_2_ = f32[8,64,256]{2,1,0:T(8,128)S(1)} collective-permute-done((f32[8,64,256]{2,1,0:T(8,128)S(1)}, f32[8,64,256]{2,1,0:T(8,128)S(1)}, u32[]{:S(2)}, u32[]{:S(2)}) %collective-permute-start.24) | collective-permute-done | bytes 524320 | tf_op jit(solution)/shard_map/ppermute | solution.py:30
  82.3 3.5 %collective-permute-start.25 = (f32[4,64,256]{2,1,0:T(8,128)S(1)}, f32[4,64,256]{2,1,0:T(8,128)S(1)}, u32[]{:S(2)}, u32[]{:S(2)}) collective-permute-start(f32[4,64,256]{2,1,0:T(8,128)S(1)} %slice.29), channel_id=1, source_target_pairs={{0,48},{1,49},{2,50},{3,51},{4,52},{5,53},{6,54},{7,55},{8,56},{9,... | collective-permute-start | bytes 786440 | tf_op jit(solution)/shard_map/ppermute | solution.py:30
  85.9 2.7 %collective-permute-start.20 = (f32[8,64,256]{2,1,0:T(8,128)S(1)}, f32[8,64,256]{2,1,0:T(8,128)S(1)}, u32[]{:S(2)}, u32[]{:S(2)}) collective-permute-start(f32[8,64,256]{2,1,0:T(8,128)S(1)} %collective-permute-done.18.refs_5_), channel_id=1, source_target_pairs={{0,48},{1,49},{2,50},{3,51},{4,52},{5,53},{6,54},{7,55},{8,56},{9,... | collective-permute-start | bytes 1572872 | tf_op jit(solution)/shard_map/ppermute | solution.py:30
  88.5 1.6 %collective-permute-done.25.refs_4_ = f32[4,64,256]{2,1,0:T(8,128)S(1)} collective-permute-done((f32[4,64,256]{2,1,0:T(8,128)S(1)}, f32[4,64,256]{2,1,0:T(8,128)S(1)}, u32[]{:S(2)}, u32[]{:S(2)}) %collective-permute-start.25) | collective-permute-done | bytes 262176 | tf_op jit(solution)/shard_map/ppermute | solution.py:30
  90.6 2.8 %collective-permute-done.22.refs_3_ = f32[4,64,256]{2,1,0:T(8,128)S(1)} collective-permute-done((f32[4,64,256]{2,1,0:T(8,128)S(1)}, f32[4,64,256]{2,1,0:T(8,128)S(1)}, u32[]{:S(2)}, u32[]{:S(2)}) %collective-permute-start.22) | collective-permute-done | bytes 262176 | tf_op jit(solution)/shard_map/ppermute | solution.py:30
  93.8 4.5 %shard_map.50.refs_4_ = f32[512,512]{1,0:T(8,128)S(1)} custom-call(s32[64,16]{1,0:T(8,128)S(1)} %multiply_add_fusion.code_ref, bf16[8,512,256]{2,1,0:T(8,128)(2,1)S(1)} %get-tuple-element.23.far_hi, bf16[8,512,256]{2,1,0:T(8,128)(2,1)S(1)} %get-tuple-element.24.far_lo, f32[8,64,256]{2,1,0:T(8,128)S(1)} %add.23.refs_0_, ...), custom_call_target="tpu_custom_call" | custom-call | bytes 12000000 | tf_op jit(solution)/shard_map/pallas_call | solution.py:211
  98.3 3.8 %collective-permute-done.23.refs_2_ = f32[4,64,256]{2,1,0:T(8,128)S(1)} collective-permute-done((f32[4,64,256]{2,1,0:T(8,128)S(1)}, f32[4,64,256]{2,1,0:T(8,128)S(1)}, u32[]{:S(2)}, u32[]{:S(2)}) %collective-permute-start.23) | collective-permute-done | bytes 262176 | tf_op jit(solution)/shard_map/ppermute | solution.py:30
  102.1 2.5 %collective-permute-done.19.refs_0_ = f32[8,64,256]{2,1,0:T(8,128)S(1)} collective-permute-done((f32[8,64,256]{2,1,0:T(8,128)S(1)}, f32[8,64,256]{2,1,0:T(8,128)S(1)}, u32[]{:S(2)}, u32[]{:S(2)}) %collective-permute-start.19) | collective-permute-done | bytes 524320 | tf_op jit(solution)/shard_map/ppermute | solution.py:30
  104.6 3.5 %shard_map.51 = (f32[8,64,256]{2,1,0:T(8,128)S(1)}, f32[8,64,256]{2,1,0:T(8,128)S(1)}) custom-call(s32[64,16]{1,0:T(8,128)S(1)} %multiply_add_fusion.code_ref, bf16[8,512,256]{2,1,0:T(8,128)(2,1)S(1)} %get-tuple-element.23.far_hi, bf16[8,512,256]{2,1,0:T(8,128)(2,1)S(1)} %get-tuple-element.24.far_lo, f32[8,64,256]{2,1,0:T(8,128)S(1)} %collective-permute-done.19.refs_0_, ...), custom_call_target="tpu_custom_call" | custom-call | bytes 12000000 | tf_op jit(solution)/shard_map/pallas_call | solution.py:211
  108.1 2.5 %collective-permute-start.27 = (f32[8,64,256]{2,1,0:T(8,128)S(1)}, f32[8,64,256]{2,1,0:T(8,128)S(1)}, u32[]{:S(2)}, u32[]{:S(2)}) collective-permute-start(f32[8,64,256]{2,1,0:T(8,128)S(1)} %get-tuple-element.28), channel_id=1, source_target_pairs={{0,1},{1,0},{2,3},{3,2},{4,5},{5,4},{6,7},{7,6},{8,9},{9,8},{10,11... | collective-permute-start | bytes 1572872 | tf_op jit(solution)/shard_map/ppermute | solution.py:34
  110.6 1.5 %collective-permute-done.27 = f32[8,64,256]{2,1,0:T(8,128)S(1)} collective-permute-done((f32[8,64,256]{2,1,0:T(8,128)S(1)}, f32[8,64,256]{2,1,0:T(8,128)S(1)}, u32[]{:S(2)}, u32[]{:S(2)}) %collective-permute-start.27) | collective-permute-done | bytes 524320 | tf_op jit(solution)/shard_map/ppermute | solution.py:34
  (70 shorter events, 9.3 us)
Async XLA Ops:
  1.1 5.4 %collective-permute-start.8 = (f32[4,64,256]{2,1,0:T(8,128)S(1)}, f32[4,64,256]{2,1,0:T(8,128)S(1)}, u32[]{:S(2)}, u32[]{:S(2)}) collective-permute-start(f32[4,64,256]{2,1,0:T(8,128)S(1)} %get-tuple-element.30), channel_id=1, source_target_pairs={{0,1},{1,0},{2,3},{3,2},{4,5},{5,4},{6,7},{7,6},{8,9},{9,8},{10,11... | collective-permute-start | bytes 786440 | tf_op jit(solution)/shard_map/ppermute | solution.py:34
  2.6 14.2 %collective-permute-start.1 = (f32[8,64,256]{2,1,0:T(8,128)}, f32[8,64,256]{2,1,0:T(8,128)S(1)}, u32[]{:S(2)}, u32[]{:S(2)}) collective-permute-start(f32[8,64,256]{2,1,0:T(8,128)} %refs_0_.1), channel_id=1, source_target_pairs={{0,6},{1,7},{2,0},{3,1},{4,2},{5,3},{6,4},{7,5},{8,14},{9,15},{10,... | collective-permute-start | bytes 1572872 | tf_op jit(solution)/shard_map/ppermute | solution.py:30
  5.1 14.5 %collective-permute-start.4 = (f32[8,64,256]{2,1,0:T(8,128)}, f32[8,64,256]{2,1,0:T(8,128)}, u32[]{:S(2)}, u32[]{:S(2)}) collective-permute-start(f32[8,64,256]{2,1,0:T(8,128)} %refs_0_.1), channel_id=1, source_target_pairs={{0,8},{1,9},{2,10},{3,11},{4,12},{5,13},{6,14},{7,15},{8,0},{9,1},... | collective-permute-start | bytes 1572872 | tf_op jit(solution)/shard_map/ppermute | solution.py:30
  6.4 16.6 %collective-permute-start = (f32[8,64,256]{2,1,0:T(8,128)}, f32[8,64,256]{2,1,0:T(8,128)S(1)}, u32[]{:S(2)}, u32[]{:S(2)}) collective-permute-start(f32[8,64,256]{2,1,0:T(8,128)} %refs_0_.1), channel_id=1, source_target_pairs={{0,2},{1,3},{2,4},{3,5},{4,6},{5,7},{6,0},{7,1},{8,10},{9,11},{10,... | collective-permute-start | bytes 1572872 | tf_op jit(solution)/shard_map/ppermute | solution.py:30
  6.5 16.7 %collective-permute-start.10 = (f32[8,64,256]{2,1,0:T(8,128)S(1)}, f32[8,64,256]{2,1,0:T(8,128)S(1)}, u32[]{:S(2)}, u32[]{:S(2)}) collective-permute-start(f32[8,64,256]{2,1,0:T(8,128)S(1)} %pad_maximum_fusion.1.refs_0_), channel_id=1, source_target_pairs={{0,48},{1,49},{2,50},{3,51},{4,52},{5,53},{6,54},{7,55},{8,56},{9,... | collective-permute-start | bytes 1572872 | tf_op jit(solution)/shard_map/ppermute | solution.py:30
  10.3 14.4 %collective-permute-start.9 = (f32[8,64,256]{2,1,0:T(8,128)S(1)}, f32[8,64,256]{2,1,0:T(8,128)S(1)}, u32[]{:S(2)}, u32[]{:S(2)}) collective-permute-start(f32[8,64,256]{2,1,0:T(8,128)S(1)} %pad_maximum_fusion.1.refs_0_), channel_id=1, source_target_pairs={{0,16},{1,17},{2,18},{3,19},{4,20},{5,21},{6,22},{7,23},{8,24},{9,... | collective-permute-start | bytes 1572872 | tf_op jit(solution)/shard_map/ppermute | solution.py:30
  16.7 15.6 %collective-permute-start.13 = (f32[8,64,256]{2,1,0:T(8,128)S(1)}, f32[8,64,256]{2,1,0:T(8,128)}, u32[]{:S(2)}, u32[]{:S(2)}) collective-permute-start(f32[8,64,256]{2,1,0:T(8,128)S(1)} %pad_maximum_fusion.1.refs_0_), channel_id=1, source_target_pairs={{0,64},{1,65},{2,66},{3,67},{4,68},{5,69},{6,70},{7,71},{8,72},{9,... | collective-permute-start | bytes 1572872 | tf_op jit(solution)/shard_map/ppermute | solution.py:30
  19.7 8.9 %collective-permute-start.3 = (f32[4,64,256]{2,1,0:T(8,128)S(1)}, f32[4,64,256]{2,1,0:T(8,128)S(1)}, u32[]{:S(2)}, u32[]{:S(2)}) collective-permute-start(f32[4,64,256]{2,1,0:T(8,128)S(1)} %slice.25), channel_id=1, source_target_pairs={{0,6},{1,7},{2,0},{3,1},{4,2},{5,3},{6,4},{7,5},{8,14},{9,15},{10,... | collective-permute-start | bytes 786440 | tf_op jit(solution)/shard_map/ppermute | solution.py:30
  23.1 15.8 %collective-permute-start.6 = (f32[8,64,256]{2,1,0:T(8,128)}, f32[8,64,256]{2,1,0:T(8,128)S(1)}, u32[]{:S(2)}, u32[]{:S(2)}) collective-permute-start(f32[8,64,256]{2,1,0:T(8,128)} %collective-permute-done.4.refs_5_), channel_id=1, source_target_pairs={{0,6},{1,7},{2,0},{3,1},{4,2},{5,3},{6,4},{7,5},{8,14},{9,15},{10,... | collective-permute-start | bytes 1572872 | tf_op jit(solution)/shard_map/ppermute | solution.py:30
  23.2 7.8 %collective-permute-start.2 = (f32[4,64,256]{2,1,0:T(8,128)S(1)}, f32[4,64,256]{2,1,0:T(8,128)S(1)}, u32[]{:S(2)}, u32[]{:S(2)}) collective-permute-start(f32[4,64,256]{2,1,0:T(8,128)S(1)} %slice.24), channel_id=1, source_target_pairs={{0,2},{1,3},{2,4},{3,5},{4,6},{5,7},{6,0},{7,1},{8,10},{9,11},{10,... | collective-permute-start | bytes 786440 | tf_op jit(solution)/shard_map/ppermute | solution.py:30
  24.7 16.4 %copy-start.9 = (s32[64,16,4]{0,2,1:T(4,128)S(1)}, s32[64,16,4]{0,2,1:T(4,128)}, u32[]{:S(2)}) copy-start(s32[64,16,4]{0,2,1:T(4,128)} %param.5) | copy-start | bytes 49156
  24.7 16.4 %copy-start.11 = (s32[4]{0:T(128)S(1)}, s32[4]{0:T(128)}, u32[]{:S(2)}) copy-start(s32[4]{0:T(128)} %constant.27.clone) | copy-start | bytes 52
  24.7 16.5 %copy-start.10 = (s32[64,16]{0,1:T(8,128)S(1)}, s32[64,16]{0,1:T(8,128)}, u32[]{:S(2)}) copy-start(s32[64,16]{0,1:T(8,128)} %param.6) | copy-start | bytes 12292
  24.7 16.6 %copy-start = (f32[8,64,256]{2,1,0:T(8,128)S(1)}, f32[8,64,256]{2,1,0:T(8,128)}, u32[]{:S(2)}) copy-start(f32[8,64,256]{2,1,0:T(8,128)} %refs_0_.1) | copy-start | bytes 1572868
  24.7 7.6 %collective-permute-start.12 = (f32[4,64,256]{2,1,0:T(8,128)S(1)}, f32[4,64,256]{2,1,0:T(8,128)S(1)}, u32[]{:S(2)}, u32[]{:S(2)}) collective-permute-start(f32[4,64,256]{2,1,0:T(8,128)S(1)} %slice.27), channel_id=1, source_target_pairs={{0,48},{1,49},{2,50},{3,51},{4,52},{5,53},{6,54},{7,55},{8,56},{9,... | collective-permute-start | bytes 786440 | tf_op jit(solution)/shard_map/ppermute | solution.py:30
  28.6 7.6 %collective-permute-start.11 = (f32[4,64,256]{2,1,0:T(8,128)S(1)}, f32[4,64,256]{2,1,0:T(8,128)S(1)}, u32[]{:S(2)}, u32[]{:S(2)}) collective-permute-start(f32[4,64,256]{2,1,0:T(8,128)S(1)} %slice.26), channel_id=1, source_target_pairs={{0,16},{1,17},{2,18},{3,19},{4,20},{5,21},{6,22},{7,23},{8,24},{9,... | collective-permute-start | bytes 786440 | tf_op jit(solution)/shard_map/ppermute | solution.py:30
  31.0 15.4 %collective-permute-start.5 = (f32[8,64,256]{2,1,0:T(8,128)}, f32[8,64,256]{2,1,0:T(8,128)}, u32[]{:S(2)}, u32[]{:S(2)}) collective-permute-start(f32[8,64,256]{2,1,0:T(8,128)} %collective-permute-done.4.refs_5_), channel_id=1, source_target_pairs={{0,2},{1,3},{2,4},{3,5},{4,6},{5,7},{6,0},{7,1},{8,10},{9,11},{10,... | collective-permute-start | bytes 1572872 | tf_op jit(solution)/shard_map/ppermute | solution.py:30
  32.3 14.0 %collective-permute-start.7 = (f32[8,64,256]{2,1,0:T(8,128)}, f32[8,64,256]{2,1,0:T(8,128)}, u32[]{:S(2)}, u32[]{:S(2)}) collective-permute-start(f32[8,64,256]{2,1,0:T(8,128)} %pad_maximum_fusion), channel_id=1, source_target_pairs={{0,8},{1,9},{2,10},{3,11},{4,12},{5,13},{6,14},{7,15},{8,0},{9,1},... | collective-permute-start | bytes 1572872 | tf_op jit(solution)/shard_map/ppermute | solution.py:30
  32.3 15.8 %collective-permute-start.15 = (f32[8,64,256]{2,1,0:T(8,128)}, f32[8,64,256]{2,1,0:T(8,128)}, u32[]{:S(2)}, u32[]{:S(2)}) collective-permute-start(f32[8,64,256]{2,1,0:T(8,128)} %collective-permute-done.13.refs_5_), channel_id=1, source_target_pairs={{0,48},{1,49},{2,50},{3,51},{4,52},{5,53},{6,54},{7,55},{8,56},{9,... | collective-permute-start | bytes 1572872 | tf_op jit(solution)/shard_map/ppermute | solution.py:30
  36.2 12.0 %collective-permute-start.14 = (f32[8,64,256]{2,1,0:T(8,128)}, f32[8,64,256]{2,1,0:T(8,128)}, u32[]{:S(2)}, u32[]{:S(2)}) collective-permute-start(f32[8,64,256]{2,1,0:T(8,128)} %collective-permute-done.13.refs_5_), channel_id=1, source_target_pairs={{0,16},{1,17},{2,18},{3,19},{4,20},{5,21},{6,22},{7,23},{8,24},{9,... | collective-permute-start | bytes 1572872 | tf_op jit(solution)/shard_map/ppermute | solution.py:30
  39.7 16.9 %collective-permute-start.16 = (f32[8,64,256]{2,1,0:T(8,128)}, f32[8,64,256]{2,1,0:T(8,128)}, u32[]{:S(2)}, u32[]{:S(2)}) collective-permute-start(f32[8,64,256]{2,1,0:T(8,128)} %pad_maximum_fusion.2), channel_id=1, source_target_pairs={{0,64},{1,65},{2,66},{3,67},{4,68},{5,69},{6,70},{7,71},{8,72},{9,... | collective-permute-start | bytes 1572872 | tf_op jit(solution)/shard_map/ppermute | solution.py:30
  63.1 4.3 %collective-permute-start.17 = (f32[8,64,256]{2,1,0:T(8,128)S(1)}, f32[8,64,256]{2,1,0:T(8,128)S(1)}, u32[]{:S(2)}, u32[]{:S(2)}) collective-permute-start(f32[8,64,256]{2,1,0:T(8,128)S(1)} %get-tuple-element.26), channel_id=1, source_target_pairs={{0,1},{1,0},{2,3},{3,2},{4,5},{5,4},{6,7},{7,6},{8,9},{9,8},{10,11... | collective-permute-start | bytes 1572872 | tf_op jit(solution)/shard_map/ppermute | solution.py:34
  67.5 14.8 %collective-permute-start.24 = (f32[8,64,256]{2,1,0:T(8,128)S(1)}, f32[8,64,256]{2,1,0:T(8,128)S(1)}, u32[]{:S(2)}, u32[]{:S(2)}) collective-permute-start(f32[8,64,256]{2,1,0:T(8,128)S(1)} %add.23.refs_0_), channel_id=1, source_target_pairs={{0,48},{1,49},{2,50},{3,51},{4,52},{5,53},{6,54},{7,55},{8,56},{9,... | collective-permute-start | bytes 1572872 | tf_op jit(solution)/shard_map/ppermute | solution.py:30
  71.3 14.4 %collective-permute-start.21 = (f32[8,64,256]{2,1,0:T(8,128)S(1)}, f32[8,64,256]{2,1,0:T(8,128)S(1)}, u32[]{:S(2)}, u32[]{:S(2)}) collective-permute-start(f32[8,64,256]{2,1,0:T(8,128)S(1)} %add.23.refs_0_), channel_id=1, source_target_pairs={{0,16},{1,17},{2,18},{3,19},{4,20},{5,21},{6,22},{7,23},{8,24},{9,... | collective-permute-start | bytes 1572872 | tf_op jit(solution)/shard_map/ppermute | solution.py:30
  71.3 14.5 %collective-permute-start.18 = (f32[8,64,256]{2,1,0:T(8,128)S(1)}, f32[8,64,256]{2,1,0:T(8,128)S(1)}, u32[]{:S(2)}, u32[]{:S(2)}) collective-permute-start(f32[8,64,256]{2,1,0:T(8,128)S(1)} %add.23.refs_0_), channel_id=1, source_target_pairs={{0,64},{1,65},{2,66},{3,67},{4,68},{5,69},{6,70},{7,71},{8,72},{9,... | collective-permute-start | bytes 1572872 | tf_op jit(solution)/shard_map/ppermute | solution.py:30
  82.3 7.9 %collective-permute-start.25 = (f32[4,64,256]{2,1,0:T(8,128)S(1)}, f32[4,64,256]{2,1,0:T(8,128)S(1)}, u32[]{:S(2)}, u32[]{:S(2)}) collective-permute-start(f32[4,64,256]{2,1,0:T(8,128)S(1)} %slice.29), channel_id=1, source_target_pairs={{0,48},{1,49},{2,50},{3,51},{4,52},{5,53},{6,54},{7,55},{8,56},{9,... | collective-permute-start | bytes 786440 | tf_op jit(solution)/shard_map/ppermute | solution.py:30
  85.8 7.6 %collective-permute-start.22 = (f32[4,64,256]{2,1,0:T(8,128)S(1)}, f32[4,64,256]{2,1,0:T(8,128)S(1)}, u32[]{:S(2)}, u32[]{:S(2)}) collective-permute-start(f32[4,64,256]{2,1,0:T(8,128)S(1)} %slice.28), channel_id=1, source_target_pairs={{0,16},{1,17},{2,18},{3,19},{4,20},{5,21},{6,22},{7,23},{8,24},{9,... | collective-permute-start | bytes 786440 | tf_op jit(solution)/shard_map/ppermute | solution.py:30
  85.9 16.2 %collective-permute-start.20 = (f32[8,64,256]{2,1,0:T(8,128)S(1)}, f32[8,64,256]{2,1,0:T(8,128)S(1)}, u32[]{:S(2)}, u32[]{:S(2)}) collective-permute-start(f32[8,64,256]{2,1,0:T(8,128)S(1)} %collective-permute-done.18.refs_5_), channel_id=1, source_target_pairs={{0,48},{1,49},{2,50},{3,51},{4,52},{5,53},{6,54},{7,55},{8,56},{9,... | collective-permute-start | bytes 1572872 | tf_op jit(solution)/shard_map/ppermute | solution.py:30
  88.5 16.1 %collective-permute-start.19 = (f32[8,64,256]{2,1,0:T(8,128)S(1)}, f32[8,64,256]{2,1,0:T(8,128)S(1)}, u32[]{:S(2)}, u32[]{:S(2)}) collective-permute-start(f32[8,64,256]{2,1,0:T(8,128)S(1)} %collective-permute-done.18.refs_5_), channel_id=1, source_target_pairs={{0,16},{1,17},{2,18},{3,19},{4,20},{5,21},{6,22},{7,23},{8,24},{9,... | collective-permute-start | bytes 1572872 | tf_op jit(solution)/shard_map/ppermute | solution.py:30
  90.2 8.2 %collective-permute-start.26 = (f32[4,64,256]{2,1,0:T(8,128)S(1)}, f32[4,64,256]{2,1,0:T(8,128)S(1)}, u32[]{:S(2)}, u32[]{:S(2)}) collective-permute-start(f32[4,64,256]{2,1,0:T(8,128)S(1)} %collective-permute-done.25.refs_4_), channel_id=1, source_target_pairs={{0,64},{1,65},{2,66},{3,67},{4,68},{5,69},{6,70},{7,71},{8,72},{9,... | collective-permute-start | bytes 786440 | tf_op jit(solution)/shard_map/ppermute | solution.py:30
  93.4 8.7 %collective-permute-start.23 = (f32[4,64,256]{2,1,0:T(8,128)S(1)}, f32[4,64,256]{2,1,0:T(8,128)S(1)}, u32[]{:S(2)}, u32[]{:S(2)}) collective-permute-start(f32[4,64,256]{2,1,0:T(8,128)S(1)} %collective-permute-done.22.refs_3_), channel_id=1, source_target_pairs={{0,64},{1,65},{2,66},{3,67},{4,68},{5,69},{6,70},{7,71},{8,72},{9,... | collective-permute-start | bytes 786440 | tf_op jit(solution)/shard_map/ppermute | solution.py:30
  108.1 4.0 %collective-permute-start.27 = (f32[8,64,256]{2,1,0:T(8,128)S(1)}, f32[8,64,256]{2,1,0:T(8,128)S(1)}, u32[]{:S(2)}, u32[]{:S(2)}) collective-permute-start(f32[8,64,256]{2,1,0:T(8,128)S(1)} %get-tuple-element.28), channel_id=1, source_target_pairs={{0,1},{1,0},{2,3},{3,2},{4,5},{5,4},{6,7},{7,6},{8,9},{9,8},{10,11... | collective-permute-start | bytes 1572872 | tf_op jit(solution)/shard_map/ppermute | solution.py:34
  (8 other events, 10.8 us)

commit v5 on v4

--- a/solution.py
+++ b/solution.py
@@ -10,7 +10,6 @@
 BS = 64
 RING = 4
 KINDS = ("M", "M", "F")
-TIE = False
 SIDES = 8
 VMEM = pl.BlockSpec(memory_space=pltpu.VMEM)
 SMEM = pl.BlockSpec(memory_space=pltpu.SMEM)
@@ -59,8 +58,6 @@
     used = None
     if use_early:
         used = list(use_early(early))
-        if TIE and two is not None and kind in ("P", "W"):
-            two, used[0] = lax.optimization_barrier((two, used[0]))
     g1, g3 = step(across, 0, 1), step(across, 0, 3)
     if kind in ("P", "W"):
         far_two = whole(step(two, 1, 0), 1, 2)
@@ -230,39 +227,40 @@
     return call(kernel, [code, *arrays], [SMEM] + [VMEM] * len(arrays), outs, [VMEM] * 2, [], 8, 2)
 
 
-def square(code, left_shards, left_dense, right_early, right_dense, right_shards):
-    right_arrays, right_plan = flatten(right_shards)
-    n_left, n_right = 2 * len(left_dense), len(right_arrays)
-    places = [(n, k, flip, shift) for n, part in enumerate(left_shards) for k, (_, flip, shift) in enumerate(part)]
+def finish_left(code, early, dense, shards):
+    arrays, plan = flatten(shards)
+    places = [(flip, shift) for _, flip, shift in early]
 
     def kernel(code_ref, *refs):
-        lefts, refs = refs[:n_left], refs[n_left:]
-        early, refs = refs[:2], refs[2:]
-        right_refs, refs = refs[:n_right], refs[n_right:]
-        keep_ref, send_ref, *stored = refs[:4]
-        right_hi, right_lo, total, load_sems, store_sems = refs[4:]
-        row, chip, core = position()
-        loads = []
-        for k, (_, flip, shift) in enumerate(right_early):
-            source = source_of(row, flip, shift)
-            for m, here in enumerate((right_hi, right_lo)):
-                loads.append(pltpu.make_async_copy(early[m].at[k], here.at[source], load_sems.at[2 * k + m]))
-        pairs, stores = [], []
-        for at, (n, k, flip, shift) in enumerate(places):
+        outs = refs[-2:]
+        _, chip, _ = position()
+        unpack_left(plan, refs[2:-2], code_ref, *outs, True)
+        for k, (flip, shift) in enumerate(places):
             source = source_of(chip, flip, shift)
-            pairs.append((lefts[2 * n], lefts[2 * n + 1], k, source))
-            for m in range(2):
-                there = stored[m].at[source]
-                stores.append(pltpu.make_async_copy(lefts[2 * n + m].at[k], there, store_sems.at[2 * at + m]))
-        for m in loads + stores:
-            m.start()
-        unpack_right(right_plan, right_refs, code_ref, right_hi, right_lo, True)
-        for m in loads:
-            m.wait()
+            for here, out in zip(refs[:2], outs):
+                out[source] = here[k]
+
+    outs = [jax.ShapeDtypeStruct(left_shape(SIDES), BF16)] * 2
+    specs = [SMEM] + [VMEM] * (2 + len(arrays))
+    return call(kernel, [code, *dense, *arrays], specs, outs, [VMEM] * 2, [], 12, 3)
+
+
+def square(code, left, right_lists, right_dense, last_shards):
+    arrays, plan = flatten(last_shards)
+    n_dense = 2 * len(right_dense)
+
+    def kernel(code_ref, left_hi, left_lo, *refs):
+        ready, refs = refs[:n_dense], refs[n_dense:]
+        arrived, (keep_ref, send_ref, last_hi, last_lo, total) = refs[: len(arrays)], refs[len(arrays) :]
+        row, _, core = position()
+        unpack_right(plan, arrived, code_ref, last_hi, last_lo, False)
         ones, others = [], []
-        for left_hi, left_lo, k, source in pairs:
-            ones += [left_hi[k], left_lo[k], left_hi[k]]
-            others += [right_hi[source], right_hi[source], right_lo[source]]
+        sides = [(ready[2 * n], ready[2 * n + 1]) for n in range(len(right_lists))] + [(last_hi, last_lo)]
+        for shards, (right_hi, right_lo) in zip([*right_lists, last_shards], sides):
+            for k, (_, flip, shift) in enumerate(shards):
+                source = source_of(row, flip, shift)
+                ones += [left_hi[source], left_lo[source], left_hi[source]]
+                others += [right_hi[k], right_hi[k], right_lo[k]]
         total[...] = jnp.dot(
             jnp.concatenate(ones, axis=1), jnp.concatenate(others, axis=0), preferred_element_type=F32
         )
@@ -272,21 +270,16 @@
                 collect(
                     total, code_ref, part, HALF * (1 - core) + n, lambda t, *_: -t, send_ref, HALF * (1 - part) + n
                 )
-        for m in stores:
-            m.wait()
-
-    left = jax.ShapeDtypeStruct(left_shape(SIDES), BF16)
+
     return call(
         kernel,
-        [code, *[a for pair in left_dense for a in pair], *right_dense, *right_arrays],
-        [SMEM] + [VMEM] * (n_left + 2 + n_right),
-        [SLOTS, SLOTS, left, left],
-        [VMEM, VMEM, ANYWHERE, ANYWHERE],
+        [code, *left, *[a for pair in right_dense for a in pair], *arrays],
+        [SMEM] + [VMEM] * (2 + n_dense + len(arrays)),
+        [SLOTS, SLOTS],
+        [VMEM, VMEM],
         [
-            *[pltpu.VMEM(right_shape(SIDES), BF16)] * 2,
+            *[pltpu.VMEM(right_shape(len(last_shards)), BF16)] * 2,
             pltpu.VMEM((ROWS * BS, 512), F32),
-            pltpu.SemaphoreType.DMA((2 * len(right_early),)),
-            pltpu.SemaphoreType.DMA((2 * len(places),)),
         ],
         20,
         8,
@@ -351,10 +344,8 @@
     halves = jnp.concatenate([keep, other_core(send)], axis=0)
     left_early, left_dense, left_late = gather(matrix, True, KINDS[0], lambda x: make_dense(code, True, x))
     right_early, right_dense, right_late = gather(halves, False, KINDS[1], lambda x: make_dense(code, False, x))
-    left_last = make_dense(code, True, left_late)
-    keep, send, *left = square(
-        code, [left_early, left_late], [left_dense, left_last], right_early, right_dense, right_late
-    )
+    left = finish_left(code, left_early, left_dense, left_late)
+    keep, send = square(code, left, [right_early], [right_dense], right_late)
 
     early, _, late = gather(keep + other_core(send), False, KINDS[2])
     part = times(code, left, early)[0]

time: 113 us -> 113 us (level)
  starting transfers between devices: 43.2 us -> 46.5 us
  waiting for transfers between devices: 42.5 us -> 40.5 us
    ppermute x3, starting transfers between devices: 6.74 us -> 9.06 us  [other_core(): return lax.ppermute(value, 'col', [(c, c ^ 1) for c in range(2 * SIDES)])]
    ppermute x25, waiting for transfers between devices: 39.4 us -> 37.4 us  [move(): return lax.ppermute(value, ('row', 'col'), pairs)]
  transfers between devices with their start and end apart: 28 -> 28, of which waited for: 12 -> 9; matrix products, arithmetic and copies ran while one was open for 2% -> 2% of each run, Pallas kernels for 9% -> 9%
where the time goes in v5:
time: 113 us
  starting transfers between devices  46.5 us (41%)
  waiting for transfers between devices  40.5 us (36%)
  Pallas kernels  19.2 us (17%)
  local copies, waits for them, and re-layouts  3.83 us (3%)
  other arithmetic  2.74 us (2%)
    ppermute x25, starting transfers between devices, move(): return lax.ppermute(value, ('row', 'col'), pairs)  37.5 us
    ppermute x25, waiting for transfers between devices, move(): return lax.ppermute(value, ('row', 'col'), pairs)  37.4 us
    pallas_call x6, Pallas kernels, call(): pl.pallas_call(kernel, out_shape=outs, in_specs=in_specs, out_specs=out_s...  19.2 us
    ppermute x3, starting transfers between devices, other_core(): return lax.ppermute(value, 'col', [(c, c ^ 1) for c in range(2 * SIDES)])  9.06 us
    ppermute x3, waiting for transfers between devices, other_core(): return lax.ppermute(value, 'col', [(c, c ^ 1) for c in range(2 * SIDES)])  3.08 us
    unnamed x25, local copies, waits for them, and re-layouts  2.57 us
  transfers between devices with their start and end apart: 28, of which 9 were waited for; matrix products, arithmetic and copies ran while one was open for 2% of the time, Pallas kernels for 9%

profile of v5, /device:TPU:1, one launch (start us, length us, event | category | flops | bytes accessed | tf_op | source)
XLA Modules:
  0.0 113.0 jit_solution(9499359898028590325)
XLA Ops:
  1.1 1.5 %collective-permute-start.8 = (f32[4,64,256]{2,1,0:T(8,128)S(1)}, f32[4,64,256]{2,1,0:T(8,128)S(1)}, u32[]{:S(2)}, u32[]{:S(2)}) collective-permute-start(f32[4,64,256]{2,1,0:T(8,128)S(1)} %get-tuple-element.26), channel_id=1, source_target_pairs={{0,1},{1,0},{2,3},{3,2},{4,5},{5,4},{6,7},{7,6},{8,9},{9,8},{10,11... | collective-permute-start | bytes 786440 | tf_op jit(solution)/shard_map/ppermute | solution.py:33
  2.6 1.3 %collective-permute-start = (f32[8,64,256]{2,1,0:T(8,128)}, f32[8,64,256]{2,1,0:T(8,128)S(1)}, u32[]{:S(2)}, u32[]{:S(2)}) collective-permute-start(f32[8,64,256]{2,1,0:T(8,128)} %refs_0_.1), channel_id=1, source_target_pairs={{0,2},{1,3},{2,4},{3,5},{4,6},{5,7},{6,0},{7,1},{8,10},{9,11},{10,... | collective-permute-start | bytes 1572872 | tf_op jit(solution)/shard_map/ppermute | solution.py:29
  3.9 1.4 %collective-permute-start.1 = (f32[8,64,256]{2,1,0:T(8,128)}, f32[8,64,256]{2,1,0:T(8,128)S(1)}, u32[]{:S(2)}, u32[]{:S(2)}) collective-permute-start(f32[8,64,256]{2,1,0:T(8,128)} %refs_0_.1), channel_id=1, source_target_pairs={{0,6},{1,7},{2,0},{3,1},{4,2},{5,3},{6,4},{7,5},{8,14},{9,15},{10,... | collective-permute-start | bytes 1572872 | tf_op jit(solution)/shard_map/ppermute | solution.py:29
  5.3 1.4 %collective-permute-start.4 = (f32[8,64,256]{2,1,0:T(8,128)}, f32[8,64,256]{2,1,0:T(8,128)}, u32[]{:S(2)}, u32[]{:S(2)}) collective-permute-start(f32[8,64,256]{2,1,0:T(8,128)} %refs_0_.1), channel_id=1, source_target_pairs={{0,8},{1,9},{2,10},{3,11},{4,12},{5,13},{6,14},{7,15},{8,0},{9,1},... | collective-permute-start | bytes 1572872 | tf_op jit(solution)/shard_map/ppermute | solution.py:29
  6.7 1.7 %collective-permute-start.9 = (f32[8,64,256]{2,1,0:T(8,128)S(1)}, f32[8,64,256]{2,1,0:T(8,128)S(1)}, u32[]{:S(2)}, u32[]{:S(2)}) collective-permute-start(f32[8,64,256]{2,1,0:T(8,128)S(1)} %pad_maximum_fusion.1.refs_0_), channel_id=1, source_target_pairs={{0,16},{1,17},{2,18},{3,19},{4,20},{5,21},{6,22},{7,23},{8,24},{9,... | collective-permute-start | bytes 1572872 | tf_op jit(solution)/shard_map/ppermute | solution.py:29
  8.4 2.2 %collective-permute-start.10 = (f32[8,64,256]{2,1,0:T(8,128)S(1)}, f32[8,64,256]{2,1,0:T(8,128)S(1)}, u32[]{:S(2)}, u32[]{:S(2)}) collective-permute-start(f32[8,64,256]{2,1,0:T(8,128)S(1)} %pad_maximum_fusion.1.refs_0_), channel_id=1, source_target_pairs={{0,48},{1,49},{2,50},{3,51},{4,52},{5,53},{6,54},{7,55},{8,56},{9,... | collective-permute-start | bytes 1572872 | tf_op jit(solution)/shard_map/ppermute | solution.py:29
  10.6 6.9 %collective-permute-done.refs_1_ = f32[8,64,256]{2,1,0:T(8,128)S(1)} collective-permute-done((f32[8,64,256]{2,1,0:T(8,128)}, f32[8,64,256]{2,1,0:T(8,128)S(1)}, u32[]{:S(2)}, u32[]{:S(2)}) %collective-permute-start) | collective-permute-done | bytes 524320 | tf_op jit(solution)/shard_map/ppermute | solution.py:29
  17.5 3.0 %collective-permute-start.13 = (f32[8,64,256]{2,1,0:T(8,128)S(1)}, f32[8,64,256]{2,1,0:T(8,128)}, u32[]{:S(2)}, u32[]{:S(2)}) collective-permute-start(f32[8,64,256]{2,1,0:T(8,128)S(1)} %pad_maximum_fusion.1.refs_0_), channel_id=1, source_target_pairs={{0,64},{1,65},{2,66},{3,67},{4,68},{5,69},{6,70},{7,71},{8,72},{9,... | collective-permute-start | bytes 1572872 | tf_op jit(solution)/shard_map/ppermute | solution.py:29
  21.9 1.5 %collective-permute-start.3 = (f32[4,64,256]{2,1,0:T(8,128)S(1)}, f32[4,64,256]{2,1,0:T(8,128)S(1)}, u32[]{:S(2)}, u32[]{:S(2)}) collective-permute-start(f32[4,64,256]{2,1,0:T(8,128)S(1)} %slice.25), channel_id=1, source_target_pairs={{0,6},{1,7},{2,0},{3,1},{4,2},{5,3},{6,4},{7,5},{8,14},{9,15},{10,... | collective-permute-start | bytes 786440 | tf_op jit(solution)/shard_map/ppermute | solution.py:29
  23.5 1.7 %collective-permute-start.11 = (f32[4,64,256]{2,1,0:T(8,128)S(1)}, f32[4,64,256]{2,1,0:T(8,128)S(1)}, u32[]{:S(2)}, u32[]{:S(2)}) collective-permute-start(f32[4,64,256]{2,1,0:T(8,128)S(1)} %slice.26), channel_id=1, source_target_pairs={{0,16},{1,17},{2,18},{3,19},{4,20},{5,21},{6,22},{7,23},{8,24},{9,... | collective-permute-start | bytes 786440 | tf_op jit(solution)/shard_map/ppermute | solution.py:29
  25.3 3.3 %collective-permute-done.2.refs_3_ = f32[4,64,256]{2,1,0:T(8,128)S(1)} collective-permute-done((f32[4,64,256]{2,1,0:T(8,128)S(1)}, f32[4,64,256]{2,1,0:T(8,128)S(1)}, u32[]{:S(2)}, u32[]{:S(2)}) %collective-permute-start.2) | collective-permute-done | bytes 262176 | tf_op jit(solution)/shard_map/ppermute | solution.py:29
  28.6 3.8 %collective-permute-start.12 = (f32[4,64,256]{2,1,0:T(8,128)S(1)}, f32[4,64,256]{2,1,0:T(8,128)S(1)}, u32[]{:S(2)}, u32[]{:S(2)}) collective-permute-start(f32[4,64,256]{2,1,0:T(8,128)S(1)} %slice.27), channel_id=1, source_target_pairs={{0,48},{1,49},{2,50},{3,51},{4,52},{5,53},{6,54},{7,55},{8,56},{9,... | collective-permute-start | bytes 786440 | tf_op jit(solution)/shard_map/ppermute | solution.py:29
  35.6 3.4 %collective-permute-start.15 = (f32[8,64,256]{2,1,0:T(8,128)}, f32[8,64,256]{2,1,0:T(8,128)}, u32[]{:S(2)}, u32[]{:S(2)}) collective-permute-start(f32[8,64,256]{2,1,0:T(8,128)} %collective-permute-done.13.refs_5_), channel_id=1, source_target_pairs={{0,48},{1,49},{2,50},{3,51},{4,52},{5,53},{6,54},{7,55},{8,56},{9,... | collective-permute-start | bytes 1572872 | tf_op jit(solution)/shard_map/ppermute | solution.py:29
  43.1 2.0 %shard_map.46 = (bf16[5,512,256]{2,1,0:T(8,128)(2,1)S(1)}, bf16[5,512,256]{2,1,0:T(8,128)(2,1)S(1)}) custom-call(s32[64,16]{1,0:T(8,128)S(1)} %multiply_add_fusion.code_ref, f32[8,64,256]{2,1,0:T(8,128)S(1)} %copy-done, f32[8,64,256]{2,1,0:T(8,128)S(1)} %collective-permute-done.refs_1_, f32[8,64,256]{2,1,0:T(8,128)S(1)} %collective-permute-done.1.refs_2_, ...), custom_call_target="tpu_custom_call" | custom-call | bytes 6000000 | tf_op jit(solution)/shard_map/pallas_call | solution.py:208
  45.2 2.0 %shard_map.48 = (bf16[5,256,512]{2,1,0:T(8,128)(2,1)S(1)}, bf16[5,256,512]{2,1,0:T(8,128)(2,1)S(1)}) custom-call(s32[64,16]{1,0:T(8,128)S(1)} %multiply_add_fusion.code_ref, f32[8,64,256]{2,1,0:T(8,128)S(1)} %pad_maximum_fusion.1.refs_0_, f32[8,64,256]{2,1,0:T(8,128)S(1)} %collective-permute-done.9.refs_1_, ...), custom_call_target="tpu_custom_call" | custom-call | bytes 6000000 | tf_op jit(solution)/shard_map/pallas_call | solution.py:208
  47.2 2.0 %shard_map.47 = (bf16[8,512,256]{2,1,0:T(8,128)(2,1)S(1)}, bf16[8,512,256]{2,1,0:T(8,128)(2,1)S(1)}) custom-call(s32[64,16]{1,0:T(8,128)S(1)} %multiply_add_fusion.code_ref, bf16[5,512,256]{2,1,0:T(8,128)(2,1)S(1)} %get-tuple-element.15.refs_0_, bf16[5,512,256]{2,1,0:T(8,128)(2,1)S(1)} %get-tuple-element.16.refs_1_, f32[8,64,256]{2,1,0:T(8,128)S(1)} %copy-done.8, ...), custom_call_target="tpu_custom_call" | custom-call | bytes 9000000 | tf_op jit(solution)/shard_map/pallas_call | solution.py:208
  49.3 7.7 %collective-permute-done.16.refs_4_ = f32[8,64,256]{2,1,0:T(8,128)} collective-permute-done((f32[8,64,256]{2,1,0:T(8,128)}, f32[8,64,256]{2,1,0:T(8,128)}, u32[]{:S(2)}, u32[]{:S(2)}) %collective-permute-start.16) | collective-permute-done | bytes 524320 | tf_op jit(solution)/shard_map/ppermute | solution.py:29
  57.0 5.2 %shard_map.49 = (f32[8,64,256]{2,1,0:T(8,128)S(1)}, f32[8,64,256]{2,1,0:T(8,128)S(1)}) custom-call(s32[64,16]{1,0:T(8,128)S(1)} %multiply_add_fusion.code_ref, bf16[8,512,256]{2,1,0:T(8,128)(2,1)S(1)} %get-tuple-element.17.left_hi.far_hi, bf16[8,512,256]{2,1,0:T(8,128)(2,1)S(1)} %get-tuple-element.18.left_lo.far_lo, ...), custom_call_target="tpu_custom_call" | custom-call | bytes 24000000 | tf_op jit(solution)/shard_map/pallas_call | solution.py:208
  62.1 3.4 %collective-permute-start.17 = (f32[8,64,256]{2,1,0:T(8,128)S(1)}, f32[8,64,256]{2,1,0:T(8,128)S(1)}, u32[]{:S(2)}, u32[]{:S(2)}) collective-permute-start(f32[8,64,256]{2,1,0:T(8,128)S(1)} %get-tuple-element.22), channel_id=1, source_target_pairs={{0,1},{1,0},{2,3},{3,2},{4,5},{5,4},{6,7},{7,6},{8,9},{9,8},{10,11... | collective-permute-start | bytes 1572872 | tf_op jit(solution)/shard_map/ppermute | solution.py:33
  65.5 1.5 %collective-permute-done.17 = f32[8,64,256]{2,1,0:T(8,128)S(1)} collective-permute-done((f32[8,64,256]{2,1,0:T(8,128)S(1)}, f32[8,64,256]{2,1,0:T(8,128)S(1)}, u32[]{:S(2)}, u32[]{:S(2)}) %collective-permute-start.17) | collective-permute-done | bytes 524320 | tf_op jit(solution)/shard_map/ppermute | solution.py:33
  67.1 1.7 %collective-permute-start.21 = (f32[8,64,256]{2,1,0:T(8,128)S(1)}, f32[8,64,256]{2,1,0:T(8,128)S(1)}, u32[]{:S(2)}, u32[]{:S(2)}) collective-permute-start(f32[8,64,256]{2,1,0:T(8,128)S(1)} %add.23.refs_0_), channel_id=1, source_target_pairs={{0,16},{1,17},{2,18},{3,19},{4,20},{5,21},{6,22},{7,23},{8,24},{9,... | collective-permute-start | bytes 1572872 | tf_op jit(solution)/shard_map/ppermute | solution.py:29
  68.9 2.2 %collective-permute-start.24 = (f32[8,64,256]{2,1,0:T(8,128)S(1)}, f32[8,64,256]{2,1,0:T(8,128)S(1)}, u32[]{:S(2)}, u32[]{:S(2)}) collective-permute-start(f32[8,64,256]{2,1,0:T(8,128)S(1)} %add.23.refs_0_), channel_id=1, source_target_pairs={{0,48},{1,49},{2,50},{3,51},{4,52},{5,53},{6,54},{7,55},{8,56},{9,... | collective-permute-start | bytes 1572872 | tf_op jit(solution)/shard_map/ppermute | solution.py:29
  71.4 11.6 %collective-permute-done.21.refs_1_ = f32[8,64,256]{2,1,0:T(8,128)S(1)} collective-permute-done((f32[8,64,256]{2,1,0:T(8,128)S(1)}, f32[8,64,256]{2,1,0:T(8,128)S(1)}, u32[]{:S(2)}, u32[]{:S(2)}) %collective-permute-start.21) | collective-permute-done | bytes 524320 | tf_op jit(solution)/shard_map/ppermute | solution.py:29
  83.1 2.7 %collective-permute-start.25 = (f32[4,64,256]{2,1,0:T(8,128)S(1)}, f32[4,64,256]{2,1,0:T(8,128)S(1)}, u32[]{:S(2)}, u32[]{:S(2)}) collective-permute-start(f32[4,64,256]{2,1,0:T(8,128)S(1)} %slice.29), channel_id=1, source_target_pairs={{0,48},{1,49},{2,50},{3,51},{4,52},{5,53},{6,54},{7,55},{8,56},{9,... | collective-permute-start | bytes 786440 | tf_op jit(solution)/shard_map/ppermute | solution.py:29
  85.8 2.7 %collective-permute-start.20 = (f32[8,64,256]{2,1,0:T(8,128)S(1)}, f32[8,64,256]{2,1,0:T(8,128)S(1)}, u32[]{:S(2)}, u32[]{:S(2)}) collective-permute-start(f32[8,64,256]{2,1,0:T(8,128)S(1)} %collective-permute-done.18.refs_5_), channel_id=1, source_target_pairs={{0,48},{1,49},{2,50},{3,51},{4,52},{5,53},{6,54},{7,55},{8,56},{9,... | collective-permute-start | bytes 1572872 | tf_op jit(solution)/shard_map/ppermute | solution.py:29
  88.5 2.7 %collective-permute-done.22.refs_3_ = f32[4,64,256]{2,1,0:T(8,128)S(1)} collective-permute-done((f32[4,64,256]{2,1,0:T(8,128)S(1)}, f32[4,64,256]{2,1,0:T(8,128)S(1)}, u32[]{:S(2)}, u32[]{:S(2)}) %collective-permute-start.22) | collective-permute-done | bytes 262176 | tf_op jit(solution)/shard_map/ppermute | solution.py:29
  91.6 2.6 %collective-permute-start.26 = (f32[4,64,256]{2,1,0:T(8,128)S(1)}, f32[4,64,256]{2,1,0:T(8,128)S(1)}, u32[]{:S(2)}, u32[]{:S(2)}) collective-permute-start(f32[4,64,256]{2,1,0:T(8,128)S(1)} %collective-permute-done.25.refs_4_), channel_id=1, source_target_pairs={{0,64},{1,65},{2,66},{3,67},{4,68},{5,69},{6,70},{7,71},{8,72},{9,... | collective-permute-start | bytes 786440 | tf_op jit(solution)/shard_map/ppermute | solution.py:29
  94.2 4.5 %shard_map.50.refs_4_ = f32[512,512]{1,0:T(8,128)S(1)} custom-call(s32[64,16]{1,0:T(8,128)S(1)} %multiply_add_fusion.code_ref, bf16[8,512,256]{2,1,0:T(8,128)(2,1)S(1)} %get-tuple-element.17.left_hi.far_hi, bf16[8,512,256]{2,1,0:T(8,128)(2,1)S(1)} %get-tuple-element.18.left_lo.far_lo, f32[8,64,256]{2,1,0:T(8,128)S(1)} %add.23.refs_0_, ...), custom_call_target="tpu_custom_call" | custom-call | bytes 12000000 | tf_op jit(solution)/shard_map/pallas_call | solution.py:208
  98.7 4.3 %collective-permute-done.26.refs_3_ = f32[4,64,256]{2,1,0:T(8,128)S(1)} collective-permute-done((f32[4,64,256]{2,1,0:T(8,128)S(1)}, f32[4,64,256]{2,1,0:T(8,128)S(1)}, u32[]{:S(2)}, u32[]{:S(2)}) %collective-permute-start.26) | collective-permute-done | bytes 262176 | tf_op jit(solution)/shard_map/ppermute | solution.py:29
  103.0 3.5 %shard_map.51 = (f32[8,64,256]{2,1,0:T(8,128)S(1)}, f32[8,64,256]{2,1,0:T(8,128)S(1)}) custom-call(s32[64,16]{1,0:T(8,128)S(1)} %multiply_add_fusion.code_ref, bf16[8,512,256]{2,1,0:T(8,128)(2,1)S(1)} %get-tuple-element.17.left_hi.far_hi, bf16[8,512,256]{2,1,0:T(8,128)(2,1)S(1)} %get-tuple-element.18.left_lo.far_lo, ...), custom_call_target="tpu_custom_call" | custom-call | bytes 12000000 | tf_op jit(solution)/shard_map/pallas_call | solution.py:208
  106.5 4.2 %collective-permute-start.27 = (f32[8,64,256]{2,1,0:T(8,128)S(1)}, f32[8,64,256]{2,1,0:T(8,128)S(1)}, u32[]{:S(2)}, u32[]{:S(2)}) collective-permute-start(f32[8,64,256]{2,1,0:T(8,128)S(1)} %get-tuple-element.24), channel_id=1, source_target_pairs={{0,1},{1,0},{2,3},{3,2},{4,5},{5,4},{6,7},{7,6},{8,9},{9,8},{10,11... | collective-permute-start | bytes 1572872 | tf_op jit(solution)/shard_map/ppermute | solution.py:33
  110.6 1.5 %collective-permute-done.27 = f32[8,64,256]{2,1,0:T(8,128)S(1)} collective-permute-done((f32[8,64,256]{2,1,0:T(8,128)S(1)}, f32[8,64,256]{2,1,0:T(8,128)S(1)}, u32[]{:S(2)}, u32[]{:S(2)}) %collective-permute-start.27) | collective-permute-done | bytes 524320 | tf_op jit(solution)/shard_map/ppermute | solution.py:33
  (70 shorter events, 11.7 us)
Async XLA Ops:
  1.1 5.6 %collective-permute-start.8 = (f32[4,64,256]{2,1,0:T(8,128)S(1)}, f32[4,64,256]{2,1,0:T(8,128)S(1)}, u32[]{:S(2)}, u32[]{:S(2)}) collective-permute-start(f32[4,64,256]{2,1,0:T(8,128)S(1)} %get-tuple-element.26), channel_id=1, source_target_pairs={{0,1},{1,0},{2,3},{3,2},{4,5},{5,4},{6,7},{7,6},{8,9},{9,8},{10,11... | collective-permute-start | bytes 786440 | tf_op jit(solution)/shard_map/ppermute | solution.py:33
  2.6 14.9 %collective-permute-start = (f32[8,64,256]{2,1,0:T(8,128)}, f32[8,64,256]{2,1,0:T(8,128)S(1)}, u32[]{:S(2)}, u32[]{:S(2)}) collective-permute-start(f32[8,64,256]{2,1,0:T(8,128)} %refs_0_.1), channel_id=1, source_target_pairs={{0,2},{1,3},{2,4},{3,5},{4,6},{5,7},{6,0},{7,1},{8,10},{9,11},{10,... | collective-permute-start | bytes 1572872 | tf_op jit(solution)/shard_map/ppermute | solution.py:29
  3.9 16.6 %collective-permute-start.1 = (f32[8,64,256]{2,1,0:T(8,128)}, f32[8,64,256]{2,1,0:T(8,128)S(1)}, u32[]{:S(2)}, u32[]{:S(2)}) collective-permute-start(f32[8,64,256]{2,1,0:T(8,128)} %refs_0_.1), channel_id=1, source_target_pairs={{0,6},{1,7},{2,0},{3,1},{4,2},{5,3},{6,4},{7,5},{8,14},{9,15},{10,... | collective-permute-start | bytes 1572872 | tf_op jit(solution)/shard_map/ppermute | solution.py:29
  5.3 15.4 %collective-permute-start.4 = (f32[8,64,256]{2,1,0:T(8,128)}, f32[8,64,256]{2,1,0:T(8,128)}, u32[]{:S(2)}, u32[]{:S(2)}) collective-permute-start(f32[8,64,256]{2,1,0:T(8,128)} %refs_0_.1), channel_id=1, source_target_pairs={{0,8},{1,9},{2,10},{3,11},{4,12},{5,13},{6,14},{7,15},{8,0},{9,1},... | collective-permute-start | bytes 1572872 | tf_op jit(solution)/shard_map/ppermute | solution.py:29
  6.7 15.2 %collective-permute-start.9 = (f32[8,64,256]{2,1,0:T(8,128)S(1)}, f32[8,64,256]{2,1,0:T(8,128)S(1)}, u32[]{:S(2)}, u32[]{:S(2)}) collective-permute-start(f32[8,64,256]{2,1,0:T(8,128)S(1)} %pad_maximum_fusion.1.refs_0_), channel_id=1, source_target_pairs={{0,16},{1,17},{2,18},{3,19},{4,20},{5,21},{6,22},{7,23},{8,24},{9,... | collective-permute-start | bytes 1572872 | tf_op jit(solution)/shard_map/ppermute | solution.py:29
  8.4 15.2 %collective-permute-start.10 = (f32[8,64,256]{2,1,0:T(8,128)S(1)}, f32[8,64,256]{2,1,0:T(8,128)S(1)}, u32[]{:S(2)}, u32[]{:S(2)}) collective-permute-start(f32[8,64,256]{2,1,0:T(8,128)S(1)} %pad_maximum_fusion.1.refs_0_), channel_id=1, source_target_pairs={{0,48},{1,49},{2,50},{3,51},{4,52},{5,53},{6,54},{7,55},{8,56},{9,... | collective-permute-start | bytes 1572872 | tf_op jit(solution)/shard_map/ppermute | solution.py:29
  17.5 15.9 %collective-permute-start.13 = (f32[8,64,256]{2,1,0:T(8,128)S(1)}, f32[8,64,256]{2,1,0:T(8,128)}, u32[]{:S(2)}, u32[]{:S(2)}) collective-permute-start(f32[8,64,256]{2,1,0:T(8,128)S(1)} %pad_maximum_fusion.1.refs_0_), channel_id=1, source_target_pairs={{0,64},{1,65},{2,66},{3,67},{4,68},{5,69},{6,70},{7,71},{8,72},{9,... | collective-permute-start | bytes 1572872 | tf_op jit(solution)/shard_map/ppermute | solution.py:29
  20.5 8.0 %collective-permute-start.2 = (f32[4,64,256]{2,1,0:T(8,128)S(1)}, f32[4,64,256]{2,1,0:T(8,128)S(1)}, u32[]{:S(2)}, u32[]{:S(2)}) collective-permute-start(f32[4,64,256]{2,1,0:T(8,128)S(1)} %slice.24), channel_id=1, source_target_pairs={{0,2},{1,3},{2,4},{3,5},{4,6},{5,7},{6,0},{7,1},{8,10},{9,11},{10,... | collective-permute-start | bytes 786440 | tf_op jit(solution)/shard_map/ppermute | solution.py:29
  20.7 19.9 %collective-permute-start.5 = (f32[8,64,256]{2,1,0:T(8,128)}, f32[8,64,256]{2,1,0:T(8,128)S(1)}, u32[]{:S(2)}, u32[]{:S(2)}) collective-permute-start(f32[8,64,256]{2,1,0:T(8,128)} %collective-permute-done.4.refs_5_), channel_id=1, source_target_pairs={{0,2},{1,3},{2,4},{3,5},{4,6},{5,7},{6,0},{7,1},{8,10},{9,11},{10,... | collective-permute-start | bytes 1572872 | tf_op jit(solution)/shard_map/ppermute | solution.py:29
  21.9 10.4 %collective-permute-start.3 = (f32[4,64,256]{2,1,0:T(8,128)S(1)}, f32[4,64,256]{2,1,0:T(8,128)S(1)}, u32[]{:S(2)}, u32[]{:S(2)}) collective-permute-start(f32[4,64,256]{2,1,0:T(8,128)S(1)} %slice.25), channel_id=1, source_target_pairs={{0,6},{1,7},{2,0},{3,1},{4,2},{5,3},{6,4},{7,5},{8,14},{9,15},{10,... | collective-permute-start | bytes 786440 | tf_op jit(solution)/shard_map/ppermute | solution.py:29
  23.5 18.4 %copy-start.9 = (s32[64,16,4]{0,2,1:T(4,128)S(1)}, s32[64,16,4]{0,2,1:T(4,128)}, u32[]{:S(2)}) copy-start(s32[64,16,4]{0,2,1:T(4,128)} %param.5) | copy-start | bytes 49156
  23.5 18.4 %copy-start.11 = (s32[4]{0:T(128)S(1)}, s32[4]{0:T(128)}, u32[]{:S(2)}) copy-start(s32[4]{0:T(128)} %constant.27.clone) | copy-start | bytes 52
  23.5 18.5 %copy-start.10 = (s32[64,16]{0,1:T(8,128)S(1)}, s32[64,16]{0,1:T(8,128)}, u32[]{:S(2)}) copy-start(s32[64,16]{0,1:T(8,128)} %param.6) | copy-start | bytes 12292
  23.5 18.6 %copy-start = (f32[8,64,256]{2,1,0:T(8,128)S(1)}, f32[8,64,256]{2,1,0:T(8,128)}, u32[]{:S(2)}) copy-start(f32[8,64,256]{2,1,0:T(8,128)} %refs_0_.1) | copy-start | bytes 1572868
  23.5 10.3 %collective-permute-start.11 = (f32[4,64,256]{2,1,0:T(8,128)S(1)}, f32[4,64,256]{2,1,0:T(8,128)S(1)}, u32[]{:S(2)}, u32[]{:S(2)}) collective-permute-start(f32[4,64,256]{2,1,0:T(8,128)S(1)} %slice.26), channel_id=1, source_target_pairs={{0,16},{1,17},{2,18},{3,19},{4,20},{5,21},{6,22},{7,23},{8,24},{9,... | collective-permute-start | bytes 786440 | tf_op jit(solution)/shard_map/ppermute | solution.py:29
  28.6 7.1 %collective-permute-start.12 = (f32[4,64,256]{2,1,0:T(8,128)S(1)}, f32[4,64,256]{2,1,0:T(8,128)S(1)}, u32[]{:S(2)}, u32[]{:S(2)}) collective-permute-start(f32[4,64,256]{2,1,0:T(8,128)S(1)} %slice.27), channel_id=1, source_target_pairs={{0,48},{1,49},{2,50},{3,51},{4,52},{5,53},{6,54},{7,55},{8,56},{9,... | collective-permute-start | bytes 786440 | tf_op jit(solution)/shard_map/ppermute | solution.py:29
  32.3 14.9 %collective-permute-start.6 = (f32[8,64,256]{2,1,0:T(8,128)}, f32[8,64,256]{2,1,0:T(8,128)}, u32[]{:S(2)}, u32[]{:S(2)}) collective-permute-start(f32[8,64,256]{2,1,0:T(8,128)} %collective-permute-done.4.refs_5_), channel_id=1, source_target_pairs={{0,6},{1,7},{2,0},{3,1},{4,2},{5,3},{6,4},{7,5},{8,14},{9,15},{10,... | collective-permute-start | bytes 1572872 | tf_op jit(solution)/shard_map/ppermute | solution.py:29
  33.4 13.8 %collective-permute-start.7 = (f32[8,64,256]{2,1,0:T(8,128)}, f32[8,64,256]{2,1,0:T(8,128)}, u32[]{:S(2)}, u32[]{:S(2)}) collective-permute-start(f32[8,64,256]{2,1,0:T(8,128)} %pad_maximum_fusion), channel_id=1, source_target_pairs={{0,8},{1,9},{2,10},{3,11},{4,12},{5,13},{6,14},{7,15},{8,0},{9,1},... | collective-permute-start | bytes 1572872 | tf_op jit(solution)/shard_map/ppermute | solution.py:29
  33.8 15.4 %collective-permute-start.14 = (f32[8,64,256]{2,1,0:T(8,128)}, f32[8,64,256]{2,1,0:T(8,128)}, u32[]{:S(2)}, u32[]{:S(2)}) collective-permute-start(f32[8,64,256]{2,1,0:T(8,128)} %collective-permute-done.13.refs_5_), channel_id=1, source_target_pairs={{0,16},{1,17},{2,18},{3,19},{4,20},{5,21},{6,22},{7,23},{8,24},{9,... | collective-permute-start | bytes 1572872 | tf_op jit(solution)/shard_map/ppermute | solution.py:29
  35.6 13.6 %collective-permute-start.15 = (f32[8,64,256]{2,1,0:T(8,128)}, f32[8,64,256]{2,1,0:T(8,128)}, u32[]{:S(2)}, u32[]{:S(2)}) collective-permute-start(f32[8,64,256]{2,1,0:T(8,128)} %collective-permute-done.13.refs_5_), channel_id=1, source_target_pairs={{0,48},{1,49},{2,50},{3,51},{4,52},{5,53},{6,54},{7,55},{8,56},{9,... | collective-permute-start | bytes 1572872 | tf_op jit(solution)/shard_map/ppermute | solution.py:29
  41.4 15.6 %collective-permute-start.16 = (f32[8,64,256]{2,1,0:T(8,128)}, f32[8,64,256]{2,1,0:T(8,128)}, u32[]{:S(2)}, u32[]{:S(2)}) collective-permute-start(f32[8,64,256]{2,1,0:T(8,128)} %pad_maximum_fusion.2), channel_id=1, source_target_pairs={{0,64},{1,65},{2,66},{3,67},{4,68},{5,69},{6,70},{7,71},{8,72},{9,... | collective-permute-start | bytes 1572872 | tf_op jit(solution)/shard_map/ppermute | solution.py:29
  62.1 4.9 %collective-permute-start.17 = (f32[8,64,256]{2,1,0:T(8,128)S(1)}, f32[8,64,256]{2,1,0:T(8,128)S(1)}, u32[]{:S(2)}, u32[]{:S(2)}) collective-permute-start(f32[8,64,256]{2,1,0:T(8,128)S(1)} %get-tuple-element.22), channel_id=1, source_target_pairs={{0,1},{1,0},{2,3},{3,2},{4,5},{5,4},{6,7},{7,6},{8,9},{9,8},{10,11... | collective-permute-start | bytes 1572872 | tf_op jit(solution)/shard_map/ppermute | solution.py:33
  67.1 15.8 %collective-permute-start.21 = (f32[8,64,256]{2,1,0:T(8,128)S(1)}, f32[8,64,256]{2,1,0:T(8,128)S(1)}, u32[]{:S(2)}, u32[]{:S(2)}) collective-permute-start(f32[8,64,256]{2,1,0:T(8,128)S(1)} %add.23.refs_0_), channel_id=1, source_target_pairs={{0,16},{1,17},{2,18},{3,19},{4,20},{5,21},{6,22},{7,23},{8,24},{9,... | collective-permute-start | bytes 1572872 | tf_op jit(solution)/shard_map/ppermute | solution.py:29
  68.9 14.2 %collective-permute-start.24 = (f32[8,64,256]{2,1,0:T(8,128)S(1)}, f32[8,64,256]{2,1,0:T(8,128)S(1)}, u32[]{:S(2)}, u32[]{:S(2)}) collective-permute-start(f32[8,64,256]{2,1,0:T(8,128)S(1)} %add.23.refs_0_), channel_id=1, source_target_pairs={{0,48},{1,49},{2,50},{3,51},{4,52},{5,53},{6,54},{7,55},{8,56},{9,... | collective-permute-start | bytes 1572872 | tf_op jit(solution)/shard_map/ppermute | solution.py:29
  71.1 14.8 %collective-permute-start.18 = (f32[8,64,256]{2,1,0:T(8,128)S(1)}, f32[8,64,256]{2,1,0:T(8,128)S(1)}, u32[]{:S(2)}, u32[]{:S(2)}) collective-permute-start(f32[8,64,256]{2,1,0:T(8,128)S(1)} %add.23.refs_0_), channel_id=1, source_target_pairs={{0,64},{1,65},{2,66},{3,67},{4,68},{5,69},{6,70},{7,71},{8,72},{9,... | collective-permute-start | bytes 1572872 | tf_op jit(solution)/shard_map/ppermute | solution.py:29
  83.0 8.2 %collective-permute-start.22 = (f32[4,64,256]{2,1,0:T(8,128)S(1)}, f32[4,64,256]{2,1,0:T(8,128)S(1)}, u32[]{:S(2)}, u32[]{:S(2)}) collective-permute-start(f32[4,64,256]{2,1,0:T(8,128)S(1)} %slice.28), channel_id=1, source_target_pairs={{0,16},{1,17},{2,18},{3,19},{4,20},{5,21},{6,22},{7,23},{8,24},{9,... | collective-permute-start | bytes 786440 | tf_op jit(solution)/shard_map/ppermute | solution.py:29
  83.1 8.5 %collective-permute-start.25 = (f32[4,64,256]{2,1,0:T(8,128)S(1)}, f32[4,64,256]{2,1,0:T(8,128)S(1)}, u32[]{:S(2)}, u32[]{:S(2)}) collective-permute-start(f32[4,64,256]{2,1,0:T(8,128)S(1)} %slice.29), channel_id=1, source_target_pairs={{0,48},{1,49},{2,50},{3,51},{4,52},{5,53},{6,54},{7,55},{8,56},{9,... | collective-permute-start | bytes 786440 | tf_op jit(solution)/shard_map/ppermute | solution.py:29
  85.8 17.1 %collective-permute-start.19 = (f32[8,64,256]{2,1,0:T(8,128)S(1)}, f32[8,64,256]{2,1,0:T(8,128)S(1)}, u32[]{:S(2)}, u32[]{:S(2)}) collective-permute-start(f32[8,64,256]{2,1,0:T(8,128)S(1)} %collective-permute-done.18.refs_5_), channel_id=1, source_target_pairs={{0,16},{1,17},{2,18},{3,19},{4,20},{5,21},{6,22},{7,23},{8,24},{9,... | collective-permute-start | bytes 1572872 | tf_op jit(solution)/shard_map/ppermute | solution.py:29
  85.8 17.1 %collective-permute-start.20 = (f32[8,64,256]{2,1,0:T(8,128)S(1)}, f32[8,64,256]{2,1,0:T(8,128)S(1)}, u32[]{:S(2)}, u32[]{:S(2)}) collective-permute-start(f32[8,64,256]{2,1,0:T(8,128)S(1)} %collective-permute-done.18.refs_5_), channel_id=1, source_target_pairs={{0,48},{1,49},{2,50},{3,51},{4,52},{5,53},{6,54},{7,55},{8,56},{9,... | collective-permute-start | bytes 1572872 | tf_op jit(solution)/shard_map/ppermute | solution.py:29
  91.2 7.5 %collective-permute-start.23 = (f32[4,64,256]{2,1,0:T(8,128)S(1)}, f32[4,64,256]{2,1,0:T(8,128)S(1)}, u32[]{:S(2)}, u32[]{:S(2)}) collective-permute-start(f32[4,64,256]{2,1,0:T(8,128)S(1)} %collective-permute-done.22.refs_3_), channel_id=1, source_target_pairs={{0,64},{1,65},{2,66},{3,67},{4,68},{5,69},{6,70},{7,71},{8,72},{9,... | collective-permute-start | bytes 786440 | tf_op jit(solution)/shard_map/ppermute | solution.py:29
  91.6 11.4 %collective-permute-start.26 = (f32[4,64,256]{2,1,0:T(8,128)S(1)}, f32[4,64,256]{2,1,0:T(8,128)S(1)}, u32[]{:S(2)}, u32[]{:S(2)}) collective-permute-start(f32[4,64,256]{2,1,0:T(8,128)S(1)} %collective-permute-done.25.refs_4_), channel_id=1, source_target_pairs={{0,64},{1,65},{2,66},{3,67},{4,68},{5,69},{6,70},{7,71},{8,72},{9,... | collective-permute-start | bytes 786440 | tf_op jit(solution)/shard_map/ppermute | solution.py:29
  106.5 5.7 %collective-permute-start.27 = (f32[8,64,256]{2,1,0:T(8,128)S(1)}, f32[8,64,256]{2,1,0:T(8,128)S(1)}, u32[]{:S(2)}, u32[]{:S(2)}) collective-permute-start(f32[8,64,256]{2,1,0:T(8,128)S(1)} %get-tuple-element.24), channel_id=1, source_target_pairs={{0,1},{1,0},{2,3},{3,2},{4,5},{5,4},{6,7},{7,6},{8,9},{9,8},{10,11... | collective-permute-start | bytes 1572872 | tf_op jit(solution)/shard_map/ppermute | solution.py:33
  (8 other events, 13.9 us)

commit v6 on v5

--- a/solution.py
+++ b/solution.py
@@ -9,7 +9,7 @@
 HALF = ROWS // 2
 BS = 64
 RING = 4
-KINDS = ("M", "M", "F")
+KINDS = ("F3", "M", "F")
 SIDES = 8
 VMEM = pl.BlockSpec(memory_space=pltpu.VMEM)
 SMEM = pl.BlockSpec(memory_space=pltpu.SMEM)

time: 113 us -> 111 us (0.982)
  waiting for transfers between devices: 40.5 us -> 31.6 us
  local copies, waits for them, and re-layouts: 3.83 us -> 8.1 us
  starting transfers between devices: 46.5 us -> 50.1 us
    ppermute x25 -> x26, waiting for transfers between devices: 37.4 us -> 28.5 us  [move(): return lax.ppermute(value, ('row', 'col'), pairs)]
    ppermute x25 -> x26, starting transfers between devices: 37.5 us -> 40.3 us  [move(): return lax.ppermute(value, ('row', 'col'), pairs)]
    unnamed x25 -> x33, local copies, waits for them, and re-layouts: 2.57 us -> 5.32 us
    slice x0 -> x2, local copies, waits for them, and re-layouts: none -> 1.47 us  [gather(): far_two = by_half(step(g1[:HALF], 0, 1), step(g3[HALF:], 0, 3), 1)]
  transfers between devices with their start and end apart: 28 -> 29, of which waited for: 9 -> 9; matrix products, arithmetic and copies ran while one was open for 2% -> 2% of each run, Pallas kernels for 9% -> 9%
where the time goes in v6:
time: 111 us
  starting transfers between devices  50.1 us (45%)
  waiting for transfers between devices  31.6 us (28%)
  Pallas kernels  19.1 us (17%)
  local copies, waits for them, and re-layouts  8.1 us (7%)
  other arithmetic  1.93 us (2%)
    ppermute x26, starting transfers between devices, move(): return lax.ppermute(value, ('row', 'col'), pairs)  40.3 us
    ppermute x26, waiting for transfers between devices, move(): return lax.ppermute(value, ('row', 'col'), pairs)  28.5 us
    pallas_call x6, Pallas kernels, call(): pl.pallas_call(kernel, out_shape=outs, in_specs=in_specs, out_specs=out_s...  19.1 us
    ppermute x3, starting transfers between devices, other_core(): return lax.ppermute(value, 'col', [(c, c ^ 1) for c in range(2 * SIDES)])  9.72 us
    unnamed x33, local copies, waits for them, and re-layouts  5.32 us
    ppermute x3, waiting for transfers between devices, other_core(): return lax.ppermute(value, 'col', [(c, c ^ 1) for c in range(2 * SIDES)])  3.08 us
  transfers between devices with their start and end apart: 29, of which 9 were waited for; matrix products, arithmetic and copies ran while one was open for 2% of the time, Pallas kernels for 9%

profile of v6, /device:TPU:1, one launch (start us, length us, event | category | flops | bytes accessed | tf_op | source)
XLA Modules:
  0.0 111.0 jit_solution(5212117168482807575)
XLA Ops:
  1.1 1.5 %collective-permute-start.9 = (f32[4,64,256]{2,1,0:T(8,128)S(1)}, f32[4,64,256]{2,1,0:T(8,128)S(1)}, u32[]{:S(2)}, u32[]{:S(2)}) collective-permute-start(f32[4,64,256]{2,1,0:T(8,128)S(1)} %get-tuple-element.26), channel_id=1, source_target_pairs={{0,1},{1,0},{2,3},{3,2},{4,5},{5,4},{6,7},{7,6},{8,9},{9,8},{10,11... | collective-permute-start | bytes 786440 | tf_op jit(solution)/shard_map/ppermute | solution.py:33
  2.6 1.4 %collective-permute-start.4 = (f32[8,64,256]{2,1,0:T(8,128)}, f32[8,64,256]{2,1,0:T(8,128)S(1)}, u32[]{:S(2)}, u32[]{:S(2)}) collective-permute-start(f32[8,64,256]{2,1,0:T(8,128)} %refs_0_.1), channel_id=1, source_target_pairs={{0,8},{1,9},{2,10},{3,11},{4,12},{5,13},{6,14},{7,15},{8,0},{9,1},... | collective-permute-start | bytes 1572872 | tf_op jit(solution)/shard_map/ppermute | solution.py:29
  4.1 1.7 %collective-permute-start.10 = (f32[8,64,256]{2,1,0:T(8,128)S(1)}, f32[8,64,256]{2,1,0:T(8,128)S(1)}, u32[]{:S(2)}, u32[]{:S(2)}) collective-permute-start(f32[8,64,256]{2,1,0:T(8,128)S(1)} %pad_maximum_fusion.refs_0_), channel_id=1, source_target_pairs={{0,16},{1,17},{2,18},{3,19},{4,20},{5,21},{6,22},{7,23},{8,24},{9,... | collective-permute-start | bytes 1572872 | tf_op jit(solution)/shard_map/ppermute | solution.py:29
  5.8 2.2 %collective-permute-start.11 = (f32[8,64,256]{2,1,0:T(8,128)S(1)}, f32[8,64,256]{2,1,0:T(8,128)S(1)}, u32[]{:S(2)}, u32[]{:S(2)}) collective-permute-start(f32[8,64,256]{2,1,0:T(8,128)S(1)} %pad_maximum_fusion.refs_0_), channel_id=1, source_target_pairs={{0,48},{1,49},{2,50},{3,51},{4,52},{5,53},{6,54},{7,55},{8,56},{9,... | collective-permute-start | bytes 1572872 | tf_op jit(solution)/shard_map/ppermute | solution.py:29
  9.2 1.5 %collective-permute-start.1 = (f32[8,64,256]{2,1,0:T(8,128)S(1)}, f32[8,64,256]{2,1,0:T(8,128)S(1)}, u32[]{:S(2)}, u32[]{:S(2)}) collective-permute-start(f32[8,64,256]{2,1,0:T(8,128)S(1)} %copy-done), channel_id=1, source_target_pairs={{0,6},{1,7},{2,0},{3,1},{4,2},{5,3},{6,4},{7,5},{8,14},{9,15},{10,... | collective-permute-start | bytes 1572872 | tf_op jit(solution)/shard_map/ppermute | solution.py:29
  10.7 5.7 %collective-permute-done.4.refs_5_ = f32[8,64,256]{2,1,0:T(8,128)S(1)} collective-permute-done((f32[8,64,256]{2,1,0:T(8,128)}, f32[8,64,256]{2,1,0:T(8,128)S(1)}, u32[]{:S(2)}, u32[]{:S(2)}) %collective-permute-start.4) | collective-permute-done | bytes 524320 | tf_op jit(solution)/shard_map/ppermute | solution.py:29
  16.3 3.0 %collective-permute-start.14 = (f32[8,64,256]{2,1,0:T(8,128)S(1)}, f32[8,64,256]{2,1,0:T(8,128)}, u32[]{:S(2)}, u32[]{:S(2)}) collective-permute-start(f32[8,64,256]{2,1,0:T(8,128)S(1)} %pad_maximum_fusion.refs_0_), channel_id=1, source_target_pairs={{0,64},{1,65},{2,66},{3,67},{4,68},{5,69},{6,70},{7,71},{8,72},{9,... | collective-permute-start | bytes 1572872 | tf_op jit(solution)/shard_map/ppermute | solution.py:29
  21.1 1.5 %collective-permute-start.6 = (f32[8,64,256]{2,1,0:T(8,128)S(1)}, f32[8,64,256]{2,1,0:T(8,128)S(1)}, u32[]{:S(2)}, u32[]{:S(2)}) collective-permute-start(f32[8,64,256]{2,1,0:T(8,128)S(1)} %collective-permute-done.4.refs_5_), channel_id=1, source_target_pairs={{0,6},{1,7},{2,0},{3,1},{4,2},{5,3},{6,4},{7,5},{8,14},{9,15},{10,... | collective-permute-start | bytes 1572872 | tf_op jit(solution)/shard_map/ppermute | solution.py:29
  23.8 2.2 %collective-permute-start.13 = (f32[4,64,256]{2,1,0:T(8,128)S(1)}, f32[4,64,256]{2,1,0:T(8,128)S(1)}, u32[]{:S(2)}, u32[]{:S(2)}) collective-permute-start(f32[4,64,256]{2,1,0:T(8,128)S(1)} %slice.37), channel_id=1, source_target_pairs={{0,48},{1,49},{2,50},{3,51},{4,52},{5,53},{6,54},{7,55},{8,56},{9,... | collective-permute-start | bytes 786440 | tf_op jit(solution)/shard_map/ppermute | solution.py:29
  26.1 4.5 %collective-permute-done.14.refs_5_ = f32[8,64,256]{2,1,0:T(8,128)} collective-permute-done((f32[8,64,256]{2,1,0:T(8,128)S(1)}, f32[8,64,256]{2,1,0:T(8,128)}, u32[]{:S(2)}, u32[]{:S(2)}) %collective-permute-start.14) | collective-permute-done | bytes 524320 | tf_op jit(solution)/shard_map/ppermute | solution.py:29
  31.8 1.4 %collective-permute-start.3 = (f32[4,64,256]{2,1,0:T(8,128)S(1)}, f32[4,64,256]{2,1,0:T(8,128)S(1)}, u32[]{:S(2)}, u32[]{:S(2)}) collective-permute-start(f32[4,64,256]{2,1,0:T(8,128)S(1)} %slice.33), channel_id=1, source_target_pairs={{0,6},{1,7},{2,0},{3,1},{4,2},{5,3},{6,4},{7,5},{8,14},{9,15},{10,... | collective-permute-start | bytes 786440 | tf_op jit(solution)/shard_map/ppermute | solution.py:29
  33.3 1.7 %collective-permute-start.15 = (f32[8,64,256]{2,1,0:T(8,128)}, f32[8,64,256]{2,1,0:T(8,128)}, u32[]{:S(2)}, u32[]{:S(2)}) collective-permute-start(f32[8,64,256]{2,1,0:T(8,128)} %collective-permute-done.14.refs_5_), channel_id=1, source_target_pairs={{0,16},{1,17},{2,18},{3,19},{4,20},{5,21},{6,22},{7,23},{8,24},{9,... | collective-permute-start | bytes 1572872 | tf_op jit(solution)/shard_map/ppermute | solution.py:29
  35.8 2.2 %collective-permute-start.16 = (f32[8,64,256]{2,1,0:T(8,128)}, f32[8,64,256]{2,1,0:T(8,128)}, u32[]{:S(2)}, u32[]{:S(2)}) collective-permute-start(f32[8,64,256]{2,1,0:T(8,128)} %collective-permute-done.14.refs_5_), channel_id=1, source_target_pairs={{0,48},{1,49},{2,50},{3,51},{4,52},{5,53},{6,54},{7,55},{8,56},{9,... | collective-permute-start | bytes 1572872 | tf_op jit(solution)/shard_map/ppermute | solution.py:29
  38.0 2.9 %collective-permute-start.17 = (f32[8,64,256]{2,1,0:T(8,128)}, f32[8,64,256]{2,1,0:T(8,128)}, u32[]{:S(2)}, u32[]{:S(2)}) collective-permute-start(f32[8,64,256]{2,1,0:T(8,128)} %pad_maximum_fusion.1), channel_id=1, source_target_pairs={{0,64},{1,65},{2,66},{3,67},{4,68},{5,69},{6,70},{7,71},{8,72},{9,... | collective-permute-start | bytes 1572872 | tf_op jit(solution)/shard_map/ppermute | solution.py:29
  44.6 2.7 %collective-permute-start.8 = (f32[4,64,256]{2,1,0:T(8,128)}, f32[4,64,256]{2,1,0:T(8,128)}, u32[]{:S(2)}, u32[]{:S(2)}) collective-permute-start(f32[4,64,256]{2,1,0:T(8,128)} %slice.35), channel_id=1, source_target_pairs={{0,6},{1,7},{2,0},{3,1},{4,2},{5,3},{6,4},{7,5},{8,14},{9,15},{10,... | collective-permute-start | bytes 786440 | tf_op jit(solution)/shard_map/ppermute | solution.py:29
  50.5 2.0 %shard_map.46 = (bf16[5,512,256]{2,1,0:T(8,128)(2,1)S(1)}, bf16[5,512,256]{2,1,0:T(8,128)(2,1)S(1)}) custom-call(s32[64,16]{1,0:T(8,128)S(1)} %multiply_add_fusion.code_ref, f32[8,64,256]{2,1,0:T(8,128)S(1)} %copy-done, f32[8,64,256]{2,1,0:T(8,128)S(1)} %collective-permute-done.refs_1_, f32[8,64,256]{2,1,0:T(8,128)S(1)} %collective-permute-done.1.refs_2_, ...), custom_call_target="tpu_custom_call" | custom-call | bytes 6000000 | tf_op jit(solution)/shard_map/pallas_call | solution.py:208
  52.5 2.0 %shard_map.48 = (bf16[5,256,512]{2,1,0:T(8,128)(2,1)S(1)}, bf16[5,256,512]{2,1,0:T(8,128)(2,1)S(1)}) custom-call(s32[64,16]{1,0:T(8,128)S(1)} %multiply_add_fusion.code_ref, f32[8,64,256]{2,1,0:T(8,128)S(1)} %pad_maximum_fusion.refs_0_, f32[8,64,256]{2,1,0:T(8,128)S(1)} %collective-permute-done.10.refs_1_, ...), custom_call_target="tpu_custom_call" | custom-call | bytes 6000000 | tf_op jit(solution)/shard_map/pallas_call | solution.py:208
  54.6 1.9 %shard_map.47 = (bf16[8,512,256]{2,1,0:T(8,128)(2,1)S(1)}, bf16[8,512,256]{2,1,0:T(8,128)(2,1)S(1)}) custom-call(s32[64,16]{1,0:T(8,128)S(1)} %multiply_add_fusion.code_ref, bf16[5,512,256]{2,1,0:T(8,128)(2,1)S(1)} %get-tuple-element.15.refs_0_, bf16[5,512,256]{2,1,0:T(8,128)(2,1)S(1)} %get-tuple-element.16.refs_1_, f32[8,64,256]{2,1,0:T(8,128)S(1)} %copy-done.2, ...), custom_call_target="tpu_custom_call" | custom-call | bytes 9000000 | tf_op jit(solution)/shard_map/pallas_call | solution.py:208
  56.6 5.2 %shard_map.49 = (f32[8,64,256]{2,1,0:T(8,128)S(1)}, f32[8,64,256]{2,1,0:T(8,128)S(1)}) custom-call(s32[64,16]{1,0:T(8,128)S(1)} %multiply_add_fusion.code_ref, bf16[8,512,256]{2,1,0:T(8,128)(2,1)S(1)} %get-tuple-element.17.left_hi.far_hi, bf16[8,512,256]{2,1,0:T(8,128)(2,1)S(1)} %get-tuple-element.18.left_lo.far_lo, ...), custom_call_target="tpu_custom_call" | custom-call | bytes 24000000 | tf_op jit(solution)/shard_map/pallas_call | solution.py:208
  61.7 3.5 %collective-permute-start.18 = (f32[8,64,256]{2,1,0:T(8,128)S(1)}, f32[8,64,256]{2,1,0:T(8,128)S(1)}, u32[]{:S(2)}, u32[]{:S(2)}) collective-permute-start(f32[8,64,256]{2,1,0:T(8,128)S(1)} %get-tuple-element.22), channel_id=1, source_target_pairs={{0,1},{1,0},{2,3},{3,2},{4,5},{5,4},{6,7},{7,6},{8,9},{9,8},{10,11... | collective-permute-start | bytes 1572872 | tf_op jit(solution)/shard_map/ppermute | solution.py:33
  65.3 1.5 %collective-permute-done.18 = f32[8,64,256]{2,1,0:T(8,128)S(1)} collective-permute-done((f32[8,64,256]{2,1,0:T(8,128)S(1)}, f32[8,64,256]{2,1,0:T(8,128)S(1)}, u32[]{:S(2)}, u32[]{:S(2)}) %collective-permute-start.18) | collective-permute-done | bytes 524320 | tf_op jit(solution)/shard_map/ppermute | solution.py:33
  67.0 2.7 %collective-permute-start.25 = (f32[8,64,256]{2,1,0:T(8,128)S(1)}, f32[8,64,256]{2,1,0:T(8,128)S(1)}, u32[]{:S(2)}, u32[]{:S(2)}) collective-permute-start(f32[8,64,256]{2,1,0:T(8,128)S(1)} %add.23.refs_0_), channel_id=1, source_target_pairs={{0,48},{1,49},{2,50},{3,51},{4,52},{5,53},{6,54},{7,55},{8,56},{9,... | collective-permute-start | bytes 1572872 | tf_op jit(solution)/shard_map/ppermute | solution.py:29
  69.7 11.6 %collective-permute-done.22.refs_1_ = f32[8,64,256]{2,1,0:T(8,128)S(1)} collective-permute-done((f32[8,64,256]{2,1,0:T(8,128)S(1)}, f32[8,64,256]{2,1,0:T(8,128)S(1)}, u32[]{:S(2)}, u32[]{:S(2)}) %collective-permute-start.22) | collective-permute-done | bytes 524320 | tf_op jit(solution)/shard_map/ppermute | solution.py:29
  81.4 2.7 %collective-permute-start.26 = (f32[4,64,256]{2,1,0:T(8,128)S(1)}, f32[4,64,256]{2,1,0:T(8,128)S(1)}, u32[]{:S(2)}, u32[]{:S(2)}) collective-permute-start(f32[4,64,256]{2,1,0:T(8,128)S(1)} %slice.39), channel_id=1, source_target_pairs={{0,48},{1,49},{2,50},{3,51},{4,52},{5,53},{6,54},{7,55},{8,56},{9,... | collective-permute-start | bytes 786440 | tf_op jit(solution)/shard_map/ppermute | solution.py:29
  84.2 2.7 %collective-permute-start.21 = (f32[8,64,256]{2,1,0:T(8,128)S(1)}, f32[8,64,256]{2,1,0:T(8,128)S(1)}, u32[]{:S(2)}, u32[]{:S(2)}) collective-permute-start(f32[8,64,256]{2,1,0:T(8,128)S(1)} %collective-permute-done.19.refs_5_), channel_id=1, source_target_pairs={{0,48},{1,49},{2,50},{3,51},{4,52},{5,53},{6,54},{7,55},{8,56},{9,... | collective-permute-start | bytes 1572872 | tf_op jit(solution)/shard_map/ppermute | solution.py:29
  86.8 2.4 %collective-permute-done.23.refs_3_ = f32[4,64,256]{2,1,0:T(8,128)S(1)} collective-permute-done((f32[4,64,256]{2,1,0:T(8,128)S(1)}, f32[4,64,256]{2,1,0:T(8,128)S(1)}, u32[]{:S(2)}, u32[]{:S(2)}) %collective-permute-start.23) | collective-permute-done | bytes 262176 | tf_op jit(solution)/shard_map/ppermute | solution.py:29
  89.3 2.9 %collective-permute-start.27 = (f32[4,64,256]{2,1,0:T(8,128)S(1)}, f32[4,64,256]{2,1,0:T(8,128)S(1)}, u32[]{:S(2)}, u32[]{:S(2)}) collective-permute-start(f32[4,64,256]{2,1,0:T(8,128)S(1)} %collective-permute-done.26.refs_4_), channel_id=1, source_target_pairs={{0,64},{1,65},{2,66},{3,67},{4,68},{5,69},{6,70},{7,71},{8,72},{9,... | collective-permute-start | bytes 786440 | tf_op jit(solution)/shard_map/ppermute | solution.py:29
  92.2 4.5 %shard_map.50.refs_4_ = f32[512,512]{1,0:T(8,128)S(1)} custom-call(s32[64,16]{1,0:T(8,128)S(1)} %multiply_add_fusion.code_ref, bf16[8,512,256]{2,1,0:T(8,128)(2,1)S(1)} %get-tuple-element.17.left_hi.far_hi, bf16[8,512,256]{2,1,0:T(8,128)(2,1)S(1)} %get-tuple-element.18.left_lo.far_lo, f32[8,64,256]{2,1,0:T(8,128)S(1)} %add.23.refs_0_, ...), custom_call_target="tpu_custom_call" | custom-call | bytes 12000000 | tf_op jit(solution)/shard_map/pallas_call | solution.py:208
  96.7 3.6 %collective-permute-done.27.refs_3_ = f32[4,64,256]{2,1,0:T(8,128)S(1)} collective-permute-done((f32[4,64,256]{2,1,0:T(8,128)S(1)}, f32[4,64,256]{2,1,0:T(8,128)S(1)}, u32[]{:S(2)}, u32[]{:S(2)}) %collective-permute-start.27) | collective-permute-done | bytes 262176 | tf_op jit(solution)/shard_map/ppermute | solution.py:29
  100.4 3.5 %shard_map.51 = (f32[8,64,256]{2,1,0:T(8,128)S(1)}, f32[8,64,256]{2,1,0:T(8,128)S(1)}) custom-call(s32[64,16]{1,0:T(8,128)S(1)} %multiply_add_fusion.code_ref, bf16[8,512,256]{2,1,0:T(8,128)(2,1)S(1)} %get-tuple-element.17.left_hi.far_hi, bf16[8,512,256]{2,1,0:T(8,128)(2,1)S(1)} %get-tuple-element.18.left_lo.far_lo, ...), custom_call_target="tpu_custom_call" | custom-call | bytes 12000000 | tf_op jit(solution)/shard_map/pallas_call | solution.py:208
  103.9 4.7 %collective-permute-start.28 = (f32[8,64,256]{2,1,0:T(8,128)S(1)}, f32[8,64,256]{2,1,0:T(8,128)S(1)}, u32[]{:S(2)}, u32[]{:S(2)}) collective-permute-start(f32[8,64,256]{2,1,0:T(8,128)S(1)} %get-tuple-element.24), channel_id=1, source_target_pairs={{0,1},{1,0},{2,3},{3,2},{4,5},{5,4},{6,7},{7,6},{8,9},{9,8},{10,11... | collective-permute-start | bytes 1572872 | tf_op jit(solution)/shard_map/ppermute | solution.py:33
  108.6 1.5 %collective-permute-done.28 = f32[8,64,256]{2,1,0:T(8,128)S(1)} collective-permute-done((f32[8,64,256]{2,1,0:T(8,128)S(1)}, f32[8,64,256]{2,1,0:T(8,128)S(1)}, u32[]{:S(2)}, u32[]{:S(2)}) %collective-permute-start.28) | collective-permute-done | bytes 524320 | tf_op jit(solution)/shard_map/ppermute | solution.py:33
  (81 shorter events, 15.9 us)
Async XLA Ops:
  1.1 2.9 %collective-permute-start.9 = (f32[4,64,256]{2,1,0:T(8,128)S(1)}, f32[4,64,256]{2,1,0:T(8,128)S(1)}, u32[]{:S(2)}, u32[]{:S(2)}) collective-permute-start(f32[4,64,256]{2,1,0:T(8,128)S(1)} %get-tuple-element.26), channel_id=1, source_target_pairs={{0,1},{1,0},{2,3},{3,2},{4,5},{5,4},{6,7},{7,6},{8,9},{9,8},{10,11... | collective-permute-start | bytes 786440 | tf_op jit(solution)/shard_map/ppermute | solution.py:33
  2.6 13.7 %collective-permute-start.4 = (f32[8,64,256]{2,1,0:T(8,128)}, f32[8,64,256]{2,1,0:T(8,128)S(1)}, u32[]{:S(2)}, u32[]{:S(2)}) collective-permute-start(f32[8,64,256]{2,1,0:T(8,128)} %refs_0_.1), channel_id=1, source_target_pairs={{0,8},{1,9},{2,10},{3,11},{4,12},{5,13},{6,14},{7,15},{8,0},{9,1},... | collective-permute-start | bytes 1572872 | tf_op jit(solution)/shard_map/ppermute | solution.py:29
  4.1 15.8 %collective-permute-start.10 = (f32[8,64,256]{2,1,0:T(8,128)S(1)}, f32[8,64,256]{2,1,0:T(8,128)S(1)}, u32[]{:S(2)}, u32[]{:S(2)}) collective-permute-start(f32[8,64,256]{2,1,0:T(8,128)S(1)} %pad_maximum_fusion.refs_0_), channel_id=1, source_target_pairs={{0,16},{1,17},{2,18},{3,19},{4,20},{5,21},{6,22},{7,23},{8,24},{9,... | collective-permute-start | bytes 1572872 | tf_op jit(solution)/shard_map/ppermute | solution.py:29
  5.8 15.3 %collective-permute-start.11 = (f32[8,64,256]{2,1,0:T(8,128)S(1)}, f32[8,64,256]{2,1,0:T(8,128)S(1)}, u32[]{:S(2)}, u32[]{:S(2)}) collective-permute-start(f32[8,64,256]{2,1,0:T(8,128)S(1)} %pad_maximum_fusion.refs_0_), channel_id=1, source_target_pairs={{0,48},{1,49},{2,50},{3,51},{4,52},{5,53},{6,54},{7,55},{8,56},{9,... | collective-permute-start | bytes 1572872 | tf_op jit(solution)/shard_map/ppermute | solution.py:29
  8.0 14.7 %collective-permute-start = (f32[8,64,256]{2,1,0:T(8,128)S(1)}, f32[8,64,256]{2,1,0:T(8,128)S(1)}, u32[]{:S(2)}, u32[]{:S(2)}) collective-permute-start(f32[8,64,256]{2,1,0:T(8,128)S(1)} %copy-done), channel_id=1, source_target_pairs={{0,2},{1,3},{2,4},{3,5},{4,6},{5,7},{6,0},{7,1},{8,10},{9,11},{10,... | collective-permute-start | bytes 1572872 | tf_op jit(solution)/shard_map/ppermute | solution.py:29
  9.2 14.6 %collective-permute-start.1 = (f32[8,64,256]{2,1,0:T(8,128)S(1)}, f32[8,64,256]{2,1,0:T(8,128)S(1)}, u32[]{:S(2)}, u32[]{:S(2)}) collective-permute-start(f32[8,64,256]{2,1,0:T(8,128)S(1)} %copy-done), channel_id=1, source_target_pairs={{0,6},{1,7},{2,0},{3,1},{4,2},{5,3},{6,4},{7,5},{8,14},{9,15},{10,... | collective-permute-start | bytes 1572872 | tf_op jit(solution)/shard_map/ppermute | solution.py:29
  16.3 14.2 %collective-permute-start.14 = (f32[8,64,256]{2,1,0:T(8,128)S(1)}, f32[8,64,256]{2,1,0:T(8,128)}, u32[]{:S(2)}, u32[]{:S(2)}) collective-permute-start(f32[8,64,256]{2,1,0:T(8,128)S(1)} %pad_maximum_fusion.refs_0_), channel_id=1, source_target_pairs={{0,64},{1,65},{2,66},{3,67},{4,68},{5,69},{6,70},{7,71},{8,72},{9,... | collective-permute-start | bytes 1572872 | tf_op jit(solution)/shard_map/ppermute | solution.py:29
  19.9 15.9 %collective-permute-start.5 = (f32[8,64,256]{2,1,0:T(8,128)S(1)}, f32[8,64,256]{2,1,0:T(8,128)S(1)}, u32[]{:S(2)}, u32[]{:S(2)}) collective-permute-start(f32[8,64,256]{2,1,0:T(8,128)S(1)} %collective-permute-done.4.refs_5_), channel_id=1, source_target_pairs={{0,2},{1,3},{2,4},{3,5},{4,6},{5,7},{6,0},{7,1},{8,10},{9,11},{10,... | collective-permute-start | bytes 1572872 | tf_op jit(solution)/shard_map/ppermute | solution.py:29
  21.1 16.9 %collective-permute-start.6 = (f32[8,64,256]{2,1,0:T(8,128)S(1)}, f32[8,64,256]{2,1,0:T(8,128)S(1)}, u32[]{:S(2)}, u32[]{:S(2)}) collective-permute-start(f32[8,64,256]{2,1,0:T(8,128)S(1)} %collective-permute-done.4.refs_5_), channel_id=1, source_target_pairs={{0,6},{1,7},{2,0},{3,1},{4,2},{5,3},{6,4},{7,5},{8,14},{9,15},{10,... | collective-permute-start | bytes 1572872 | tf_op jit(solution)/shard_map/ppermute | solution.py:29
  22.6 9.2 %collective-permute-start.12 = (f32[4,64,256]{2,1,0:T(8,128)S(1)}, f32[4,64,256]{2,1,0:T(8,128)S(1)}, u32[]{:S(2)}, u32[]{:S(2)}) collective-permute-start(f32[4,64,256]{2,1,0:T(8,128)S(1)} %slice.36), channel_id=1, source_target_pairs={{0,16},{1,17},{2,18},{3,19},{4,20},{5,21},{6,22},{7,23},{8,24},{9,... | collective-permute-start | bytes 786440 | tf_op jit(solution)/shard_map/ppermute | solution.py:29
  23.8 9.5 %collective-permute-start.13 = (f32[4,64,256]{2,1,0:T(8,128)S(1)}, f32[4,64,256]{2,1,0:T(8,128)S(1)}, u32[]{:S(2)}, u32[]{:S(2)}) collective-permute-start(f32[4,64,256]{2,1,0:T(8,128)S(1)} %slice.37), channel_id=1, source_target_pairs={{0,48},{1,49},{2,50},{3,51},{4,52},{5,53},{6,54},{7,55},{8,56},{9,... | collective-permute-start | bytes 786440 | tf_op jit(solution)/shard_map/ppermute | solution.py:29
  26.0 21.3 %copy-start.13 = (s32[64,16,4]{0,2,1:T(4,128)S(1)}, s32[64,16,4]{0,2,1:T(4,128)}, u32[]{:S(2)}) copy-start(s32[64,16,4]{0,2,1:T(4,128)} %param.5) | copy-start | bytes 49156
  26.0 21.3 %copy-start.15 = (s32[4]{0:T(128)S(1)}, s32[4]{0:T(128)}, u32[]{:S(2)}) copy-start(s32[4]{0:T(128)} %constant.27.clone) | copy-start | bytes 52
  26.0 21.5 %copy-start.14 = (s32[64,16]{0,1:T(8,128)S(1)}, s32[64,16]{0,1:T(8,128)}, u32[]{:S(2)}) copy-start(s32[64,16]{0,1:T(8,128)} %param.6) | copy-start | bytes 12292
  30.6 12.6 %collective-permute-start.2 = (f32[4,64,256]{2,1,0:T(8,128)S(1)}, f32[4,64,256]{2,1,0:T(8,128)S(1)}, u32[]{:S(2)}, u32[]{:S(2)}) collective-permute-start(f32[4,64,256]{2,1,0:T(8,128)S(1)} %slice.32), channel_id=1, source_target_pairs={{0,2},{1,3},{2,4},{3,5},{4,6},{5,7},{6,0},{7,1},{8,10},{9,11},{10,... | collective-permute-start | bytes 786440 | tf_op jit(solution)/shard_map/ppermute | solution.py:29
  31.8 12.1 %collective-permute-start.3 = (f32[4,64,256]{2,1,0:T(8,128)S(1)}, f32[4,64,256]{2,1,0:T(8,128)S(1)}, u32[]{:S(2)}, u32[]{:S(2)}) collective-permute-start(f32[4,64,256]{2,1,0:T(8,128)S(1)} %slice.33), channel_id=1, source_target_pairs={{0,6},{1,7},{2,0},{3,1},{4,2},{5,3},{6,4},{7,5},{8,14},{9,15},{10,... | collective-permute-start | bytes 786440 | tf_op jit(solution)/shard_map/ppermute | solution.py:29
  33.3 23.3 %collective-permute-start.15 = (f32[8,64,256]{2,1,0:T(8,128)}, f32[8,64,256]{2,1,0:T(8,128)}, u32[]{:S(2)}, u32[]{:S(2)}) collective-permute-start(f32[8,64,256]{2,1,0:T(8,128)} %collective-permute-done.14.refs_5_), channel_id=1, source_target_pairs={{0,16},{1,17},{2,18},{3,19},{4,20},{5,21},{6,22},{7,23},{8,24},{9,... | collective-permute-start | bytes 1572872 | tf_op jit(solution)/shard_map/ppermute | solution.py:29
  35.8 20.8 %collective-permute-start.16 = (f32[8,64,256]{2,1,0:T(8,128)}, f32[8,64,256]{2,1,0:T(8,128)}, u32[]{:S(2)}, u32[]{:S(2)}) collective-permute-start(f32[8,64,256]{2,1,0:T(8,128)} %collective-permute-done.14.refs_5_), channel_id=1, source_target_pairs={{0,48},{1,49},{2,50},{3,51},{4,52},{5,53},{6,54},{7,55},{8,56},{9,... | collective-permute-start | bytes 1572872 | tf_op jit(solution)/shard_map/ppermute | solution.py:29
  38.0 18.6 %collective-permute-start.17 = (f32[8,64,256]{2,1,0:T(8,128)}, f32[8,64,256]{2,1,0:T(8,128)}, u32[]{:S(2)}, u32[]{:S(2)}) collective-permute-start(f32[8,64,256]{2,1,0:T(8,128)} %pad_maximum_fusion.1), channel_id=1, source_target_pairs={{0,64},{1,65},{2,66},{3,67},{4,68},{5,69},{6,70},{7,71},{8,72},{9,... | collective-permute-start | bytes 1572872 | tf_op jit(solution)/shard_map/ppermute | solution.py:29
  43.9 10.7 %collective-permute-start.7 = (f32[4,64,256]{2,1,0:T(8,128)}, f32[4,64,256]{2,1,0:T(8,128)}, u32[]{:S(2)}, u32[]{:S(2)}) collective-permute-start(f32[4,64,256]{2,1,0:T(8,128)} %slice.34), channel_id=1, source_target_pairs={{0,2},{1,3},{2,4},{3,5},{4,6},{5,7},{6,0},{7,1},{8,10},{9,11},{10,... | collective-permute-start | bytes 786440 | tf_op jit(solution)/shard_map/ppermute | solution.py:29
  44.6 10.0 %collective-permute-start.8 = (f32[4,64,256]{2,1,0:T(8,128)}, f32[4,64,256]{2,1,0:T(8,128)}, u32[]{:S(2)}, u32[]{:S(2)}) collective-permute-start(f32[4,64,256]{2,1,0:T(8,128)} %slice.35), channel_id=1, source_target_pairs={{0,6},{1,7},{2,0},{3,1},{4,2},{5,3},{6,4},{7,5},{8,14},{9,15},{10,... | collective-permute-start | bytes 786440 | tf_op jit(solution)/shard_map/ppermute | solution.py:29
  61.7 5.1 %collective-permute-start.18 = (f32[8,64,256]{2,1,0:T(8,128)S(1)}, f32[8,64,256]{2,1,0:T(8,128)S(1)}, u32[]{:S(2)}, u32[]{:S(2)}) collective-permute-start(f32[8,64,256]{2,1,0:T(8,128)S(1)} %get-tuple-element.22), channel_id=1, source_target_pairs={{0,1},{1,0},{2,3},{3,2},{4,5},{5,4},{6,7},{7,6},{8,9},{9,8},{10,11... | collective-permute-start | bytes 1572872 | tf_op jit(solution)/shard_map/ppermute | solution.py:33
  66.9 14.4 %collective-permute-start.22 = (f32[8,64,256]{2,1,0:T(8,128)S(1)}, f32[8,64,256]{2,1,0:T(8,128)S(1)}, u32[]{:S(2)}, u32[]{:S(2)}) collective-permute-start(f32[8,64,256]{2,1,0:T(8,128)S(1)} %add.23.refs_0_), channel_id=1, source_target_pairs={{0,16},{1,17},{2,18},{3,19},{4,20},{5,21},{6,22},{7,23},{8,24},{9,... | collective-permute-start | bytes 1572872 | tf_op jit(solution)/shard_map/ppermute | solution.py:29
  67.0 14.4 %collective-permute-start.25 = (f32[8,64,256]{2,1,0:T(8,128)S(1)}, f32[8,64,256]{2,1,0:T(8,128)S(1)}, u32[]{:S(2)}, u32[]{:S(2)}) collective-permute-start(f32[8,64,256]{2,1,0:T(8,128)S(1)} %add.23.refs_0_), channel_id=1, source_target_pairs={{0,48},{1,49},{2,50},{3,51},{4,52},{5,53},{6,54},{7,55},{8,56},{9,... | collective-permute-start | bytes 1572872 | tf_op jit(solution)/shard_map/ppermute | solution.py:29
  69.6 14.5 %collective-permute-start.19 = (f32[8,64,256]{2,1,0:T(8,128)S(1)}, f32[8,64,256]{2,1,0:T(8,128)S(1)}, u32[]{:S(2)}, u32[]{:S(2)}) collective-permute-start(f32[8,64,256]{2,1,0:T(8,128)S(1)} %add.23.refs_0_), channel_id=1, source_target_pairs={{0,64},{1,65},{2,66},{3,67},{4,68},{5,69},{6,70},{7,71},{8,72},{9,... | collective-permute-start | bytes 1572872 | tf_op jit(solution)/shard_map/ppermute | solution.py:29
  81.3 7.9 %collective-permute-start.23 = (f32[4,64,256]{2,1,0:T(8,128)S(1)}, f32[4,64,256]{2,1,0:T(8,128)S(1)}, u32[]{:S(2)}, u32[]{:S(2)}) collective-permute-start(f32[4,64,256]{2,1,0:T(8,128)S(1)} %slice.38), channel_id=1, source_target_pairs={{0,16},{1,17},{2,18},{3,19},{4,20},{5,21},{6,22},{7,23},{8,24},{9,... | collective-permute-start | bytes 786440 | tf_op jit(solution)/shard_map/ppermute | solution.py:29
  81.4 7.8 %collective-permute-start.26 = (f32[4,64,256]{2,1,0:T(8,128)S(1)}, f32[4,64,256]{2,1,0:T(8,128)S(1)}, u32[]{:S(2)}, u32[]{:S(2)}) collective-permute-start(f32[4,64,256]{2,1,0:T(8,128)S(1)} %slice.39), channel_id=1, source_target_pairs={{0,48},{1,49},{2,50},{3,51},{4,52},{5,53},{6,54},{7,55},{8,56},{9,... | collective-permute-start | bytes 786440 | tf_op jit(solution)/shard_map/ppermute | solution.py:29
  84.2 16.3 %collective-permute-start.20 = (f32[8,64,256]{2,1,0:T(8,128)S(1)}, f32[8,64,256]{2,1,0:T(8,128)S(1)}, u32[]{:S(2)}, u32[]{:S(2)}) collective-permute-start(f32[8,64,256]{2,1,0:T(8,128)S(1)} %collective-permute-done.19.refs_5_), channel_id=1, source_target_pairs={{0,16},{1,17},{2,18},{3,19},{4,20},{5,21},{6,22},{7,23},{8,24},{9,... | collective-permute-start | bytes 1572872 | tf_op jit(solution)/shard_map/ppermute | solution.py:29
  84.2 16.3 %collective-permute-start.21 = (f32[8,64,256]{2,1,0:T(8,128)S(1)}, f32[8,64,256]{2,1,0:T(8,128)S(1)}, u32[]{:S(2)}, u32[]{:S(2)}) collective-permute-start(f32[8,64,256]{2,1,0:T(8,128)S(1)} %collective-permute-done.19.refs_5_), channel_id=1, source_target_pairs={{0,48},{1,49},{2,50},{3,51},{4,52},{5,53},{6,54},{7,55},{8,56},{9,... | collective-permute-start | bytes 1572872 | tf_op jit(solution)/shard_map/ppermute | solution.py:29
  89.2 7.5 %collective-permute-start.24 = (f32[4,64,256]{2,1,0:T(8,128)S(1)}, f32[4,64,256]{2,1,0:T(8,128)S(1)}, u32[]{:S(2)}, u32[]{:S(2)}) collective-permute-start(f32[4,64,256]{2,1,0:T(8,128)S(1)} %collective-permute-done.23.refs_3_), channel_id=1, source_target_pairs={{0,64},{1,65},{2,66},{3,67},{4,68},{5,69},{6,70},{7,71},{8,72},{9,... | collective-permute-start | bytes 786440 | tf_op jit(solution)/shard_map/ppermute | solution.py:29
  89.3 11.0 %collective-permute-start.27 = (f32[4,64,256]{2,1,0:T(8,128)S(1)}, f32[4,64,256]{2,1,0:T(8,128)S(1)}, u32[]{:S(2)}, u32[]{:S(2)}) collective-permute-start(f32[4,64,256]{2,1,0:T(8,128)S(1)} %collective-permute-done.26.refs_4_), channel_id=1, source_target_pairs={{0,64},{1,65},{2,66},{3,67},{4,68},{5,69},{6,70},{7,71},{8,72},{9,... | collective-permute-start | bytes 786440 | tf_op jit(solution)/shard_map/ppermute | solution.py:29
  103.9 6.2 %collective-permute-start.28 = (f32[8,64,256]{2,1,0:T(8,128)S(1)}, f32[8,64,256]{2,1,0:T(8,128)S(1)}, u32[]{:S(2)}, u32[]{:S(2)}) collective-permute-start(f32[8,64,256]{2,1,0:T(8,128)S(1)} %get-tuple-element.24), channel_id=1, source_target_pairs={{0,1},{1,0},{2,3},{3,2},{4,5},{5,4},{6,7},{7,6},{8,9},{9,8},{10,11... | collective-permute-start | bytes 1572872 | tf_op jit(solution)/shard_map/ppermute | solution.py:33
  (13 other events, 52.4 us)
